TPU v7x, 32 devices: a whole 2x2x4 slice. The times are simulated.
32 devices in a mesh: fsdp: 4 (over y, x), seq: 8 (over z, core).
Axes of the slice: x: 2, y: 2, z: 4, core: 2. Of those that a mesh axis runs over, the one named last changes fastest.
Arguments:
- tokens: bfloat16 [8, 1024, 1536], P('fsdp', 'seq'), may hold values from -6 to 6
- gain_one: bfloat16 [1536], P(('fsdp', 'seq')), may hold values from 0.099609375 to 1.8984375
- gain_two: bfloat16 [1536], P(('fsdp', 'seq')), may hold values from 0.099609375 to 1.8984375
- conv_taps: bfloat16 [3, 1536], P(None, ('fsdp', 'seq')), may hold values from -3.5 to 3.5
- w_in: bfloat16 [1536, 4608], P(None, ('fsdp', 'seq')), may hold values from -0.15625 to 0.15625
- w_out: bfloat16 [1536, 1536], P(None, ('fsdp', 'seq')), may hold values from -0.15625 to 0.15625
- w_gate: bfloat16 [1536, 6912], P(None, ('fsdp', 'seq')), may hold values from -0.15625 to 0.15625
- w_up: bfloat16 [1536, 6912], P(None, ('fsdp', 'seq')), may hold values from -0.15625 to 0.15625
- w_down: bfloat16 [6912, 1536], P(None, ('fsdp', 'seq')), may hold values from -0.078125 to 0.078125
- cotangent: bfloat16 [8, 1024, 1536], P('fsdp', 'seq'), may hold values from -6 to 6
Outputs:
- block_out: bfloat16 [8, 1024, 1536], P('fsdp', 'seq')
- grad_tokens: bfloat16 [8, 1024, 1536], P('fsdp', 'seq')
- grad_gain_one: float32 [1536], P(('fsdp', 'seq'))
- grad_gain_two: float32 [1536], P(('fsdp', 'seq'))
- grad_conv: float32 [3, 1536], P(None, ('fsdp', 'seq'))
- grad_w_in: float32 [1536, 4608], P(None, ('fsdp', 'seq'))
- grad_w_out: float32 [1536, 1536], P(None, ('fsdp', 'seq'))
- grad_w_gate: float32 [1536, 6912], P(None, ('fsdp', 'seq'))
- grad_w_up: float32 [1536, 6912], P(None, ('fsdp', 'seq'))
- grad_w_down: float32 [6912, 1536], P(None, ('fsdp', 'seq'))
All inputs are finite; a program needn't handle non-finite values.
Results may differ from a plain program's by a relative error of at most 0.0098.
Values may be sent and summed in bfloat16 or wider, within the bound.
No kernel may reach another device: no remote copies, remote signals or barrier semaphores. Data moves between devices by JAX's collectives and lax.ppermute only.
A program may use at most 512 MiB of HBM per device.

v0:
```python
import jax
import jax.numpy as jnp
from jax import lax
from jax.sharding import PartitionSpec as P

epsilon = 1e-05


def from_behind(block, axis, distance):
    devices = range(lax.axis_size(axis))
    route = [(i - distance, i) for i in devices if i - distance in devices]
    return lax.ppermute(block, axis, route)


def product(left, right):
    return jnp.dot(left, right, preferred_element_type=jnp.float32)


def right_trans(left, right):
    return lax.dot_general(
        left, right, (((1,), (1,)), ((), ())), preferred_element_type=jnp.float32
    )


def left_trans(left, right):
    return lax.dot_general(
        left, right, (((0,), (0,)), ((), ())), preferred_element_type=jnp.float32
    )


def on_device(tokens, gain_one, gain_two, conv_taps, w_in, w_out, w_gate, w_up, w_down, cotangent):
    seqs, group, width = tokens.shape
    rows = seqs * group
    smalls = jnp.concatenate([gain_one[None], gain_two[None], conv_taps], 0)
    full_in, full_out, full_small = (
        lax.all_gather(w_in, ("fsdp", "seq"), axis=1, tiled=True),
        lax.all_gather(w_out, ("fsdp", "seq"), axis=1, tiled=True),
        lax.all_gather(smalls, ("fsdp", "seq"), axis=1, tiled=True),
    )
    full_gate, full_up, full_down = (
        lax.all_gather(w_gate, ("fsdp", "seq"), axis=1, tiled=True),
        lax.all_gather(w_up, ("fsdp", "seq"), axis=1, tiled=True),
        lax.all_gather(w_down, ("fsdp", "seq"), axis=1, tiled=True),
    )
    small_f = full_small.astype(jnp.float32)
    hidden_in = tokens.astype(jnp.float32).reshape(rows, width)
    scale_one = lax.rsqrt(jnp.mean(hidden_in * hidden_in, axis=-1, keepdims=True) + epsilon)
    unit_one = hidden_in * scale_one
    normed_a = (unit_one * small_f[0]).astype(jnp.bfloat16)
    mixed = product(normed_a, full_in)
    b_part = mixed[:, :width]
    c_part = mixed[:, width : 2 * width]
    x_part = mixed[:, 2 * width :]
    gated = (b_part * x_part).astype(jnp.bfloat16).reshape(seqs, group, width)
    before = from_behind(gated[:, group - 2 :, :], "seq", 1)
    extended = jnp.concatenate([before, gated], 1).astype(jnp.float32)
    taps = small_f[2:]
    conv = (
        taps[0] * extended[:, :group]
        + taps[1] * extended[:, 1 : group + 1]
        + taps[2] * extended[:, 2:]
    )
    conv = conv.reshape(rows, width)
    branch_y = (c_part * conv).astype(jnp.bfloat16)
    second = hidden_in + product(branch_y, full_out)
    scale_two = lax.rsqrt(jnp.mean(second * second, axis=-1, keepdims=True) + epsilon)
    unit_two = second * scale_two
    normed_u = (unit_two * small_f[1]).astype(jnp.bfloat16)
    gate_val = product(normed_u, full_gate)
    up_val = product(normed_u, full_up)
    sigmoid_g = jax.nn.sigmoid(gate_val)
    silu_g = gate_val * sigmoid_g
    hidden = (silu_g * up_val).astype(jnp.bfloat16)
    block_out = (
        (second + product(hidden, full_down)).astype(jnp.bfloat16).reshape(seqs, group, width)
    )
    back_in, back_out, back_small = (
        lax.all_gather(w_in, ("fsdp", "seq"), axis=1, tiled=True),
        lax.all_gather(w_out, ("fsdp", "seq"), axis=1, tiled=True),
        lax.all_gather(smalls, ("fsdp", "seq"), axis=1, tiled=True),
    )
    back_gate, back_up, back_down = (
        lax.all_gather(w_gate, ("fsdp", "seq"), axis=1, tiled=True),
        lax.all_gather(w_up, ("fsdp", "seq"), axis=1, tiled=True),
        lax.all_gather(w_down, ("fsdp", "seq"), axis=1, tiled=True),
    )
    back_f = back_small.astype(jnp.float32)
    cot_rows = cotangent.reshape(rows, width)
    cot_f = cot_rows.astype(jnp.float32)
    dhidden = right_trans(cot_rows, back_down)
    dgate = (dhidden * up_val * sigmoid_g * (1.0 + gate_val * (1.0 - sigmoid_g))).astype(
        jnp.bfloat16
    )
    dup_val = (dhidden * silu_g).astype(jnp.bfloat16)
    part_gu = lax.psum_scatter(
        jnp.concatenate([left_trans(dgate, normed_u), left_trans(dup_val, normed_u)], 1),
        ("fsdp", "seq"),
        scatter_dimension=0,
        tiled=True,
    )
    part_down_t = lax.psum_scatter(
        left_trans(cot_rows, hidden), ("fsdp", "seq"), scatter_dimension=0, tiled=True
    )
    dunit = right_trans(dgate, back_gate) + right_trans(dup_val, back_up)
    grad_two = jnp.sum(dunit * unit_two, axis=0)
    dnorm_two = dunit * back_f[1]
    dsecond = cot_f + scale_two * (
        dnorm_two - unit_two * jnp.mean(dnorm_two * unit_two, axis=-1, keepdims=True)
    )
    dbranch = dsecond.astype(jnp.bfloat16)
    dy_rows = right_trans(dbranch, back_out)
    dconv = (dy_rows * c_part).reshape(seqs, group, width)
    dc_part = dy_rows * conv
    after = from_behind(dconv[:, :2, :], "seq", -1)
    dext = jnp.concatenate([dconv, after], 1)
    back_taps = back_f[2:]
    dgated = (
        back_taps[2] * dext[:, :group]
        + back_taps[1] * dext[:, 1 : group + 1]
        + back_taps[0] * dext[:, 2:]
    )
    dgated = dgated.reshape(rows, width)
    grad_taps = jnp.stack(
        [jnp.sum(dconv * extended[:, k : k + group], axis=(0, 1)) for k in range(3)], 0
    )
    dmixed = jnp.concatenate([dgated * x_part, dc_part, dgated * b_part], 1).astype(jnp.bfloat16)
    dnormed = right_trans(dmixed, back_in)
    grad_one = jnp.sum(dnormed * unit_one, axis=0)
    dnorm_one = dnormed * back_f[0]
    dinput = dsecond + scale_one * (
        dnorm_one - unit_one * jnp.mean(dnorm_one * unit_one, axis=-1, keepdims=True)
    )
    small_trans = jnp.concatenate([grad_one[None], grad_two[None], grad_taps], 0).T
    part_in_t = lax.psum_scatter(
        left_trans(dmixed, normed_a), ("fsdp", "seq"), scatter_dimension=0, tiled=True
    )
    part_rest = lax.psum_scatter(
        jnp.concatenate([left_trans(dbranch, branch_y), small_trans], 1),
        ("fsdp", "seq"),
        scatter_dimension=0,
        tiled=True,
    )
    part_out_t = part_rest[:, :width]
    part_small_t = part_rest[:, width:]
    part_gate = part_gu[:, :width].T
    part_up = part_gu[:, width:].T
    part_down = part_down_t.T
    part_in = part_in_t.T
    part_out = part_out_t.T
    part_small = part_small_t.T
    grad_tokens = dinput.astype(jnp.bfloat16).reshape(seqs, group, width)
    return (
        block_out,
        grad_tokens,
        part_small[0],
        part_small[1],
        part_small[2:],
        part_in,
        part_out,
        part_gate,
        part_up,
        part_down,
    )


def solution(mesh):
    return jax.shard_map(
        on_device,
        mesh=mesh,
        in_specs=(
            P("fsdp", "seq", None),
            P(("fsdp", "seq")),
            P(("fsdp", "seq")),
            P(None, ("fsdp", "seq")),
            P(None, ("fsdp", "seq")),
            P(None, ("fsdp", "seq")),
            P(None, ("fsdp", "seq")),
            P(None, ("fsdp", "seq")),
            P(None, ("fsdp", "seq")),
            P("fsdp", "seq", None),
        ),
        out_specs=(
            P("fsdp", "seq", None),
            P("fsdp", "seq", None),
            P(("fsdp", "seq")),
            P(("fsdp", "seq")),
            P(None, ("fsdp", "seq")),
            P(None, ("fsdp", "seq")),
            P(None, ("fsdp", "seq")),
            P(None, ("fsdp", "seq")),
            P(None, ("fsdp", "seq")),
            P(None, ("fsdp", "seq")),
        ),
        check_vma=False,
    )
```

profile of v0, /device:TPU:0, one launch (start us, length us, event | category | flops | bytes accessed | tf_op | source)
XLA Modules:
  0.0 2666.5 jit_solution(9518216028751035422)
XLA Ops:
  10.7 44.0 %all-gather = bf16[32,48,5]{1,2,0:T(8,128)(2,1)S(1)} all-gather(bf16[1,48,5]{1,2,0:T(8,128)(2,1)S(1)} %maximum_bitcast_fusion), channel_id=1, replica_groups=mesh['fsdp'=4,'seq'=8] {'fsdp','seq'}, dimensions={0}, use_global_device_ids=true | all-gather | bytes 15840 | tf_op jit(solution)/shard_map/all_gather | solution.py:38
  55.4 61.7 %all-gather.7.cloned.1.call-done = bf16[1536,4608]{0,1:T(8,128)(2,1)} async-done(((bf16[1536,144]{0,1:T(8,128)(2,1)}), bf16[1536,4608]{0,1:T(8,128)(2,1)}) %all-gather.7.cloned.1.call-update) | async-done | bytes 14155792 | tf_op jit(solution)/shard_map/all_gather | solution.py:36
  117.1 7.1 fusion.19
  124.4 2.2 collective-permute-start
  129.3 52.7 %all-gather.9.cloned.1.call-done = bf16[1536,1536]{0,1:T(8,128)(2,1)} async-done(((bf16[1536,48]{0,1:T(8,128)(2,1)}), bf16[1536,1536]{0,1:T(8,128)(2,1)}) %all-gather.9.cloned.1.call-update) | async-done | bytes 4718608 | tf_op jit(solution)/shard_map/all_gather | solution.py:37
  181.9 4.3 multiply_reduce_fusion.7
  188.5 131.3 %all-gather.11.cloned.1.call-done = bf16[1536,6912]{0,1:T(8,128)(2,1)} async-done(((bf16[1536,216]{0,1:T(8,128)(2,1)}), bf16[1536,6912]{0,1:T(8,128)(2,1)}) %all-gather.11.cloned.1.call-update) | async-done | bytes 21233680 | tf_op jit(solution)/shard_map/all_gather | solution.py:41
  319.7 12.6 fusion.20
  332.3 124.4 %all-gather.13.cloned.1.call-done = bf16[1536,6912]{0,1:T(8,128)(2,1)} async-done(((bf16[1536,216]{0,1:T(8,128)(2,1)}), bf16[1536,6912]{0,1:T(8,128)(2,1)}) %all-gather.13.cloned.1.call-update) | async-done | bytes 21233680 | tf_op jit(solution)/shard_map/all_gather | solution.py:42
  456.7 12.1 fusion.21
  468.8 124.9 %all-gather.15.cloned.1.call-done = bf16[6912,1536]{0,1:T(8,128)(2,1)} async-done(((bf16[6912,48]{0,1:T(8,128)(2,1)}), bf16[6912,1536]{0,1:T(8,128)(2,1)}) %all-gather.15.cloned.1.call-update) | async-done | bytes 21233680 | tf_op jit(solution)/shard_map/all_gather | solution.py:43
  593.7 17.5 multiply_convert_fusion
  611.2 11.1 fusion.22
  622.4 10.5 multiply_reduce_fusion.3
  633.5 1.8 multiply_reduce_fusion
  637.8 5.1 fusion.13
  644.6 10.7 multiply_reduce_fusion.4
  655.3 8.2 pad_maximum_fusion.1
  663.5 10.6 copy.39
  675.2 21.0 fusion.24
  696.2 18.7 fusion.23
  714.9 56.3 %pad_maximum_fusion = f32[6912,3072]{0,1:T(8,128)} fusion(f32[6912,1536]{0,1:T(8,128)} %fusion.24, f32[6912,1536]{0,1:T(8,128)} %fusion.23), kind=kLoop, calls=%fused_computation | loop fusion | flops 21233664 | bytes 169869312 | tf_op jit(solution)/shard_map/concatenate | solution.py:96
  772.6 11.5 fusion.11
  784.1 1.9 copy-done.10
  786.1 18.1 convolution_bitcast_fusion
  804.2 42.7 %copy.43 = f32[1536,6912]{1,0:T(8,128)} copy(f32[1536,6912]{0,1:T(8,128)} %convolution_bitcast_fusion) | data formatting | bytes 84934656
  848.3 12.2 fusion.1
  863.9 1.7 slice_bitcast_fusion
  865.6 1138.1 %all-reduce.3.cloned.1.call-done = f32[6912,3072]{0,1:T(8,128)} async-done(((f32[6912,3072]{0,1:T(8,128)}), f32[6912,3072]{0,1:T(8,128)}) %all-reduce.3.cloned.1.call-update) | async-done | bytes 84934672
  2003.6 3.3 dynamic-slice_bitcast_fusion
  2010.0 264.5 %reduce-scatter.9.cloned.1.call-done = f32[144,1536]{1,0:T(8,128)} async-done(((f32[4608,1536]{1,0:T(8,128)}), f32[144,1536]{1,0:T(8,128)}) %reduce-scatter.9.cloned.1.call-update) | async-done | bytes 884752 | tf_op jit(solution)/shard_map/reduce_scatter | solution.py:134
  2274.4 385.3 %reduce-scatter.13.cloned.1.call-done = f32[48,6912]{1,0:T(8,128)} async-done(((f32[1536,6912]{1,0:T(8,128)}), f32[48,6912]{1,0:T(8,128)}) %reduce-scatter.13.cloned.1.call-update) | async-done | bytes 1327120
  (121 shorter events, 24.1 us)
Async XLA Ops:
  7.2 3.5 copy-start.25
  7.2 47.7 %copy-start.4 = (bf16[2,128,1536]{2,1,0:T(8,128)(2,1)S(1)}, bf16[2,128,1536]{2,1,0:T(8,128)(2,1)}, u32[]{:S(2)}) copy-start(bf16[2,128,1536]{2,1,0:T(8,128)(2,1)} %param.10) | copy-start | bytes 2359300
  7.2 109.9 %all-gather.7.cloned.1.call-start = ((), (), s32[]{:S(2)}) async-start(), calls=%async_computation.3 | async-start | bytes 14598144 | tf_op jit(solution)/shard_map/all_gather | solution.py:36
  8.0 174.0 %all-gather.9.cloned.1.call-start = ((), (), s32[]{:S(2)}) async-start(), calls=%async_computation.4 | async-start | bytes 4866048 | tf_op jit(solution)/shard_map/all_gather | solution.py:37
  8.7 311.0 %all-gather.11.cloned.1.call-start = ((), (), s32[]{:S(2)}) async-start(), calls=%async_computation.5 | async-start | bytes 21897216 | tf_op jit(solution)/shard_map/all_gather | solution.py:41
  9.4 447.3 %all-gather.13.cloned.1.call-start = ((), (), s32[]{:S(2)}) async-start(), calls=%async_computation.6 | async-start | bytes 21897216 | tf_op jit(solution)/shard_map/all_gather | solution.py:42
  10.0 583.7 %all-gather.15.cloned.1.call-start = ((), (), s32[]{:S(2)}) async-start(), calls=%async_computation.7 | async-start | bytes 21897216 | tf_op jit(solution)/shard_map/all_gather | solution.py:43
  10.6 851.3 %reduce-scatter.11.cloned.1.call-start = ((), (), s32[]{:S(2)}) async-start(), calls=%async_computation.9 | async-start | bytes 10543104
  54.9 589.1 %copy-start.20 = (f32[1536]{0:T(1024)}, f32[1536]{0:T(1024)S(1)}, u32[]{:S(2)}) copy-start(f32[1536]{0:T(1024)S(1)} %get-tuple-element.61) | copy-start | bytes 18436
  55.1 588.8 %copy-start.22 = (f32[256]{0:T(256)}, f32[256]{0:T(256)S(1)}, u32[]{:S(2)}) copy-start(f32[256]{0:T(256)S(1)} %rsqrt_bitcast_fusion) | copy-start | bytes 3076
  55.4 68.8 %copy-start.14 = (bf16[256,1536]{1,0:T(8,128)(2,1)}, bf16[256,1536]{1,0:T(8,128)(2,1)S(1)}, u32[]{:S(2)}) copy-start(bf16[256,1536]{1,0:T(8,128)(2,1)S(1)} %multiply_convert_fusion.5) | copy-start | bytes 2359300
  124.2 3.9 copy-start.2
  124.4 3.0 collective-permute-start
  611.2 11.2 copy-start.8
  611.2 11.2 copy-start.12
  611.2 22.2 slice-start
  611.2 22.2 slice-start.2
  622.4 10.5 copy-start.13
  622.4 11.0 slice-start.1
  622.4 11.0 slice-start.3
  635.3 7.6 collective-permute-start.1
  637.8 6.2 copy-start.16
  674.1 1329.5 %all-reduce.3.cloned.1.call-start = ((), (), s32[]{:S(2)}) async-start(), calls=%async_computation.11 | async-start | bytes 169869312
  675.2 21.0 copy-start.11
  771.3 1503.1 %reduce-scatter.9.cloned.1.call-start = ((), (), s32[]{:S(2)}) async-start(), calls=%async_computation.8 | async-start | bytes 29196288 | tf_op jit(solution)/shard_map/reduce_scatter | solution.py:134
  784.1 1875.6 %reduce-scatter.13.cloned.1.call-start = ((), (), s32[]{:S(2)}) async-start(), calls=%async_computation.10 | async-start | bytes 43794432
  848.3 12.2 copy-start.24
  848.3 12.2 copy-start.1
  848.3 12.2 copy-start.6
  848.3 12.2 copy-start.19
  848.3 12.2 copy-start.21
  848.3 12.2 copy-start.23
  (11 other events, 20.9 us)
Sparse Core Ops, SparseCore 0:
  11.1 105.9 all-gather.6
  120.1 61.7 all-gather.8
  185.0 134.7 all-gather.10
  322.6 134.0 all-gather.12
  459.6 134.0 all-gather.14
  674.2 139.4 reduce-scatter.10
  820.2 1183.4 all-reduce.2
  2010.6 263.7 reduce-scatter.8
  2281.4 378.2 reduce-scatter.12
where the time goes:
time: 2670 us
  waiting for transfers between devices  2290 us (86%)
  matrix products  174 us (7%)
  local copies, waits for them, and re-layouts  71.8 us (3%)
  other arithmetic  71.3 us (3%)
  blocking collectives  44 us (2%)
    unnamed x12, waiting for transfers between devices  1530 us
    reduce_scatter x1, waiting for transfers between devices, on_device(): lax.psum_scatter(left_trans(dmixed, normed_a), ('fsdp', 'seq'), scatter_d...  264 us
    all_gather x1, waiting for transfers between devices, on_device(): lax.all_gather(w_gate, ('fsdp', 'seq'), axis=1, tiled=True)  131 us
    all_gather x1, waiting for transfers between devices, on_device(): lax.all_gather(w_down, ('fsdp', 'seq'), axis=1, tiled=True)  125 us
    all_gather x1, waiting for transfers between devices, on_device(): lax.all_gather(w_up, ('fsdp', 'seq'), axis=1, tiled=True)  124 us
    dot_general x5, matrix products, left_trans(): lax.dot_general(left, right, (((0,), (0,)), ((), ())), preferred_element_...  74.4 us
    unnamed x69, local copies, waits for them, and re-layouts  64.7 us
    all_gather x1, waiting for transfers between devices, on_device(): lax.all_gather(w_in, ('fsdp', 'seq'), axis=1, tiled=True)  61.7 us
  transfers between devices with their start and end apart: 11, of which 9 were waited for; matrix products, arithmetic and copies ran while one was open for 9% of the time, Pallas kernels for 0%

commit v1 on v0

v1 whole, which is shorter than its diff:
```python
import jax
import jax.numpy as jnp
from jax import lax
from jax.sharding import Mesh, PartitionSpec as P

epsilon = 1e-05
every = ("fsdp", "line", "core")
bf16 = jnp.bfloat16
f32 = jnp.float32


def product(left, right):
    return jnp.dot(left, right, preferred_element_type=f32)


def right_trans(left, right):
    return lax.dot_general(left, right, (((1,), (1,)), ((), ())), preferred_element_type=f32)


def left_trans(left, right):
    return lax.dot_general(left, right, (((0,), (0,)), ((), ())), preferred_element_type=f32)


def cuts(rows, parts):
    ends = [min(rows, -(-rows * (p + 1) // (16 * parts)) * 16) for p in range(parts)]
    return list(zip([0] + ends[:-1], ends))


def flip(block, axis, bit):
    size = lax.axis_size(axis)
    return lax.ppermute(block, axis, [(i, i ^ bit) for i in range(size)])


def cube_gather(block, axis):
    size = lax.axis_size(axis)
    bits = size.bit_length() - 1
    held = [{0: block[a:b]} for a, b in cuts(block.shape[0], bits)]
    for step in range(bits):
        for p in range(bits):
            bit = 1 << (p + step) % bits
            slots = sorted(held[p])
            other = flip(jnp.stack([held[p][r] for r in slots]), axis, bit)
            held[p].update({r ^ bit: other[n] for n, r in enumerate(slots)})
    return jnp.stack([jnp.concatenate([h[r] for h in held], 0) for r in range(size)])


def cube_scatter(slots, axis):
    size = lax.axis_size(axis)
    bits = size.bit_length() - 1
    held = [{r: slots[r, a:b] for r in range(size)} for a, b in cuts(slots.shape[1], bits)]
    for step in reversed(range(bits)):
        for p in range(bits):
            bit = 1 << (p + step) % bits
            keep = sorted(r for r in held[p] if not r & bit)
            other = flip(jnp.stack([held[p][r | bit].astype(bf16) for r in keep]), axis, bit)
            held[p] = {r: held[p][r] + other[n].astype(f32) for n, r in enumerate(keep)}
    return jnp.concatenate([h[0] for h in held], 0)


def line_gather(block, axis):
    size = lax.axis_size(axis)
    me = lax.axis_index(axis)
    up = [(i, i + 1) for i in range(size - 1)]
    down = [(i + 1, i) for i in range(size - 1)]
    left, right = [block], [block]
    for s in range(1, size):
        left.append(lax.ppermute(left[-1], axis, up[s - 1 :]))
        right.append(lax.ppermute(right[-1], axis, down[: size - s]))
    return jnp.stack([block] + [jnp.where(me >= s, left[s], right[size - s]) for s in range(1, size)])


def line_scatter(slots, axis):
    size = lax.axis_size(axis)
    up = [(i, i + 1) for i in range(size - 1)]
    down = [(i + 1, i) for i in range(size - 1)]
    left = right = None
    for t in range(1, size):
        to_left = slots[size - t] if left is None else slots[size - t] + left.astype(f32)
        to_right = slots[t] if right is None else slots[t] + right.astype(f32)
        left = lax.ppermute(to_left.astype(bf16), axis, down[size - 1 - t :])
        right = lax.ppermute(to_right.astype(bf16), axis, up[:t])
    return slots[0] + left.astype(f32) + right.astype(f32)


def exchange(blocks, axis):
    size = lax.axis_size(axis)
    me = lax.axis_index(axis)
    own = lax.dynamic_index_in_dim(blocks, me, 0, keepdims=False)
    got = jnp.zeros_like(blocks)
    got = lax.dynamic_update_index_in_dim(got, own, me, 0)
    for k in range(1, size):
        sent = lax.dynamic_index_in_dim(blocks, (me + k) % size, 0, keepdims=False)
        came = lax.ppermute(sent, axis, [(i, (i + k) % size) for i in range(size)])
        got = lax.dynamic_update_index_in_dim(got, came, (me - k) % size, 0)
    return got


def on_device(tokens, gain_one, gain_two, conv_taps, w_in, w_out, w_gate, w_up, w_down, cotangent):
    seqs, group, width = tokens.shape
    rows = seqs * group
    lanes, line = lax.axis_size("fsdp"), lax.axis_size("line")
    pieces = 2 * line
    count = lanes * pieces
    feats = width // count
    mine = width // lanes
    hid = w_gate.shape[1]
    wide = lanes * 2 * hid
    f_index = lax.axis_index("fsdp")
    index = lax.axis_index(every)

    in_blocks = w_in.T.reshape(3, feats, width)
    routes = [[(k, (3 * k + j) % count) for k in range(count)] for j in range(3)]
    came = jnp.stack([lax.ppermute(in_blocks[j], every, routes[j]) for j in range(3)])
    in_parts = [
        lax.dynamic_index_in_dim(came, (index + p * count) % 3, 0, keepdims=False) for p in range(3)
    ]
    smalls = jnp.concatenate([gain_one[None], gain_two[None], conv_taps], 0)
    smalls = jnp.pad(smalls, ((0, 11), (0, mine - feats)))
    out_blocks = w_out.T.reshape(feats, lanes, mine).transpose(1, 0, 2)
    out_blocks = jnp.concatenate([out_blocks, jnp.broadcast_to(smalls, (lanes, 16, mine))], 1)
    out_blocks = exchange(out_blocks, "fsdp").transpose(1, 0, 2).reshape(feats + 16, width)
    mixer_w = lax.all_gather(
        jnp.concatenate(in_parts + [out_blocks], 0), ("line", "core"), axis=0
    )
    full_in = mixer_w[:, : 3 * feats].reshape(pieces, 3, feats, width)
    full_in = full_in.transpose(1, 0, 2, 3).reshape(3, mine, width)
    full_out = mixer_w[:, 3 * feats : 4 * feats].reshape(pieces, feats, lanes, mine)
    full_out = full_out.transpose(2, 0, 1, 3).reshape(width, mine)
    small = mixer_w[:, 4 * feats : 4 * feats + 5].reshape(pieces, 5, lanes, mine)[..., :feats]
    small = small.transpose(1, 2, 0, 3).reshape(5, width).astype(f32)
    taps = lax.dynamic_slice_in_dim(small[2:], f_index * mine, mine, 1)

    down_blocks = w_down.reshape(lanes, line, 2 * hid, feats).transpose(1, 3, 0, 2)
    down_blocks = exchange(down_blocks.reshape(line, feats, wide), "line")
    full_down = lax.all_gather(down_blocks, ("fsdp", "core"), axis=0)
    full_down = full_down.reshape(lanes, 2, line, feats, wide).transpose(0, 2, 1, 3, 4)
    full_down = full_down.reshape(width, wide)
    gate_up = lax.all_gather(
        jnp.concatenate([w_gate.T, w_up.T], 0), ("fsdp", "core"), axis=0
    )
    full_gate = gate_up[:, :hid].reshape(wide, width)
    full_up = gate_up[:, hid:].reshape(wide, width)

    token_rows = tokens.reshape(rows, width)
    all_tokens = cube_gather(token_rows, "fsdp").reshape(lanes * rows, width)
    all_in = all_tokens.astype(f32)
    scale_all = lax.rsqrt(jnp.mean(all_in * all_in, axis=-1, keepdims=True) + epsilon)
    unit_all = all_in * scale_all
    normed_a = (unit_all * small[0]).astype(bf16)
    b_part = right_trans(normed_a, full_in[0])
    c_part = right_trans(normed_a, full_in[1])
    x_part = right_trans(normed_a, full_in[2])
    every_seq = lanes * seqs
    gated = (b_part * x_part).astype(bf16).reshape(every_seq, group, mine)
    onward = [(i, i + 1) for i in range(pieces - 1)]
    back = [(i + 1, i) for i in range(pieces - 1)]
    before = lax.ppermute(gated[:, group - 2 :, :], ("line", "core"), onward)
    extended = jnp.concatenate([before, gated], 1).astype(f32)
    conv = (
        taps[0] * extended[:, :group]
        + taps[1] * extended[:, 1 : group + 1]
        + taps[2] * extended[:, 2:]
    ).reshape(lanes * rows, mine)
    branch_y = (c_part * conv).astype(bf16)
    branch_o = cube_scatter(
        right_trans(branch_y, full_out).reshape(lanes, rows, width), "fsdp"
    )
    hidden_in = token_rows.astype(f32)
    second = hidden_in + branch_o
    scale_two = lax.rsqrt(jnp.mean(second * second, axis=-1, keepdims=True) + epsilon)
    unit_two = second * scale_two
    normed_u = (unit_two * small[1]).astype(bf16)

    cot_rows = cotangent.reshape(rows, width)
    all_cot = line_gather(cot_rows, "line").reshape(line * rows, width)
    dhidden = product(all_cot, full_down)
    all_u = line_gather(normed_u, "line").reshape(line * rows, width)
    gate_val = right_trans(all_u, full_gate)
    up_val = right_trans(all_u, full_up)
    sigmoid_g = jax.nn.sigmoid(gate_val)
    silu_g = gate_val * sigmoid_g
    hidden = (silu_g * up_val).astype(bf16)
    dgate = (dhidden * up_val * sigmoid_g * (1.0 + gate_val * (1.0 - sigmoid_g))).astype(bf16)
    dup_val = (dhidden * silu_g).astype(bf16)
    dunit = product(dgate, full_gate) + product(dup_val, full_up)
    dunit = line_scatter(dunit.reshape(line, rows, width), "line")
    part_out = right_trans(hidden, full_down)
    part_out = line_scatter(part_out.reshape(line, rows, width), "line")
    block_out = (second + part_out).astype(bf16).reshape(seqs, group, width)

    g_down = left_trans(all_cot, hidden).astype(bf16)
    g_down = g_down.reshape(lanes, line, 2, feats, wide).transpose(0, 2, 1, 3, 4)
    g_down = lax.psum_scatter(
        g_down.reshape(lanes * 2, line, feats, wide), ("fsdp", "core"), scatter_dimension=0
    )
    g_down = exchange(g_down, "line").reshape(line, feats, lanes, 2 * hid)
    grad_down = g_down.transpose(2, 0, 3, 1).reshape(count * hid, feats).astype(f32)
    g_gate = left_trans(dgate, all_u).astype(bf16).reshape(lanes * 2, hid, width)
    g_up = left_trans(dup_val, all_u).astype(bf16).reshape(lanes * 2, hid, width)
    g_gu = lax.psum_scatter(
        jnp.concatenate([g_gate, g_up], 1), ("fsdp", "core"), scatter_dimension=0
    )
    grad_gate = g_gu[:hid].T.astype(f32)
    grad_up = g_gu[hid:].T.astype(f32)

    grad_two = jnp.sum(dunit * unit_two, axis=0)
    dnorm_two = dunit * small[1]
    dsecond = cot_rows.astype(f32) + scale_two * (
        dnorm_two - unit_two * jnp.mean(dnorm_two * unit_two, axis=-1, keepdims=True)
    )
    all_branch = cube_gather(dsecond.astype(bf16), "fsdp").reshape(lanes * rows, width)
    dy_rows = product(all_branch, full_out)
    dconv = (dy_rows * c_part).reshape(every_seq, group, mine)
    dc_part = dy_rows * conv
    after = lax.ppermute(dconv[:, :2, :], ("line", "core"), back)
    dext = jnp.concatenate([dconv, after], 1)
    dgated = (
        taps[2] * dext[:, :group] + taps[1] * dext[:, 1 : group + 1] + taps[0] * dext[:, 2:]
    ).reshape(lanes * rows, mine)
    grad_taps = jnp.stack(
        [jnp.sum(dconv * extended[:, k : k + group], axis=(0, 1)) for k in range(3)], 0
    )
    dmixed = [(dgated * x_part).astype(bf16), dc_part.astype(bf16), (dgated * b_part).astype(bf16)]
    dnormed = sum(product(dmixed[p], full_in[p]) for p in range(3))
    grad_one = jnp.sum(dnormed * unit_all, axis=0)
    dnormed = cube_scatter(dnormed.reshape(lanes, rows, width), "fsdp")
    scale_one = lax.rsqrt(jnp.mean(hidden_in * hidden_in, axis=-1, keepdims=True) + epsilon)
    unit_one = hidden_in * scale_one
    dnorm_one = dnormed * small[0]
    dinput = dsecond + scale_one * (
        dnorm_one - unit_one * jnp.mean(dnorm_one * unit_one, axis=-1, keepdims=True)
    )
    grad_tokens = dinput.astype(bf16).reshape(seqs, group, width)

    g_in = jnp.stack([left_trans(d, normed_a).astype(bf16) for d in dmixed])
    g_in = g_in.reshape(3, pieces, feats, width).transpose(1, 0, 2, 3)
    g_out = left_trans(all_branch, branch_y).astype(bf16).reshape(lanes, pieces, feats, mine)
    g_out = g_out.transpose(1, 2, 0, 3).reshape(pieces, feats, width)
    gains = jnp.stack([grad_one, grad_two]).reshape(2, lanes, pieces, feats)
    gains = gains.transpose(2, 1, 0, 3).reshape(pieces, lanes * 2 * feats)
    g_taps = grad_taps.reshape(3, pieces, feats).transpose(1, 0, 2).reshape(pieces, 3 * feats)
    g_small = jnp.concatenate([gains, g_taps], 1)
    g_small = jnp.pad(g_small[:, None], ((0, 0), (0, 15), (0, width - g_small.shape[1])))
    g_mixer = lax.psum_scatter(
        jnp.concatenate(
            [g_in.reshape(pieces, 3 * feats, width), g_out, g_small.astype(bf16)], 1
        ),
        ("line", "core"),
        scatter_dimension=0,
    )
    g_in = g_mixer[: 3 * feats].reshape(3, feats, width)
    homes = [[(d, k) for k, d in route] for route in routes]
    parts = []
    for j in range(3):
        p = ((j - index) * pow(count, -1, 3)) % 3
        block = lax.dynamic_index_in_dim(g_in, p, 0, keepdims=False)
        parts.append(lax.ppermute(block, every, homes[j]))
    grad_in = jnp.concatenate(parts, 0).T.astype(f32)
    g_out = g_mixer[3 * feats : 4 * feats].reshape(feats, lanes, mine).transpose(1, 0, 2)
    g_small = g_mixer[4 * feats]
    gains = g_small[: lanes * 2 * feats].reshape(lanes, 1, 2 * feats)
    gains = jnp.pad(gains, ((0, 0), (0, 15), (0, mine - 2 * feats)))
    got = exchange(jnp.concatenate([g_out, gains], 1), "fsdp")
    grad_out = got[:, :feats].transpose(0, 2, 1).reshape(width, feats).astype(f32)
    gains = jnp.sum(got[:, feats].astype(f32), axis=0)
    grad_taps = g_small[lanes * 2 * feats :][: 3 * feats].reshape(3, feats).astype(f32)
    return (
        block_out,
        grad_tokens,
        gains[:feats],
        gains[feats : 2 * feats],
        grad_taps,
        grad_in,
        grad_out,
        grad_gate,
        grad_up,
        grad_down,
    )


def solution(mesh):
    lanes, pieces = mesh.devices.shape
    fine = Mesh(mesh.devices.reshape(lanes, pieces // 2, 2), every)
    token = P("fsdp", ("line", "core"), None)
    vector = P(every)
    columns = P(None, every)
    return jax.shard_map(
        on_device,
        mesh=fine,
        in_specs=(token, vector, vector) + (columns,) * 6 + (token,),
        out_specs=(token, token, vector, vector) + (columns,) * 6,
        check_vma=False,
    )
```

time: 2670 us -> 709 us (0.27)
  waiting for transfers between devices: 2290 us -> 247 us
  starting transfers between devices: 3.82 us -> 159 us
  matrix products: 174 us -> 118 us
  blocking collectives: 44 us -> 0 us
    unnamed x12 -> x6, waiting for transfers between devices: 1530 us -> 0.1 us
    all_gather x5 -> x3, waiting for transfers between devices: 495 us -> 1.62 us  [the longest x1 1.62 us: on_device(): lax.all_gather(jnp.concatenate(in_parts + [out_blocks], 0), ('line', 'cor...]
    reduce_scatter x1 -> x3, waiting for transfers between devices: 264 us -> 42.3 us  [the longest x1 42.3 us: on_device(): lax.psum_scatter(jnp.concatenate([g_gate, g_up], 1), ('fsdp', 'core'), sc...]
    ppermute x2 -> x60, waiting for transfers between devices: 0.82 us -> 203 us  [the longest x16 92 us: flip(): return lax.ppermute(block, axis, [(i, i ^ bit) for i in range(size)])]
    ppermute x2 -> x60, starting transfers between devices: 3.46 us -> 158 us  [the longest x6 50.7 us: line_scatter(): right = lax.ppermute(to_right.astype(bf16), axis, up[:t])]
    concatenate x2 -> x9, other arithmetic: 64.6 us -> 13.2 us  [the longest x1 6.66 us: on_device(): jnp.concatenate([g_gate, g_up], 1)]
    dot_general x5 -> x7, matrix products: 74.4 us -> 29.8 us  [left_trans(): lax.dot_general(left, right, (((0,), (0,)), ((), ())), preferred_element_...]
    unnamed x69 -> x156, local copies, waits for them, and re-layouts: 64.7 us -> 20.3 us
  transfers between devices with their start and end apart: 11 -> 66, of which waited for: 9 -> 30; matrix products, arithmetic and copies ran while one was open for 9% -> 27% of each run, Pallas kernels for 0% -> 0%
where the time goes in v1:
time: 709 us; the launch traced here: 698 us
  waiting for transfers between devices  247 us (35%)
  starting transfers between devices  159 us (22%)
  matrix products  118 us (17%)
  local copies, waits for them, and re-layouts  97.5 us (14%)
  other arithmetic  61 us (9%)
  between operations  16.3 us (2%)
    ppermute x16, waiting for transfers between devices, flip(): return lax.ppermute(block, axis, [(i, i ^ bit) for i in range(size)])  92 us
    dot_general x7, matrix products, product(): return jnp.dot(left, right, preferred_element_type=f32)  52.2 us
    ppermute x6, starting transfers between devices, line_scatter(): right = lax.ppermute(to_right.astype(bf16), axis, up[:t])  50.7 us
    reduce_scatter x1, waiting for transfers between devices, on_device(): lax.psum_scatter(jnp.concatenate([g_gate, g_up], 1), ('fsdp', 'core'), sc...  42.3 us
    ppermute x6, waiting for transfers between devices, line_scatter(): right = lax.ppermute(to_right.astype(bf16), axis, up[:t])  39.7 us
    dot_general x7, matrix products, right_trans(): lax.dot_general(left, right, (((1,), (1,)), ((), ())), preferred_element_...  36.1 us
    ppermute x6, waiting for transfers between devices, line_gather(): right.append(lax.ppermute(right[-1], axis, down[:size - s]))  31.1 us
    dot_general x7, matrix products, left_trans(): lax.dot_general(left, right, (((0,), (0,)), ((), ())), preferred_element_...  29.8 us
  transfers between devices with their start and end apart: 66, of which 30 were waited for; matrix products, arithmetic and copies ran while one was open for 27% of the time, Pallas kernels for 0%

profile of v1, /device:TPU:0, one launch (start us, length us, event | category | flops | bytes accessed | tf_op | source)
XLA Modules:
  0.0 698.3 jit_solution(16566627166858268890)
XLA Ops:
  43.6 7.1 %collective-permute-done.21 = bf16[48,1728]{1,0:T(8,128)(2,1)S(1)} collective-permute-done((bf16[48,1728]{1,0:T(8,128)(2,1)}, bf16[48,1728]{1,0:T(8,128)(2,1)S(1)}, u32[]{:S(2)}, u32[]{:S(2)}) %collective-permute-start.21) | collective-permute-done | bytes 165920 | tf_op jit(solution)/shard_map/ppermute | solution.py:93
  50.7 12.5 %collective-permute-done.22 = bf16[48,1728]{1,0:T(8,128)(2,1)S(1)} collective-permute-done((bf16[48,1728]{1,0:T(8,128)(2,1)}, bf16[48,1728]{1,0:T(8,128)(2,1)S(1)}, u32[]{:S(2)}, u32[]{:S(2)}) %collective-permute-start.22) | collective-permute-done | bytes 165920 | tf_op jit(solution)/shard_map/ppermute | solution.py:93
  67.6 9.1 %collective-permute-done.1 = bf16[1,128,1536]{2,1,0:T(8,128)(2,1)S(1)} collective-permute-done((bf16[1,128,1536]{2,1,0:T(8,128)(2,1)S(1)}, bf16[1,128,1536]{2,1,0:T(8,128)(2,1)S(1)}, u32[]{:S(2)}, u32[]{:S(2)}) %collective-permute-start.1) | collective-permute-done | bytes 393248 | tf_op jit(solution)/shard_map/ppermute | solution.py:31
  78.8 16.6 %collective-permute-done.2 = bf16[2,128,1536]{2,1,0:T(8,128)(2,1)S(1)} collective-permute-done((bf16[2,128,1536]{2,1,0:T(8,128)(2,1)S(1)}, bf16[2,128,1536]{2,1,0:T(8,128)(2,1)S(1)}, u32[]{:S(2)}, u32[]{:S(2)}) %collective-permute-start.2) | collective-permute-done | bytes 786464 | tf_op jit(solution)/shard_map/ppermute | solution.py:31
  130.9 14.7 %collective-permute-start.30 = (bf16[256,1536]{1,0:T(8,128)(2,1)S(1)}, bf16[256,1536]{1,0:T(8,128)(2,1)S(1)}, u32[]{:S(2)}, u32[]{:S(2)}) collective-permute-start(bf16[256,1536]{1,0:T(8,128)(2,1)S(1)} %bitcast.385), channel_id=1, source_target_pairs={{0,2},{2,4},{4,6},{1,3},{3,5},{5,7},{8,10},{10,12},{12,14},{9,11},... | collective-permute-start | bytes 2359304 | tf_op jit(solution)/shard_map/ppermute | solution.py:67
  155.1 6.9 collective-permute-done.30
  168.7 15.0 %collective-permute-done.12 = bf16[1,128,1536]{2,1,0:T(8,128)(2,1)S(1)} collective-permute-done((bf16[1,128,1536]{2,1,0:T(8,128)(2,1)S(1)}, bf16[1,128,1536]{2,1,0:T(8,128)(2,1)S(1)}, u32[]{:S(2)}, u32[]{:S(2)}) %collective-permute-start.12) | collective-permute-done | bytes 393248 | tf_op jit(solution)/shard_map/ppermute | solution.py:31
  195.4 6.7 collective-permute-start.15
  213.6 8.7 %collective-permute-done.16 = bf16[256,1536]{1,0:T(8,128)(2,1)} collective-permute-done((bf16[256,1536]{1,0:T(8,128)(2,1)S(1)}, bf16[256,1536]{1,0:T(8,128)(2,1)}, u32[]{:S(2)}, u32[]{:S(2)}) %collective-permute-start.16) | collective-permute-done | bytes 786464 | tf_op jit(solution)/shard_map/ppermute | solution.py:68
  232.3 7.7 %collective-permute-done.17 = bf16[256,1536]{1,0:T(8,128)(2,1)} collective-permute-done((bf16[256,1536]{1,0:T(8,128)(2,1)}, bf16[256,1536]{1,0:T(8,128)(2,1)}, u32[]{:S(2)}, u32[]{:S(2)}) %collective-permute-start.17) | collective-permute-done | bytes 786464 | tf_op jit(solution)/shard_map/ppermute | solution.py:68
  244.1 12.0 %collective-permute-done.18 = bf16[256,1536]{1,0:T(8,128)(2,1)S(1)} collective-permute-done((bf16[256,1536]{1,0:T(8,128)(2,1)}, bf16[256,1536]{1,0:T(8,128)(2,1)S(1)}, u32[]{:S(2)}, u32[]{:S(2)}) %collective-permute-start.18) | collective-permute-done | bytes 786464 | tf_op jit(solution)/shard_map/ppermute | solution.py:68
  258.1 9.1 %fusion.59 = (bf16[8,216,1536]{2,1,0:T(8,128)(2,1)}, bf16[8,216,1536]{2,1,0:T(8,128)(2,1)}) fusion(bf16[8,432,1536]{2,1,0:T(8,128)(2,1)} %bitcast.359), kind=kLoop, calls=%fused_computation.227 | loop fusion | bytes 21233664 | tf_op jit(solution)/shard_map/slice | solution.py:141
  267.2 10.8 %fusion.70 = f32[1024,1728]{0,1:T(8,128)} fusion(bf16[1024,1536]{1,0:T(8,128)(2,1)} %bitcast.388, bf16[1728,1536]{1,0:T(8,128)(2,1)} %bitcast.368), kind=kOutput, calls=%fused_computation.238 | convolution fusion | flops 5435817984 | bytes 15532032 | tf_op jit(solution)/shard_map/dot_general | solution.py:17
  278.1 7.6 %fusion.71 = f32[1024,1728]{0,1:T(8,128)} fusion(bf16[1024,1536]{1,0:T(8,128)(2,1)S(1)} %bitcast.390, bf16[1728,1536]{1,0:T(8,128)(2,1)S(1)} %bitcast.354), kind=kOutput, calls=%fused_computation.239 | convolution fusion | flops 5435817984 | bytes 15532032 | tf_op jit(solution)/shard_map/dot_general | solution.py:17
  285.7 17.5 %multiply_convert_fusion = (bf16[1024,1728]{0,1:T(8,128)(2,1)}, bf16[1024,1728]{0,1:T(8,128)(2,1)}, bf16[1024,1728]{0,1:T(8,128)(2,1)}) fusion(f32[1024,1728]{0,1:T(8,128)} %fusion.70, f32[1024,1728]{0,1:T(8,128)} %fusion.71, bf16[1024,1536]{1,0:T(8,128)(2,1)} %bitcast.392, bf16[1536,1728]{1,0:T(8,128)(2,1)} %bitcast.366), kind=kOutput, calls=%fused_computation.6 | convolution fusion | flops 5462360064 | bytes 33226752 | tf_op jit(solution)/shard_map/dot_general | solution.py:13
  303.2 9.6 %fusion.73 = f32[1024,1536]{1,0:T(8,128)S(1)} fusion(bf16[1024,1728]{0,1:T(8,128)(2,1)} %get-tuple-element.24, bf16[1728,1536]{1,0:T(8,128)(2,1)} %bitcast.369), kind=kOutput, calls=%fused_computation.241 | convolution fusion | flops 5435817984 | bytes 15138816 | tf_op jit(solution)/shard_map/dot_general | solution.py:13
  312.8 8.6 %convolution_add_fusion = f32[1024,1536]{1,0:T(8,128)S(1)} fusion(f32[1024,1536]{1,0:T(8,128)S(1)} %fusion.73, bf16[1024,1728]{0,1:T(8,128)(2,1)S(1)} %copy-done.26, bf16[1728,1536]{1,0:T(8,128)(2,1)} %bitcast.353), kind=kOutput, calls=%fused_computation.18 | convolution fusion | flops 5437390848 | bytes 21430272 | tf_op jit(solution)/shard_map/dot_general | solution.py:13
  322.3 8.1 %fusion.72 = f32[1024,1536]{1,0:T(8,128)S(1)} fusion(bf16[1024,1728]{0,1:T(8,128)(2,1)S(1)} %copy-done.72, bf16[1536,1728]{1,0:T(8,128)(2,1)} %bitcast.367), kind=kOutput, calls=%fused_computation.240 | convolution fusion | flops 5435817984 | bytes 15138816 | tf_op jit(solution)/shard_map/dot_general | solution.py:17
  337.7 14.2 %collective-permute-done.39 = bf16[256,1536]{1,0:T(8,128)(2,1)S(1)} collective-permute-done((bf16[256,1536]{1,0:T(8,128)(2,1)S(1)}, bf16[256,1536]{1,0:T(8,128)(2,1)S(1)}, u32[]{:S(2)}, u32[]{:S(2)}) %collective-permute-start.39) | collective-permute-done | bytes 786464 | tf_op jit(solution)/shard_map/ppermute | solution.py:81
  352.4 11.9 %collective-permute-start.40 = (bf16[256,1536]{1,0:T(8,128)(2,1)S(1)}, bf16[256,1536]{1,0:T(8,128)(2,1)S(1)}, u32[]{:S(2)}, u32[]{:S(2)}) collective-permute-start(bf16[256,1536]{1,0:T(8,128)(2,1)S(1)} %get-tuple-element.31), channel_id=1, source_target_pairs={{0,2},{2,4},{1,3},{3,5},{8,10},{10,12},{9,11},{11,13},{16,18},{18,... | collective-permute-start | bytes 2359304 | tf_op jit(solution)/shard_map/ppermute | solution.py:81
  369.3 10.8 %collective-permute-start.28 = (bf16[256,1536]{1,0:T(8,128)(2,1)S(1)}, bf16[256,1536]{1,0:T(8,128)(2,1)S(1)}, u32[]{:S(2)}, u32[]{:S(2)}) collective-permute-start(bf16[256,1536]{1,0:T(8,128)(2,1)S(1)} %get-tuple-element.35), channel_id=1, source_target_pairs={{0,2},{2,4},{1,3},{3,5},{8,10},{10,12},{9,11},{11,13},{16,18},{18,... | collective-permute-start | bytes 2359304 | tf_op jit(solution)/shard_map/ppermute | solution.py:81
  385.8 11.6 %collective-permute-start.41 = (bf16[256,1536]{1,0:T(8,128)(2,1)S(1)}, bf16[256,1536]{1,0:T(8,128)(2,1)S(1)}, u32[]{:S(2)}, u32[]{:S(2)}) collective-permute-start(bf16[256,1536]{1,0:T(8,128)(2,1)S(1)} %add_convert_fusion), channel_id=1, source_target_pairs={{0,2},{2,4},{4,6},{1,3},{3,5},{5,7},{8,10},{10,12},{12,14},{9,11},... | collective-permute-start | bytes 2359304 | tf_op jit(solution)/shard_map/ppermute | solution.py:81
  402.7 11.8 %collective-permute-start.29 = (bf16[256,1536]{1,0:T(8,128)(2,1)S(1)}, bf16[256,1536]{1,0:T(8,128)(2,1)S(1)}, u32[]{:S(2)}, u32[]{:S(2)}) collective-permute-start(bf16[256,1536]{1,0:T(8,128)(2,1)S(1)} %add_convert_fusion.4), channel_id=1, source_target_pairs={{0,2},{2,4},{4,6},{1,3},{3,5},{5,7},{8,10},{10,12},{12,14},{9,11},... | collective-permute-start | bytes 2359304 | tf_op jit(solution)/shard_map/ppermute | solution.py:81
  420.7 8.2 %collective-permute-done.29 = bf16[256,1536]{1,0:T(8,128)(2,1)S(1)} collective-permute-done((bf16[256,1536]{1,0:T(8,128)(2,1)S(1)}, bf16[256,1536]{1,0:T(8,128)(2,1)S(1)}, u32[]{:S(2)}, u32[]{:S(2)}) %collective-permute-start.29) | collective-permute-done | bytes 786464 | tf_op jit(solution)/shard_map/ppermute | solution.py:81
  447.1 7.3 %convolution_convert_fusion = bf16[1536,1728]{0,1:T(8,128)(2,1)} fusion(bf16[1024,1728]{0,1:T(8,128)(2,1)S(1)} %copy-done.72, bf16[1024,1536]{1,0:T(8,128)(2,1)S(1)} %bitcast.393), kind=kOutput, calls=%fused_computation.3 | convolution fusion | flops 5438472192 | bytes 11993088 | tf_op jit(solution)/shard_map/dot_general | solution.py:21
  454.4 7.9 %copy.91 = bf16[1536,1728]{1,0:T(8,128)(2,1)} copy(bf16[1536,1728]{0,1:T(8,128)(2,1)} %convolution_convert_fusion) | data formatting | bytes 10616832 | tf_op jit(solution)/shard_map/convert_element_type | solution.py:191
  502.0 7.2 %multiply_convert_fusion.3 = (bf16[1024,1536]{1,0:T(8,128)(2,1)}, bf16[1536]{0:T(1024)(128)(2,1)}, f32[1024,1536]{1,0:T(8,128)}) fusion(f32[1536]{0:T(1024)S(1)} %copy-done.59, f32[1024]{0:T(1024)S(1)} %bitcast.438, bf16[1,256,1536]{2,1,0:T(8,128)(2,1)S(1)} %copy-done.8, bf16[1,256,1536]{2,1,0:T(8,128)(2,1)S(1)} %copy-done.10, ...), kind=kOutput, calls=%fused_computation.13 | convolution fusion | flops 1231550976 | bytes 27145216 | tf_op jit(solution)/shard_map/dot_general | solution.py:13
  523.5 8.5 %convolution_convert_fusion.1 = bf16[1728,1536]{1,0:T(8,128)(2,1)S(1)} fusion(bf16[1024,1728]{0,1:T(8,128)(2,1)} %get-tuple-element.23, bf16[1024,1536]{1,0:T(8,128)(2,1)} %bitcast.389), kind=kOutput, calls=%fused_computation.4 | convolution fusion | flops 5438472192 | bytes 11993088 | tf_op jit(solution)/shard_map/dot_general | solution.py:21
  550.6 17.5 %collective-permute-done.47 = bf16[2,128,1536]{2,1,0:T(8,128)(2,1)S(1)} collective-permute-done((bf16[2,128,1536]{2,1,0:T(8,128)(2,1)S(1)}, bf16[2,128,1536]{2,1,0:T(8,128)(2,1)S(1)}, u32[]{:S(2)}, u32[]{:S(2)}) %collective-permute-start.47) | collective-permute-done | bytes 786464 | tf_op jit(solution)/shard_map/ppermute | solution.py:31
  571.4 9.6 %collective-permute-done.48 = bf16[1,128,1536]{2,1,0:T(8,128)(2,1)S(1)} collective-permute-done((bf16[1,128,1536]{2,1,0:T(8,128)(2,1)S(1)}, bf16[1,128,1536]{2,1,0:T(8,128)(2,1)S(1)}, u32[]{:S(2)}, u32[]{:S(2)}) %collective-permute-start.48) | collective-permute-done | bytes 393248 | tf_op jit(solution)/shard_map/ppermute | solution.py:31
  584.3 9.4 %collective-permute-done.50 = bf16[1,128,1536]{2,1,0:T(8,128)(2,1)S(1)} collective-permute-done((bf16[1,128,1536]{2,1,0:T(8,128)(2,1)S(1)}, bf16[1,128,1536]{2,1,0:T(8,128)(2,1)S(1)}, u32[]{:S(2)}, u32[]{:S(2)}) %collective-permute-start.50) | collective-permute-done | bytes 393248 | tf_op jit(solution)/shard_map/ppermute | solution.py:31
  645.8 42.3 %reduce-scatter.6.cloned.1.call-done = bf16[1,432,1536]{2,1,0:T(8,128)(2,1)} async-done(((bf16[8,432,1536]{2,1,0:T(8,128)(2,1)}), bf16[1,432,1536]{2,1,0:T(8,128)(2,1)}) %reduce-scatter.6.cloned.1.call-update) | async-done | bytes 1327120 | tf_op jit(solution)/shard_map/reduce_scatter | solution.py:200
  (456 shorter events, 315.6 us)
Async XLA Ops:
  7.2 93.5 %all-gather.8.cloned.1.call-start = ((), (), s32[]{:S(2)}) async-start(), calls=%async_computation.7 | async-start | bytes 5750784 | tf_op jit(solution)/shard_map/all_gather | solution.py:122
  8.3 26.5 %collective-permute-start.6 = (bf16[48,1536]{1,0:T(8,128)(2,1)S(1)}, bf16[48,1536]{1,0:T(8,128)(2,1)S(1)}, u32[]{:S(2)}, u32[]{:S(2)}) collective-permute-start(bf16[48,1536]{1,0:T(8,128)(2,1)S(1)} %get-tuple-element.81), channel_id=1, source_target_pairs={{0,2},{1,5},{2,8},{3,11},{4,14},{5,17},{6,20},{7,23},{8,26},{9,29}... | collective-permute-start | bytes 442376 | tf_op jit(solution)/shard_map/ppermute | solution.py:113
  13.2 21.5 %collective-permute-start.5 = (bf16[48,1536]{1,0:T(8,128)(2,1)S(1)}, bf16[48,1536]{1,0:T(8,128)(2,1)S(1)}, u32[]{:S(2)}, u32[]{:S(2)}) collective-permute-start(bf16[48,1536]{1,0:T(8,128)(2,1)S(1)} %get-tuple-element.82), channel_id=1, source_target_pairs={{0,1},{1,4},{2,7},{3,10},{4,13},{5,16},{6,19},{7,22},{8,25},{9,28}... | collective-permute-start | bytes 442376 | tf_op jit(solution)/shard_map/ppermute | solution.py:113
  13.9 20.9 %collective-permute-start.4 = (bf16[48,1536]{1,0:T(8,128)(2,1)S(1)}, bf16[48,1536]{1,0:T(8,128)(2,1)S(1)}, u32[]{:S(2)}, u32[]{:S(2)}) collective-permute-start(bf16[48,1536]{1,0:T(8,128)(2,1)S(1)} %get-tuple-element.80), channel_id=1, source_target_pairs={{0,0},{1,3},{2,6},{3,9},{4,12},{5,15},{6,18},{7,21},{8,24},{9,27},... | collective-permute-start | bytes 442376 | tf_op jit(solution)/shard_map/ppermute | solution.py:113
  35.8 189.7 %all-gather.6.cloned.1.call-start = ((), (), s32[]{:S(2)}) async-start(), calls=%async_computation.3 | async-start | bytes 6193152 | tf_op jit(solution)/shard_map/all_gather | solution.py:135
  41.1 22.1 %collective-permute-start.22 = (bf16[48,1728]{1,0:T(8,128)(2,1)}, bf16[48,1728]{1,0:T(8,128)(2,1)S(1)}, u32[]{:S(2)}, u32[]{:S(2)}) collective-permute-start(bf16[48,1728]{1,0:T(8,128)(2,1)} %get-tuple-element.72), channel_id=1, source_target_pairs={{0,4},{2,6},{4,0},{6,2},{1,5},{3,7},{5,1},{7,3},{8,12},{10,14},{12... | collective-permute-start | bytes 497672 | tf_op jit(solution)/shard_map/ppermute | solution.py:93
  42.6 20.6 %collective-permute-start.23 = (bf16[48,1728]{1,0:T(8,128)(2,1)S(1)}, bf16[48,1728]{1,0:T(8,128)(2,1)S(1)}, u32[]{:S(2)}, u32[]{:S(2)}) collective-permute-start(bf16[48,1728]{1,0:T(8,128)(2,1)S(1)} %get-tuple-element.71), channel_id=1, source_target_pairs={{0,6},{2,0},{4,2},{6,4},{1,7},{3,1},{5,3},{7,5},{8,14},{10,8},{12,... | collective-permute-start | bytes 497672 | tf_op jit(solution)/shard_map/ppermute | solution.py:93
  64.1 194.0 %all-gather.10.cloned.1.call-start = ((), (), s32[]{:S(2)}) async-start(), calls=%async_computation.8 | async-start | bytes 11943936 | tf_op jit(solution)/shard_map/all_gather | solution.py:138
  65.4 532.4 %reduce-scatter.8.cloned.1.call-start = ((), (), s32[]{:S(2)}) async-start(), calls=%async_computation.6 | async-start | bytes 6193152 | tf_op jit(solution)/shard_map/reduce_scatter | solution.py:193
  130.8 22.0 %collective-permute-start.11 = (bf16[2,128,1536]{2,1,0:T(8,128)(2,1)S(1)}, bf16[2,128,1536]{2,1,0:T(8,128)(2,1)S(1)}, u32[]{:S(2)}, u32[]{:S(2)}) collective-permute-start(bf16[2,128,1536]{2,1,0:T(8,128)(2,1)S(1)} %slice.406), channel_id=1, source_target_pairs={{0,16},{8,24},{16,0},{24,8},{1,17},{9,25},{17,1},{25,9},{2,18},{10... | collective-permute-start | bytes 2359304 | tf_op jit(solution)/shard_map/ppermute | solution.py:31
  130.9 31.1 %collective-permute-start.30 = (bf16[256,1536]{1,0:T(8,128)(2,1)S(1)}, bf16[256,1536]{1,0:T(8,128)(2,1)S(1)}, u32[]{:S(2)}, u32[]{:S(2)}) collective-permute-start(bf16[256,1536]{1,0:T(8,128)(2,1)S(1)} %bitcast.385), channel_id=1, source_target_pairs={{0,2},{2,4},{4,6},{1,3},{3,5},{5,7},{8,10},{10,12},{12,14},{9,11},... | collective-permute-start | bytes 2359304 | tf_op jit(solution)/shard_map/ppermute | solution.py:67
  145.6 20.6 %collective-permute-start.31 = (bf16[256,1536]{1,0:T(8,128)(2,1)S(1)}, bf16[256,1536]{1,0:T(8,128)(2,1)}, u32[]{:S(2)}, u32[]{:S(2)}) collective-permute-start(bf16[256,1536]{1,0:T(8,128)(2,1)S(1)} %bitcast.386), channel_id=1, source_target_pairs={{2,0},{4,2},{6,4},{3,1},{5,3},{7,5},{10,8},{12,10},{14,12},{11,9},... | collective-permute-start | bytes 2359304 | tf_op jit(solution)/shard_map/ppermute | solution.py:68
  147.0 21.6 %collective-permute-start.13 = (bf16[2,128,1536]{2,1,0:T(8,128)(2,1)S(1)}, bf16[2,128,1536]{2,1,0:T(8,128)(2,1)S(1)}, u32[]{:S(2)}, u32[]{:S(2)}) collective-permute-start(bf16[2,128,1536]{2,1,0:T(8,128)(2,1)S(1)} %pad_maximum_fusion.12), channel_id=1, source_target_pairs={{0,8},{8,0},{16,24},{24,16},{1,9},{9,1},{17,25},{25,17},{2,10},{10... | collective-permute-start | bytes 2359304 | tf_op jit(solution)/shard_map/ppermute | solution.py:31
  152.8 30.8 %collective-permute-start.12 = (bf16[1,128,1536]{2,1,0:T(8,128)(2,1)S(1)}, bf16[1,128,1536]{2,1,0:T(8,128)(2,1)S(1)}, u32[]{:S(2)}, u32[]{:S(2)}) collective-permute-start(bf16[1,128,1536]{2,1,0:T(8,128)(2,1)S(1)} %fusion.37), channel_id=1, source_target_pairs={{0,8},{8,0},{16,24},{24,16},{1,9},{9,1},{17,25},{25,17},{2,10},{10... | collective-permute-start | bytes 1179656 | tf_op jit(solution)/shard_map/ppermute | solution.py:31
  162.0 25.7 %collective-permute-start.34 = (bf16[256,1536]{1,0:T(8,128)(2,1)S(1)}, bf16[256,1536]{1,0:T(8,128)(2,1)}, u32[]{:S(2)}, u32[]{:S(2)}) collective-permute-start(bf16[256,1536]{1,0:T(8,128)(2,1)S(1)} %collective-permute-done.30), channel_id=1, source_target_pairs={{2,4},{4,6},{3,5},{5,7},{10,12},{12,14},{11,13},{13,15},{18,20},{2... | collective-permute-start | bytes 2359304 | tf_op jit(solution)/shard_map/ppermute | solution.py:67
  166.2 22.9 %collective-permute-start.32 = (bf16[256,1536]{1,0:T(8,128)(2,1)}, bf16[256,1536]{1,0:T(8,128)(2,1)}, u32[]{:S(2)}, u32[]{:S(2)}) collective-permute-start(bf16[256,1536]{1,0:T(8,128)(2,1)} %collective-permute-done.31), channel_id=1, source_target_pairs={{2,0},{4,2},{3,1},{5,3},{10,8},{12,10},{11,9},{13,11},{18,16},{20,... | collective-permute-start | bytes 2359304 | tf_op jit(solution)/shard_map/ppermute | solution.py:68
  189.1 23.2 %collective-permute-start.33 = (bf16[256,1536]{1,0:T(8,128)(2,1)}, bf16[256,1536]{1,0:T(8,128)(2,1)}, u32[]{:S(2)}, u32[]{:S(2)}) collective-permute-start(bf16[256,1536]{1,0:T(8,128)(2,1)} %collective-permute-done.32), channel_id=1, source_target_pairs={{2,0},{3,1},{10,8},{11,9},{18,16},{19,17},{26,24},{27,25}} | collective-permute-start | bytes 2359304 | tf_op jit(solution)/shard_map/ppermute | solution.py:68
  210.8 20.4 %collective-permute-start.19 = (bf16[256,1536]{1,0:T(8,128)(2,1)}, bf16[256,1536]{1,0:T(8,128)(2,1)}, u32[]{:S(2)}, u32[]{:S(2)}) collective-permute-start(bf16[256,1536]{1,0:T(8,128)(2,1)} %collective-permute-done.15), channel_id=1, source_target_pairs={{2,4},{4,6},{3,5},{5,7},{10,12},{12,14},{11,13},{13,15},{18,20},{2... | collective-permute-start | bytes 2359304 | tf_op jit(solution)/shard_map/ppermute | solution.py:67
  331.3 20.7 %collective-permute-start.39 = (bf16[256,1536]{1,0:T(8,128)(2,1)S(1)}, bf16[256,1536]{1,0:T(8,128)(2,1)S(1)}, u32[]{:S(2)}, u32[]{:S(2)}) collective-permute-start(bf16[256,1536]{1,0:T(8,128)(2,1)S(1)} %get-tuple-element.33), channel_id=1, source_target_pairs={{0,2},{1,3},{8,10},{9,11},{16,18},{17,19},{24,26},{25,27}} | collective-permute-start | bytes 2359304 | tf_op jit(solution)/shard_map/ppermute | solution.py:81
  334.9 33.9 %collective-permute-start.27 = (bf16[256,1536]{1,0:T(8,128)(2,1)S(1)}, bf16[256,1536]{1,0:T(8,128)(2,1)S(1)}, u32[]{:S(2)}, u32[]{:S(2)}) collective-permute-start(bf16[256,1536]{1,0:T(8,128)(2,1)S(1)} %get-tuple-element.37), channel_id=1, source_target_pairs={{0,2},{1,3},{8,10},{9,11},{16,18},{17,19},{24,26},{25,27}} | collective-permute-start | bytes 2359304 | tf_op jit(solution)/shard_map/ppermute | solution.py:81
  337.0 31.8 %collective-permute-start.25 = (bf16[256,1536]{1,0:T(8,128)(2,1)S(1)}, bf16[256,1536]{1,0:T(8,128)(2,1)S(1)}, u32[]{:S(2)}, u32[]{:S(2)}) collective-permute-start(bf16[256,1536]{1,0:T(8,128)(2,1)S(1)} %add_convert_fusion.7), channel_id=1, source_target_pairs={{4,2},{6,4},{5,3},{7,5},{12,10},{14,12},{13,11},{15,13},{20,18},{2... | collective-permute-start | bytes 2359304 | tf_op jit(solution)/shard_map/ppermute | solution.py:80
  352.4 33.2 %collective-permute-start.40 = (bf16[256,1536]{1,0:T(8,128)(2,1)S(1)}, bf16[256,1536]{1,0:T(8,128)(2,1)S(1)}, u32[]{:S(2)}, u32[]{:S(2)}) collective-permute-start(bf16[256,1536]{1,0:T(8,128)(2,1)S(1)} %get-tuple-element.31), channel_id=1, source_target_pairs={{0,2},{2,4},{1,3},{3,5},{8,10},{10,12},{9,11},{11,13},{16,18},{18,... | collective-permute-start | bytes 2359304 | tf_op jit(solution)/shard_map/ppermute | solution.py:81
  369.3 33.2 %collective-permute-start.28 = (bf16[256,1536]{1,0:T(8,128)(2,1)S(1)}, bf16[256,1536]{1,0:T(8,128)(2,1)S(1)}, u32[]{:S(2)}, u32[]{:S(2)}) collective-permute-start(bf16[256,1536]{1,0:T(8,128)(2,1)S(1)} %get-tuple-element.35), channel_id=1, source_target_pairs={{0,2},{2,4},{1,3},{3,5},{8,10},{10,12},{9,11},{11,13},{16,18},{18,... | collective-permute-start | bytes 2359304 | tf_op jit(solution)/shard_map/ppermute | solution.py:81
  380.1 34.4 %collective-permute-start.38 = (bf16[256,1536]{1,0:T(8,128)(2,1)S(1)}, bf16[256,1536]{1,0:T(8,128)(2,1)S(1)}, u32[]{:S(2)}, u32[]{:S(2)}) collective-permute-start(bf16[256,1536]{1,0:T(8,128)(2,1)S(1)} %get-tuple-element.30), channel_id=1, source_target_pairs={{2,0},{4,2},{6,4},{3,1},{5,3},{7,5},{10,8},{12,10},{14,12},{11,9},... | collective-permute-start | bytes 2359304 | tf_op jit(solution)/shard_map/ppermute | solution.py:80
  385.8 33.5 %collective-permute-start.41 = (bf16[256,1536]{1,0:T(8,128)(2,1)S(1)}, bf16[256,1536]{1,0:T(8,128)(2,1)S(1)}, u32[]{:S(2)}, u32[]{:S(2)}) collective-permute-start(bf16[256,1536]{1,0:T(8,128)(2,1)S(1)} %add_convert_fusion), channel_id=1, source_target_pairs={{0,2},{2,4},{4,6},{1,3},{3,5},{5,7},{8,10},{10,12},{12,14},{9,11},... | collective-permute-start | bytes 2359304 | tf_op jit(solution)/shard_map/ppermute | solution.py:81
  397.5 23.2 %collective-permute-start.26 = (bf16[256,1536]{1,0:T(8,128)(2,1)S(1)}, bf16[256,1536]{1,0:T(8,128)(2,1)S(1)}, u32[]{:S(2)}, u32[]{:S(2)}) collective-permute-start(bf16[256,1536]{1,0:T(8,128)(2,1)S(1)} %get-tuple-element.34), channel_id=1, source_target_pairs={{2,0},{4,2},{6,4},{3,1},{5,3},{7,5},{10,8},{12,10},{14,12},{11,9},... | collective-permute-start | bytes 2359304 | tf_op jit(solution)/shard_map/ppermute | solution.py:80
  402.7 26.2 %collective-permute-start.29 = (bf16[256,1536]{1,0:T(8,128)(2,1)S(1)}, bf16[256,1536]{1,0:T(8,128)(2,1)S(1)}, u32[]{:S(2)}, u32[]{:S(2)}) collective-permute-start(bf16[256,1536]{1,0:T(8,128)(2,1)S(1)} %add_convert_fusion.4), channel_id=1, source_target_pairs={{0,2},{2,4},{4,6},{1,3},{3,5},{5,7},{8,10},{10,12},{12,14},{9,11},... | collective-permute-start | bytes 2359304 | tf_op jit(solution)/shard_map/ppermute | solution.py:81
  441.9 26.6 %collective-permute-start.44 = (bf16[2,128,1536]{2,1,0:T(8,128)(2,1)}, bf16[2,128,1536]{2,1,0:T(8,128)(2,1)}, u32[]{:S(2)}, u32[]{:S(2)}) collective-permute-start(bf16[2,128,1536]{2,1,0:T(8,128)(2,1)} %pad_maximum_fusion.13), channel_id=1, source_target_pairs={{0,8},{8,0},{16,24},{24,16},{1,9},{9,1},{17,25},{25,17},{2,10},{10... | collective-permute-start | bytes 2359304 | tf_op jit(solution)/shard_map/ppermute | solution.py:31
  446.7 23.0 %collective-permute-start.45 = (bf16[2,128,1536]{2,1,0:T(8,128)(2,1)}, bf16[2,128,1536]{2,1,0:T(8,128)(2,1)}, u32[]{:S(2)}, u32[]{:S(2)}) collective-permute-start(bf16[2,128,1536]{2,1,0:T(8,128)(2,1)} %pad_maximum_fusion.14), channel_id=1, source_target_pairs={{0,16},{8,24},{16,0},{24,8},{1,17},{9,25},{17,1},{25,9},{2,18},{10... | collective-permute-start | bytes 2359304 | tf_op jit(solution)/shard_map/ppermute | solution.py:31
  467.8 153.8 %reduce-scatter.4.cloned.1.call-start = ((), (), s32[]{:S(2)}) async-start(), calls=%async_computation.4 | async-start | bytes 5750784 | tf_op jit(solution)/shard_map/reduce_scatter | solution.py:244
  523.3 164.8 %reduce-scatter.6.cloned.1.call-start = ((), (), s32[]{:S(2)}) async-start(), calls=%async_computation.5 | async-start | bytes 11943936 | tf_op jit(solution)/shard_map/reduce_scatter | solution.py:200
  549.7 21.7 %collective-permute-start.49 = (bf16[2,128,1536]{2,1,0:T(8,128)(2,1)S(1)}, bf16[2,128,1536]{2,1,0:T(8,128)(2,1)S(1)}, u32[]{:S(2)}, u32[]{:S(2)}) collective-permute-start(bf16[2,128,1536]{2,1,0:T(8,128)(2,1)S(1)} %pad_maximum_fusion.15), channel_id=1, source_target_pairs={{0,8},{8,0},{16,24},{24,16},{1,9},{9,1},{17,25},{25,17},{2,10},{10... | collective-permute-start | bytes 2359304 | tf_op jit(solution)/shard_map/ppermute | solution.py:31
  (111 other events, 930.6 us)
Sparse Core Ops, SparseCore 0:
  35.9 64.7 all-gather.7
  102.6 43.4 all-gather.5
  148.5 79.1 all-gather.9
  467.9 64.6 reduce-scatter.7
  534.8 58.6 reduce-scatter.3
  596.9 91.1 reduce-scatter.5

commit v2 on v1

v2 whole, which is shorter than its diff:
```python
import functools

import jax
import jax.numpy as jnp
from jax import lax
from jax.experimental import pallas as pl
from jax.experimental.pallas import tpu as pltpu
from jax.sharding import Mesh, PartitionSpec as P

epsilon = 1e-05
every = ("fsdp", "line", "core")
bf16 = jnp.bfloat16
f32 = jnp.float32
vmem_bytes = 58 * 2**20


def dot(left, right):
    return jnp.dot(left, right, preferred_element_type=f32)


def dot_nt(left, right):
    return lax.dot_general(left, right, (((1,), (1,)), ((), ())), preferred_element_type=f32)


def dot_tn(left, right):
    return lax.dot_general(left, right, (((0,), (0,)), ((), ())), preferred_element_type=f32)


def tie(block, *earlier):
    anywhere = pl.BlockSpec(memory_space=pl.ANY)
    return pl.pallas_call(
        lambda *refs: None,
        in_specs=[anywhere] * (1 + len(earlier)),
        out_specs=anywhere,
        out_shape=jax.ShapeDtypeStruct(block.shape, block.dtype),
        input_output_aliases={0: 0},
    )(block, *earlier)


def flip(block, axis, bits):
    size = lax.axis_size(axis)
    return lax.ppermute(block, axis, [(i, i ^ bits) for i in range(size)])


def gather(block, axis):
    return [block] + [flip(block, axis, r) for r in range(1, lax.axis_size(axis))]


def scatter(slots, axis):
    return [slots[0]] + [flip(slots[r], axis, r) for r in range(1, lax.axis_size(axis))]


def total(terms):
    return sum(t.astype(f32) for t in terms)


def exchange(blocks, axis):
    size = lax.axis_size(axis)
    me = lax.axis_index(axis)
    came = []
    for r in range(size):
        sent = lax.dynamic_index_in_dim(blocks, me ^ r, 0, keepdims=False)
        came.append(flip(sent, axis, r) if r else sent)
    out = []
    for d in range(size):
        block = came[0]
        for r in range(1, size):
            block = jnp.where(me ^ r == d, came[r], block)
        out.append(block)
    return out


def whole(shape):
    return pl.BlockSpec(shape, lambda *_: (0,) * len(shape))


def kernel_call(body, grid, ins, outs, scratch, flops, *args):
    shapes = [jax.ShapeDtypeStruct(shape, dtype) for shape, dtype, _ in outs]
    moved = sum(a.size * a.dtype.itemsize for a in args)
    moved += sum(s.size * s.dtype.itemsize for s in shapes)
    return pl.pallas_call(
        body,
        grid=grid,
        in_specs=ins,
        out_specs=[spec for _, _, spec in outs],
        out_shape=shapes,
        scratch_shapes=scratch,
        compiler_params=pltpu.CompilerParams(
            dimension_semantics=("arbitrary",) * len(grid), vmem_limit_bytes=vmem_bytes
        ),
        cost_estimate=pl.CostEstimate(flops=flops, bytes_accessed=moved, transcendentals=0),
    )(*args)


def shifted(block, distance, edge):
    rows = block.shape[0]
    moved = pltpu.roll(block, distance % rows, 0)
    row = lax.broadcasted_iota(jnp.int32, block.shape, 0)
    for n in range(abs(distance)):
        at = n if distance > 0 else rows - abs(distance) + n
        moved = jnp.where(row == at, edge[n : n + 1], moved)
    return moved


def mixer_forward(seqs, group, lanes, line, in_place, *refs):
    tok_refs, (gain_ref, taps_ref), refs = refs[:lanes], refs[lanes : lanes + 2], refs[lanes + 2 :]
    if in_place:
        places_ref, source_refs, refs = refs[0], refs[1 : 1 + 2 * line], refs[1 + 2 * line :]
        win_ref, wout_ref = refs[lanes + 8 : lanes + 10]
        bring_weights(2 * line, places_ref, source_refs, win_ref, wout_ref, refs[-1])
    else:
        (win_ref, wout_ref), refs = refs[:2], refs[2:]
    part_refs, refs = refs[:lanes], refs[lanes:]
    norm_ref, b_ref, c_ref, x_ref, conv_ref, gated_ref, halo_ref, y_ref = refs[:8]
    tok_ref = refs[10 if in_place else 8]
    pick(tok_refs, tok_ref)
    rows = seqs * group
    h = tok_ref[...].astype(f32)
    unit = h * lax.rsqrt(jnp.mean(h * h, axis=-1, keepdims=True) + epsilon)
    norm = (unit * gain_ref[...]).astype(bf16)
    norm_ref[0] = norm[:rows]
    b_all, x_all = dot_nt(norm, win_ref[0]), dot_nt(norm, win_ref[2])
    c_part = dot_nt(norm[:rows], win_ref[1])
    b_ref[0], c_ref[0], x_ref[0] = b_all[:rows], c_part, x_all[:rows]
    gated = (b_all * x_all).astype(bf16)
    gated_ref[0], halo_ref[0] = gated[:rows], gated[rows:]
    halo = gated[rows:].astype(f32)
    for q in range(seqs):
        at = slice(q * group, (q + 1) * group)
        now = gated[at].astype(f32)
        edge = halo[2 * q : 2 * q + 2]
        conv = (
            taps_ref[0:1] * shifted(now, 2, edge)
            + taps_ref[1:2] * shifted(now, 1, edge[1:])
            + taps_ref[2:3] * now
        )
        conv_ref[0, at] = conv
        y_ref[0, at] = (c_part[at] * conv).astype(bf16)
    hand(dot_nt(y_ref[0], wout_ref[...]).astype(bf16), part_refs)


def merged(ref):
    n, units, width = ref.shape
    return ref[...].reshape(n * units, width)


def hidden_gradient(line, *refs):
    cot_refs, down_ref, out_refs = refs[:line], refs[line], refs[line + 1 :]
    w_down = merged(down_ref)
    rows = cot_refs[0].shape[0]
    for r in range(line):
        at = slice(r // 2 * rows, (r // 2 + 1) * rows)
        out_refs[r % 2][0, at] = dot_nt(cot_refs[r][...], w_down)


def add_up(acc_ref, at, part, out_ref):
    j = pl.program_id(0)

    @pl.when(j == 0)
    def _():
        acc_ref[at] = part

    @pl.when(j == 1)
    def _():
        out_ref[...] = (acc_ref[at] + part).astype(bf16)


def feed_forward(n, *refs):
    u_refs, (gate_ref, up_ref, dh_ref), refs = refs[:n], refs[n : n + 3], refs[n + 3 :]
    (hid_ref, dg_ref, dup_ref), du_refs, acc_ref = refs[:3], refs[3 : 3 + n], refs[3 + n]
    w_gate, w_up = merged(gate_ref), merged(up_ref)
    rows = u_refs[0].shape[0]
    for r in range(n):
        at = slice(r * rows, (r + 1) * rows)
        gate = dot_nt(u_refs[r][...], w_gate)
        up = dot_nt(u_refs[r][...], w_up)
        dh = dh_ref[0, at]
        sig = jax.nn.sigmoid(gate)
        silu = gate * sig
        hid_ref[0, at] = (silu * up).astype(bf16)
        dgate = (dh * up * sig * (1.0 + gate * (1.0 - sig))).astype(bf16)
        dup = (dh * silu).astype(bf16)
        dg_ref[0, at] = dgate
        dup_ref[0, at] = dup
        add_up(acc_ref, at, dot(dgate, w_gate) + dot(dup, w_up), du_refs[r])


def feed_forward_out(line, *refs):
    hid_refs, down_ref, out_refs, acc_ref = refs[:2], refs[2], refs[3 : 3 + line], refs[3 + line]
    w_down = merged(down_ref)
    rows = out_refs[0].shape[0]
    for r in range(line):
        part = dot(hid_refs[r % 2][0, r // 2 * rows : (r // 2 + 1) * rows], w_down)
        add_up(acc_ref, slice(r * rows, (r + 1) * rows), part, out_refs[r])


def feed_forward_grads(line, *refs):
    u_refs, cot_refs, refs = refs[:line], refs[line : 2 * line], refs[2 * line :]
    halves, out_ref, (u_all, cot_all) = (refs[:3], refs[3:6]), refs[6], refs[7:]
    rows = u_refs[0].shape[0]

    @pl.when(pl.program_id(0) == 0)
    def _():
        for r in range(line):
            at = slice(r // 2 * rows, (r // 2 + 1) * rows)
            u_all[r % 2, at] = u_refs[r][...]
            cot_all[r % 2, at] = cot_refs[r][...]

    n, units, width = out_ref.shape
    units //= 3
    for k, right in enumerate((cot_all, u_all, u_all)):
        part = sum(dot_tn(halves[h][k][0], right[h]) for h in range(2))
        at = (k - 1) % 3 * units
        out_ref[:, at : at + units] = part.astype(bf16).reshape(n, units, width)


def pick(slot_refs, out_ref):
    for r, ref in enumerate(slot_refs):

        @pl.when(pl.program_id(0) == r)
        def _(ref=ref):
            out_ref[...] = ref[...]


def hand(block, out_refs):
    for r, ref in enumerate(out_refs):

        @pl.when(pl.program_id(0) == r)
        def _(ref=ref):
            ref[...] = block


def bring_weights(pieces, places_ref, sources, win_ref, wout_ref, sems):
    width, mine = wout_ref.shape
    feats = mine // pieces
    copies = []
    for k, source in enumerate(sources):
        s = places_ref[k]
        for p in range(3):
            rows = pl.ds(pl.multiple_of(s * feats, 16), feats)
            copies.append((source.at[pl.ds(p * feats, feats)], win_ref.at[p, rows]))
        for f in range(width // mine):
            rows = pl.ds(pl.multiple_of((f * pieces + s) * feats, 16), feats)
            columns = source.at[pl.ds(3 * feats, feats), pl.ds(f * mine, mine)]
            copies.append((columns, wout_ref.at[rows]))
    copies = [pltpu.make_async_copy(a, b, sems.at[n]) for n, (a, b) in enumerate(copies)]

    @pl.when(pl.program_id(0) == 0)
    def _():
        for copy in copies:
            copy.start()
        for copy in copies:
            copy.wait()


def mixer_backward_one(lanes, *refs):
    branch_refs, (wout_ref, c_ref, conv_ref, dconv_ref, dc_ref, now_ref) = refs[:lanes], refs[lanes:]
    pick(branch_refs, now_ref)
    dy = dot(now_ref[...], wout_ref[...])
    dconv_ref[0] = dy * c_ref[0]
    dc_ref[0] = (dy * conv_ref[0]).astype(bf16)


def mixer_backward_two(seqs, group, pieces, lanes, *refs):
    tok_refs, branch_refs, refs = refs[:lanes], refs[lanes : 2 * lanes], refs[2 * lanes :]
    (dconv_ref, ahead_ref, dc_ref, b_ref, x_ref, gated_ref, halo_ref, taps_ref, two_ref) = refs[:9]
    (win_ref, norm_ref, y_ref), refs = refs[9:12], refs[12:]
    part_refs, (out_ref, dm_ref, one_ref, dt_ref, tok_ref) = refs[:lanes], refs[lanes:]
    pick(tok_refs, tok_ref)
    r = pl.program_id(0)
    rows = seqs * group
    width = norm_ref.shape[2]
    mine = win_ref.shape[1]

    @pl.when(r == 0)
    def _():
        one_ref[...] = jnp.zeros_like(one_ref)
        dt_ref[...] = jnp.zeros_like(dt_ref)

    for q in range(seqs):
        at = slice(q * group, (q + 1) * group)
        now = dconv_ref[0, at]
        edge = ahead_ref[0, 2 * q : 2 * q + 2]
        dgated = (
            taps_ref[2:3] * now
            + taps_ref[1:2] * shifted(now, -1, edge)
            + taps_ref[0:1] * shifted(now, -2, edge)
        )
        dm_ref[0, r, at] = (dgated * x_ref[0, at]).astype(bf16)
        dm_ref[2, r, at] = (dgated * b_ref[0, at]).astype(bf16)
        held = gated_ref[0, at].astype(f32)
        past = halo_ref[0].astype(f32)[2 * q : 2 * q + 2]
        for k, block in enumerate((shifted(held, 2, past), shifted(held, 1, past[1:]), held)):
            dt_ref[k : k + 1] += jnp.sum(now * block, axis=0, keepdims=True)
    dm_ref[1, r] = dc_ref[0]
    da = sum(dot(dm_ref[p, r], win_ref[p]) for p in range(3))
    hand(da.astype(bf16), part_refs)
    h = tok_ref[:rows].astype(f32)
    unit = h * lax.rsqrt(jnp.mean(h * h, axis=-1, keepdims=True) + epsilon)
    one_ref[...] += jnp.sum(da * unit, axis=0, keepdims=True)

    @pl.when(r == pl.num_programs(0) - 1)
    def _():
        slots = norm_ref.shape[0]
        feats = mine // pieces
        norm = norm_ref[...].reshape(slots * rows, width)
        for p in range(3):
            g_in = dot_tn(dm_ref[p].reshape(slots * rows, mine), norm).astype(bf16)
            for s in range(pieces):
                out_ref[s, p * feats : (p + 1) * feats] = g_in[s * feats : (s + 1) * feats]
        g_out = sum(dot_tn(branch_refs[f][...], y_ref[f]) for f in range(lanes)).astype(bf16)
        small = jnp.concatenate([one_ref[...], two_ref[...], jnp.zeros((14, width), f32)], 0)
        small = small.astype(bf16)
        for s in range(pieces):
            for f in range(lanes):
                a = (f * pieces + s) * feats
                out_ref[s, 3 * feats : 4 * feats, f * mine : (f + 1) * mine] = g_out[a : a + feats]
            out_ref[s, 4 * feats :] = small
            out_ref[s, 4 * feats + 2 : 4 * feats + 5, :mine] = dt_ref[...].astype(bf16)


def on_device(tokens, gain_one, gain_two, conv_taps, w_in, w_out, w_gate, w_up, w_down, cotangent):
    seqs, group, width = tokens.shape
    rows = seqs * group
    lanes, line = lax.axis_size("fsdp"), lax.axis_size("line")
    pieces = 2 * line
    count = lanes * pieces
    feats = width // count
    mine = width // lanes
    hid = w_gate.shape[1]
    units = -(-hid // 16) * 16
    blocks = lanes * 2
    f_index = lax.axis_index("fsdp")
    s_index = lax.axis_index(("line", "core"))
    index = lax.axis_index(every)
    onward = [(i, i + 1) for i in range(pieces - 1)]
    back = [(i + 1, i) for i in range(pieces - 1)]

    in_blocks = w_in.T.reshape(3, feats, width)
    routes = [[(k, (3 * k + j) % count) for k in range(count)] for j in range(3)]
    came = jnp.stack([lax.ppermute(in_blocks[j], every, routes[j]) for j in range(3)])
    in_parts = [
        lax.dynamic_index_in_dim(came, (index + p * count) % 3, 0, keepdims=False) for p in range(3)
    ]
    smalls = jnp.concatenate([gain_one[None], gain_two[None], conv_taps], 0)
    smalls = jnp.pad(smalls, ((0, 11), (0, mine - feats)))
    out_blocks = w_out.T.reshape(feats, lanes, mine).transpose(1, 0, 2)
    out_blocks = jnp.concatenate([out_blocks, jnp.broadcast_to(smalls, (lanes, 16, mine))], 1)
    out_blocks = jnp.concatenate(exchange(out_blocks, "fsdp"), 1)
    edge = lax.ppermute(tokens[:, group - 2 :], ("line", "core"), onward).reshape(2 * seqs, width)
    edge = jnp.pad(edge, ((0, -2 * seqs % 16), (0, 0)))
    mixer_own = tie(jnp.concatenate(in_parts + [out_blocks], 0), edge)
    down_rows = tie(w_down.T.reshape(feats, count, hid).transpose(1, 0, 2), mixer_own)
    down_rows = lax.all_to_all(down_rows, every, 0, 0, tiled=True)
    mixer_slots = gather(mixer_own, "line")

    token_rows = tokens.reshape(rows, width)
    token_slots = gather(tie(jnp.concatenate([token_rows, edge], 0), mixer_own), "fsdp")

    swapped = list(flip(jnp.stack(mixer_slots[:1] + mixer_slots[1::2]), "core", 1))
    late = flip(tie(jnp.stack(mixer_slots[2::2]), *token_slots[1:], down_rows), "core", 1)
    swapped = [swapped[0]] + [s for pair in zip(swapped[1:], list(late) + [None]) for s in pair][:-1]
    cot_rows = cotangent.reshape(rows, width)
    cot_slots = gather(tie(cot_rows, *mixer_slots[1:]), "line")
    z_index, c_index = lax.axis_index("line"), lax.axis_index("core")
    near = jnp.arange(line, dtype=jnp.int32) ^ z_index
    places = jnp.concatenate([2 * near + c_index, 2 * near + 1 - c_index])
    small = jnp.stack([m[4 * feats : 4 * feats + 5] for m in mixer_slots + swapped])
    small = small.reshape(pieces, 5, lanes, mine)[..., :feats].reshape(pieces, 5 * lanes * feats)
    order = (places[None] == jnp.arange(pieces)[:, None]).astype(bf16)
    small = dot(order, small).reshape(pieces, 5, lanes, feats)
    small = small.transpose(1, 2, 0, 3).reshape(5, width)
    taps = lax.dynamic_slice_in_dim(small[2:], f_index * mine, mine, 1)
    anywhere = pl.BlockSpec(memory_space=pl.ANY)
    in_place = feats % 16 == 0 and mine % 128 == 0
    if in_place:
        weights = [places] + mixer_slots + swapped
        weight_specs = [pl.BlockSpec(memory_space=pltpu.SMEM)] + [anywhere] * pieces
        weight_outs = [((3, mine, width), bf16, whole((3, mine, width)))]
        weight_outs += [((width, mine), bf16, whole((width, mine)))]
        weight_scratch = [pltpu.SemaphoreType.DMA((pieces * (3 + lanes),))]
    else:
        mixer_w = jnp.stack(mixer_slots + swapped)[jnp.argsort(places)]
        full_in = mixer_w[:, : 3 * feats].reshape(pieces, 3, feats, width)
        full_in = full_in.transpose(1, 0, 2, 3).reshape(3, mine, width)
        full_out = mixer_w[:, 3 * feats : 4 * feats].reshape(pieces, feats, lanes, mine)
        full_out = full_out.transpose(2, 0, 1, 3).reshape(width, mine)
        weights = [full_in, full_out]
        weight_specs = [whole((3, mine, width)), whole((width, mine))]
        weight_outs = weight_scratch = []

    pad = ((0, units - hid), (0, 0))
    gate_up = jnp.concatenate([jnp.pad(w, pad) for w in (w_gate.T, w_up.T)], 0)
    gate_up = lax.all_gather(gate_up, ("fsdp", "core"), axis=0)

    more = token_slots[0].shape[0]
    everyone = lanes * rows
    slot = lambda *shape: pl.BlockSpec((1,) + shape, lambda r: (r,) + (0,) * len(shape))
    per_slot = lambda dtype, *shape: ((lanes,) + shape, dtype, slot(*shape))
    flat = lambda n, count: [((n, width), bf16, whole((n, width)))] * count
    made = kernel_call(
        functools.partial(mixer_forward, seqs, group, lanes, line, in_place),
        (lanes,),
        [whole((more, width))] * lanes + [whole((1, width)), whole((3, mine))] + weight_specs,
        flat(rows, lanes)
        + [per_slot(bf16, rows, width)]
        + [per_slot(f32, rows, mine)] * 4
        + [per_slot(bf16, rows, mine), per_slot(bf16, more - rows, mine), per_slot(bf16, rows, mine)]
        + weight_outs,
        [pltpu.VMEM((more, width), bf16)] + weight_scratch,
        8 * everyone * width * mine,
        *token_slots[:1],
        tie(token_slots[1], *cot_slots[1::2]),
        *token_slots[2:],
        small[:1],
        taps,
        *weights,
    )
    branch_o, held = made[:lanes], made[lanes + 8 :]
    normed_a, b_part, c_part, x_part, conv, gated, halo, branch_y = made[lanes : lanes + 8]
    full_in, full_out = held if in_place else weights
    branch_terms = scatter(branch_o, "fsdp")
    branch_o = total(branch_terms)
    hidden_in = token_rows.astype(f32)
    second = hidden_in + branch_o
    scale_two = lax.rsqrt(jnp.mean(second * second, axis=-1, keepdims=True) + epsilon)
    unit_two = second * scale_two
    normed_u = (unit_two * small[1]).astype(bf16)

    down_rows = down_rows.reshape(width, hid).T
    full_down = tie(jnp.pad(down_rows, pad), gate_up, normed_a)
    full_down = lax.all_gather(full_down, ("fsdp", "core"), axis=0)

    u_slots = gather(normed_u, "line")
    some, half_rows = blocks // 2, line // 2 * rows
    third = lambda k: pl.BlockSpec((some, units, width), lambda j: (j, k, 0))
    half = (2, half_rows, some * units)
    per_half = pl.BlockSpec((1,) + half[1:], lambda j: (j, 0, 0))
    slot_specs = [whole((rows, width))] * line
    unit_flops = 2 * line * rows * blocks * units * width
    dhidden = kernel_call(
        functools.partial(hidden_gradient, line),
        (2,),
        slot_specs + [third(0)],
        [(half, f32, per_half)] * 2,
        [],
        unit_flops,
        *cot_slots,
        full_down,
    )
    done, du_terms = [None, None], [None] * line
    u_slots[1] = tie(u_slots[1], *dhidden)
    for odd in (1, 0):
        made = kernel_call(
            functools.partial(feed_forward, line // 2),
            (2,),
            slot_specs[: line // 2] + [third(0), third(1), per_half],
            [(half, bf16, per_half)] * 3 + flat(rows, line // 2),
            [pltpu.VMEM((half_rows, width), f32)],
            2 * unit_flops,
            *u_slots[odd::2],
            gate_up,
            gate_up,
            dhidden[odd],
        )
        done[odd] = made[:3]
        du_terms[odd::2] = made[3:]
    du_terms = scatter(du_terms, "line")
    (g_ff,) = kernel_call(
        functools.partial(feed_forward_grads, line),
        (2,),
        slot_specs * 2 + [per_half] * 6,
        [((blocks, 3 * units, width), bf16, pl.BlockSpec((some, 3 * units, width), lambda j: (j, 0, 0)))],
        [pltpu.VMEM((2, half_rows, width), bf16)] * 2,
        3 * unit_flops,
        *u_slots,
        *cot_slots,
        *done[0],
        *done[1],
    )
    g_ff = lax.psum_scatter(tie(g_ff, *du_terms[1::2]), ("fsdp", "core"), scatter_dimension=0)
    part_out = kernel_call(
        functools.partial(feed_forward_out, line),
        (2,),
        [per_half, per_half, third(0)],
        flat(rows, line),
        [pltpu.VMEM((line * rows, width), f32)],
        unit_flops,
        done[0][0],
        done[1][0],
        full_down,
    )
    dunit = total([tie(du_terms[0], part_out[0])] + du_terms[1:])
    out_terms = scatter([part_out[0]] + [tie(p, *du_terms[1:]) for p in part_out[1:]], "line")

    grad_two = jnp.sum(dunit * unit_two, axis=0)
    dnorm_two = dunit * small[1]
    dsecond = cot_rows.astype(f32) + scale_two * (
        dnorm_two - unit_two * jnp.mean(dnorm_two * unit_two, axis=-1, keepdims=True)
    )
    dbranch = dsecond.astype(bf16)
    branch_slots = gather(dbranch, "fsdp")
    everyone = lanes * rows
    dconv, dc_part = kernel_call(
        functools.partial(mixer_backward_one, lanes),
        (lanes,),
        [whole((rows, width))] * lanes + [whole((width, mine)), slot(rows, mine), slot(rows, mine)],
        [per_slot(f32, rows, mine), per_slot(bf16, rows, mine)],
        [pltpu.VMEM((rows, width), bf16)],
        2 * everyone * width * mine,
        *branch_slots,
        full_out,
        c_part,
        conv,
    )
    block_out = second + total([tie(out_terms[0], dconv)] + out_terms[1:])
    block_out = block_out.astype(bf16).reshape(seqs, group, width)
    ahead = dconv.reshape(lanes, seqs, group, mine)[:, :, :2]
    ahead = lax.ppermute(ahead, ("line", "core"), back).reshape(lanes, 2 * seqs, mine)
    *dnormed, g_mixer = kernel_call(
        functools.partial(mixer_backward_two, seqs, group, pieces, lanes),
        (lanes,),
        [whole((more, width))] * lanes
        + [whole((rows, width))] * lanes
        + [
            slot(rows, mine),
            slot(2 * seqs, mine),
            slot(rows, mine),
            slot(rows, mine),
            slot(rows, mine),
            slot(rows, mine),
            slot(more - rows, mine),
            whole((3, mine)),
            whole((1, width)),
            whole((3, mine, width)),
            whole((lanes, rows, width)),
            whole((lanes, rows, mine)),
        ],
        flat(rows, lanes)
        + [((pieces, 4 * feats + 16, width), bf16, whole((pieces, 4 * feats + 16, width)))],
        [
            pltpu.VMEM((3, lanes, rows, mine), bf16),
            pltpu.VMEM((1, width), f32),
            pltpu.VMEM((3, mine), f32),
            pltpu.VMEM((more, width), bf16),
        ],
        14 * everyone * width * mine,
        *token_slots,
        *branch_slots,
        tie(dconv, *out_terms[1:]),
        ahead,
        dc_part,
        b_part,
        x_part,
        gated,
        halo,
        taps,
        grad_two[None],
        full_in,
        normed_a,
        branch_y,
    )
    dnormed = total(scatter(dnormed, "fsdp"))
    scale_one = lax.rsqrt(jnp.mean(hidden_in * hidden_in, axis=-1, keepdims=True) + epsilon)
    unit_one = hidden_in * scale_one
    dnorm_one = dnormed * small[0]
    dinput = dsecond + scale_one * (
        dnorm_one - unit_one * jnp.mean(dnorm_one * unit_one, axis=-1, keepdims=True)
    )
    grad_tokens = dinput.astype(bf16).reshape(seqs, group, width)

    g_mixer = lax.psum_scatter(g_mixer, ("line", "core"), scatter_dimension=0)
    g_down = g_ff[2 * units : 2 * units + hid].T.reshape(count, feats, hid)
    g_down = lax.all_to_all(g_down, every, 0, 0, tiled=True)
    g_mixer = tie(g_mixer, g_down)
    g_in = g_mixer[: 3 * feats].reshape(3, feats, width)
    homes = [[(d, k) for k, d in route] for route in routes]
    parts = []
    for j in range(3):
        p = ((j - index) * pow(count, -1, 3)) % 3
        block = lax.dynamic_index_in_dim(g_in, p, 0, keepdims=False)
        parts.append(lax.ppermute(block, every, homes[j]))
    grad_in = jnp.concatenate(parts, 0).T.astype(f32)
    g_out = g_mixer[3 * feats : 4 * feats].reshape(feats, lanes, mine).transpose(1, 0, 2)
    gains = g_mixer[4 * feats : 4 * feats + 2].reshape(2, lanes, pieces, feats)
    gains = lax.dynamic_index_in_dim(gains, s_index, 2, keepdims=False).transpose(1, 0, 2)
    gains = jnp.pad(gains, ((0, 0), (0, 14), (0, mine - feats)))
    got = jnp.stack(exchange(jnp.concatenate([g_out, gains], 1), "fsdp"))
    grad_out = got[:, :feats].transpose(0, 2, 1).reshape(width, feats).astype(f32)
    gains = jnp.sum(got[:, feats : feats + 2, :feats].astype(f32), axis=0)
    grad_taps = g_mixer[4 * feats + 2 : 4 * feats + 5, :mine].reshape(3, pieces, feats)
    grad_taps = lax.dynamic_index_in_dim(grad_taps, s_index, 1, keepdims=False).astype(f32)
    grad_gate = g_ff[:hid].T.astype(f32)
    grad_up = g_ff[units : units + hid].T.astype(f32)
    grad_down = g_down.transpose(0, 2, 1).reshape(count * hid, feats).astype(f32)
    return (
        block_out,
        grad_tokens,
        gains[0],
        gains[1],
        grad_taps,
        grad_in,
        grad_out,
        grad_gate,
        grad_up,
        grad_down,
    )


def solution(mesh):
    lanes, pieces = mesh.devices.shape
    fine = Mesh(mesh.devices.reshape(lanes, pieces // 2, 2), every)
    token = P("fsdp", ("line", "core"), None)
    vector = P(every)
    columns = P(None, every)
    return jax.shard_map(
        on_device,
        mesh=fine,
        in_specs=(token, vector, vector) + (columns,) * 6 + (token,),
        out_specs=(token, token, vector, vector) + (columns,) * 6,
        check_vma=False,
    )
```

time: 709 us -> 631 us (0.89)
  Pallas kernels: 0 us -> 140 us
  matrix products: 118 us -> 0.13 us
  starting transfers between devices: 159 us -> 96.7 us
  local copies, waits for them, and re-layouts: 97.5 us -> 41.5 us
  waiting for transfers between devices: 247 us -> 299 us
  other arithmetic: 61 us -> 30.8 us
    pallas_call x0 -> x24, Pallas kernels: none -> 140 us  [the longest x8 140 us: kernel_call(): pl.pallas_call(body, grid=grid, in_specs=ins, out_specs=[spec for _, _, s...]
    dot_general x21 -> x1, matrix products: 118 us -> 0.13 us  [dot(): return jnp.dot(left, right, preferred_element_type=f32)]
    ppermute x54 -> x37, starting transfers between devices: 145 us -> 66.5 us  [the longest x35 62.8 us: flip(): return lax.ppermute(block, axis, [(i, i ^ bits) for i in range(size)])]
    ppermute x54 -> x37, waiting for transfers between devices: 203 us -> 249 us  [the longest x35 249 us: flip(): return lax.ppermute(block, axis, [(i, i ^ bits) for i in range(size)])]
    slice x17 -> x12, local copies, waits for them, and re-layouts: 21.1 us -> 6.27 us  [the longest x6 3.15 us: on_device(): m[4 * feats:4 * feats + 5]]
    another operation x24 -> x2, other arithmetic: 16.9 us -> 2.61 us  [the longest x1 2.57 us: on_device(): jnp.stack(mixer_slots[:1] + mixer_slots[1::2])]
    dynamic_update_slice x16 -> x0, local copies, waits for them, and re-layouts: 13.5 us -> none  [the longest x12 9.42 us: exchange(): got = lax.dynamic_update_index_in_dim(got, came, (me - k) % size, 0)]
    transpose x5 -> x1, local copies, waits for them, and re-layouts: 12 us -> 1.15 us  [on_device(): g_down = g_ff[2 * units:2 * units + hid].T.reshape(count, feats, hid)]
  transfers between devices with their start and end apart: 66 -> 49, of which waited for: 30 -> 23; matrix products, arithmetic and copies ran while one was open for 27% -> 9% of each run, Pallas kernels for 0% -> 22%
where the time goes in v2:
time: 631 us; the launch traced here: 623 us
  waiting for transfers between devices  299 us (47%)
  Pallas kernels  140 us (22%)
  starting transfers between devices  96.7 us (15%)
  local copies, waits for them, and re-layouts  41.5 us (7%)
  other arithmetic  30.8 us (5%)
  between operations  15.2 us (2%)
    ppermute x35, waiting for transfers between devices, flip(): return lax.ppermute(block, axis, [(i, i ^ bits) for i in range(size)])  249 us
    pallas_call x8, Pallas kernels, kernel_call(): pl.pallas_call(body, grid=grid, in_specs=ins, out_specs=[spec for _, _, s...  140 us
    ppermute x35, starting transfers between devices, flip(): return lax.ppermute(block, axis, [(i, i ^ bits) for i in range(size)])  62.8 us
    reduce_scatter x1, waiting for transfers between devices, on_device(): g_mixer = lax.psum_scatter(g_mixer, ('line', 'core'), scatter_dimension=0)  33.5 us
    unnamed x78, local copies, waits for them, and re-layouts  13.8 us
  transfers between devices with their start and end apart: 49, of which 23 were waited for; matrix products, arithmetic and copies ran while one was open for 9% of the time, Pallas kernels for 22%

profile of v2, /device:TPU:0, one launch (start us, length us, event | category | flops | bytes accessed | tf_op | source)
XLA Modules:
  0.0 623.4 jit_solution(13199165909245372394)
XLA Ops:
  17.3 7.9 %collective-permute-start.3 = (bf16[48,1536]{1,0:T(8,128)(2,1)S(1)}, bf16[48,1536]{1,0:T(8,128)(2,1)S(1)}, u32[]{:S(2)}, u32[]{:S(2)}) collective-permute-start(bf16[48,1536]{1,0:T(8,128)(2,1)S(1)} %get-tuple-element.106), channel_id=1, source_target_pairs={{0,2},{1,5},{2,8},{3,11},{4,14},{5,17},{6,20},{7,23},{8,26},{9,29}... | collective-permute-start | bytes 442376 | tf_op jit(solution)/shard_map/ppermute | solution.py:341
  26.1 5.8 collective-permute-done.3
  35.0 4.7 collective-permute-start.10
  46.2 9.0 %collective-permute-done.10.refs_3_.refs_10_ = bf16[208,1536]{1,0:T(8,128)(2,1)S(1)} collective-permute-done((bf16[208,1536]{1,0:T(8,128)(2,1)}, bf16[208,1536]{1,0:T(8,128)(2,1)S(1)}, u32[]{:S(2)}, u32[]{:S(2)}) %collective-permute-start.10) | collective-permute-done | bytes 639008 | tf_op jit(solution)/shard_map/ppermute | solution.py:42
  55.2 13.3 %collective-permute-done.8.refs_1_.refs_8_ = bf16[208,1536]{1,0:T(8,128)(2,1)} collective-permute-done((bf16[208,1536]{1,0:T(8,128)(2,1)}, bf16[208,1536]{1,0:T(8,128)(2,1)}, u32[]{:S(2)}, u32[]{:S(2)}) %collective-permute-start.8) | collective-permute-done | bytes 639008 | tf_op jit(solution)/shard_map/ppermute | solution.py:42
  79.8 30.0 %collective-permute-done.9.refs_2_.refs_9_ = bf16[208,1536]{1,0:T(8,128)(2,1)} collective-permute-done((bf16[208,1536]{1,0:T(8,128)(2,1)S(1)}, bf16[208,1536]{1,0:T(8,128)(2,1)}, u32[]{:S(2)}, u32[]{:S(2)}) %collective-permute-start.9) | collective-permute-done | bytes 639008 | tf_op jit(solution)/shard_map/ppermute | solution.py:42
  114.0 8.7 %collective-permute-done.13.refs_2_ = bf16[272,1536]{1,0:T(8,128)(2,1)} collective-permute-done((bf16[272,1536]{1,0:T(8,128)(2,1)}, bf16[272,1536]{1,0:T(8,128)(2,1)}, u32[]{:S(2)}, u32[]{:S(2)}) %collective-permute-start.13) | collective-permute-done | bytes 835616 | tf_op jit(solution)/shard_map/ppermute | solution.py:42
  132.4 14.6 %collective-permute-done.11.refs_1_.refs_5_ = bf16[256,1536]{1,0:T(8,128)(2,1)} collective-permute-done((bf16[256,1536]{1,0:T(8,128)(2,1)}, bf16[256,1536]{1,0:T(8,128)(2,1)}, u32[]{:S(2)}, u32[]{:S(2)}) %collective-permute-start.11) | collective-permute-done | bytes 786464 | tf_op jit(solution)/shard_map/ppermute | solution.py:42
  152.7 18.4 %shard_map.183 = (bf16[256,1536]{1,0:T(8,128)(2,1)}, bf16[256,1536]{1,0:T(8,128)(2,1)}, bf16[256,1536]{1,0:T(8,128)(2,1)}, bf16[256,1536]{1,0:T(8,128)(2,1)}, bf...) custom-call(bf16[272,1536]{1,0:T(8,128)(2,1)} %shard_map.178.refs_0_, ...), custom_call_target="tpu_custom_call" | custom-call | flops 4831838208 | bytes 27388448 | tf_op jit(solution)/shard_map/pallas_call | solution.py:81
  176.4 23.4 %collective-permute-done.17 = bf16[256,1536]{1,0:T(8,128)(2,1)S(1)} collective-permute-done((bf16[256,1536]{1,0:T(8,128)(2,1)}, bf16[256,1536]{1,0:T(8,128)(2,1)S(1)}, u32[]{:S(2)}, u32[]{:S(2)}) %collective-permute-start.17) | collective-permute-done | bytes 786464 | tf_op jit(solution)/shard_map/ppermute | solution.py:42
  199.8 11.2 %collective-permute-done.18 = bf16[256,1536]{1,0:T(8,128)(2,1)S(1)} collective-permute-done((bf16[256,1536]{1,0:T(8,128)(2,1)}, bf16[256,1536]{1,0:T(8,128)(2,1)S(1)}, u32[]{:S(2)}, u32[]{:S(2)}) %collective-permute-start.18) | collective-permute-done | bytes 786464 | tf_op jit(solution)/shard_map/ppermute | solution.py:42
  211.0 17.3 %collective-permute-done.19 = bf16[256,1536]{1,0:T(8,128)(2,1)} collective-permute-done((bf16[256,1536]{1,0:T(8,128)(2,1)}, bf16[256,1536]{1,0:T(8,128)(2,1)}, u32[]{:S(2)}, u32[]{:S(2)}) %collective-permute-start.19) | collective-permute-done | bytes 786464 | tf_op jit(solution)/shard_map/ppermute | solution.py:42
  235.4 10.9 %shard_map.185 = (f32[2,512,896]{2,1,0:T(8,128)}, f32[2,512,896]{2,1,0:T(8,128)}) custom-call(bf16[256,1536]{1,0:T(8,128)(2,1)} %shard_map.179.refs_0_.refs_4_, bf16[256,1536]{1,0:T(8,128)(2,1)} %collective-permute-done.11.refs_1_.refs_5_, bf16[256,1536]{1,0:T(8,128)(2,1)} %collective-permute-done.21.refs_2_.refs_6_, ...), custom_call_target="tpu_custom_call" | custom-call | flops 5637144576 | bytes 15990784 | tf_op jit(solution)/shard_map/pallas_call | solution.py:81
  246.3 19.0 %collective-permute-done.22.refs_0_ = bf16[256,1536]{1,0:T(8,128)(2,1)S(1)} collective-permute-done((bf16[256,1536]{1,0:T(8,128)(2,1)}, bf16[256,1536]{1,0:T(8,128)(2,1)S(1)}, u32[]{:S(2)}, u32[]{:S(2)}) %collective-permute-start.22) | collective-permute-done | bytes 786464 | tf_op jit(solution)/shard_map/ppermute | solution.py:42
  268.0 20.6 %shard_map.188 = (bf16[2,512,896]{2,1,0:T(8,128)(2,1)}, bf16[2,512,896]{2,1,0:T(8,128)(2,1)}, bf16[2,512,896]{2,1,0:T(8,128)(2,1)}, bf16[256,1536]{1,0:T(8,128)(2,1)}, bf16[256,1536]{1,0:T(8,128)(2,1)}) custom-call(bf16[256,1536]{1,0:T(8,128)(2,1)} %shard_map.187.refs_0_.refs_1_, bf16[256,1536]{1,0:T(8,128)(2,1)} %collective-permute-done.23.refs_1_.refs_3_, ...), custom_call_target="tpu_custom_call" | custom-call | flops 11274289152 | bytes 34340864 | tf_op jit(solution)/shard_map/pallas_call | solution.py:81
  288.6 20.5 %collective-permute-start.24 = (bf16[256,1536]{1,0:T(8,128)(2,1)}, bf16[256,1536]{1,0:T(8,128)(2,1)S(1)}, u32[]{:S(2)}, u32[]{:S(2)}) collective-permute-start(bf16[256,1536]{1,0:T(8,128)(2,1)} %get-tuple-element.58), channel_id=1, source_target_pairs={{0,2},{2,0},{4,6},{6,4},{1,3},{3,1},{5,7},{7,5},{8,10},{10,8},{12,... | collective-permute-start | bytes 2359304 | tf_op jit(solution)/shard_map/ppermute | solution.py:42
  310.1 20.8 %shard_map.186 = (bf16[2,512,896]{2,1,0:T(8,128)(2,1)}, bf16[2,512,896]{2,1,0:T(8,128)(2,1)}, bf16[2,512,896]{2,1,0:T(8,128)(2,1)}, bf16[256,1536]{1,0:T(8,128)(2,1)}, bf16[256,1536]{1,0:T(8,128)(2,1)}) custom-call(bf16[256,1536]{1,0:T(8,128)(2,1)} %multiply_convert_fusion.refs_0_, bf16[256,1536]{1,0:T(8,128)(2,1)} %collective-permute-done.20.refs_1_.refs_2_, ...), custom_call_target="tpu_custom_call" | custom-call | flops 11274289152 | bytes 34340864 | tf_op jit(solution)/shard_map/pallas_call | solution.py:81
  330.9 26.5 %shard_map.198.refs_0_ = bf16[8,672,1536]{2,1,0:T(8,128)(2,1)} custom-call(bf16[256,1536]{1,0:T(8,128)(2,1)} %multiply_convert_fusion.refs_0_, bf16[256,1536]{1,0:T(8,128)(2,1)} %shard_map.187.refs_0_.refs_1_, bf16[256,1536]{1,0:T(8,128)(2,1)} %collective-permute-done.20.refs_1_.refs_2_, bf16[256,1536]{1,0:T(8,128)(2,1)} %collective-permute-done.23.refs_1_.refs_3_, ...), custom_call_target="tpu_custom_call" | custom-call | flops 16911433728 | bytes 33816576 | tf_op jit(solution)/shard_map/pallas_call | solution.py:81
  360.1 12.9 %shard_map.189 = (bf16[256,1536]{1,0:T(8,128)(2,1)}, bf16[256,1536]{1,0:T(8,128)(2,1)}, bf16[256,1536]{1,0:T(8,128)(2,1)}, bf16[256,1536]{1,0:T(8,128)(2,1)}) custom-call(bf16[2,512,896]{2,1,0:T(8,128)(2,1)} %get-tuple-element.53.refs_0_.refs_8_, bf16[2,512,896]{2,1,0:T(8,128)(2,1)} %get-tuple-element.55.refs_1_.refs_11_, bf16[8,224,1536]{2,1,0:T(8,128)(2,1)} %bitcast.227), custom_call_target="tpu_custom_call" | custom-call | flops 5637144576 | bytes 12320768 | tf_op jit(solution)/shard_map/pallas_call | solution.py:81
  373.0 16.5 %collective-permute-done.25.refs_2_ = bf16[256,1536]{1,0:T(8,128)(2,1)} collective-permute-done((bf16[256,1536]{1,0:T(8,128)(2,1)}, bf16[256,1536]{1,0:T(8,128)(2,1)}, u32[]{:S(2)}, u32[]{:S(2)}) %collective-permute-start.25) | collective-permute-done | bytes 786464 | tf_op jit(solution)/shard_map/ppermute | solution.py:42
  402.0 31.4 %collective-permute-done.29.refs_3_.refs_7_ = bf16[256,1536]{1,0:T(8,128)(2,1)} collective-permute-done((bf16[256,1536]{1,0:T(8,128)(2,1)}, bf16[256,1536]{1,0:T(8,128)(2,1)}, u32[]{:S(2)}, u32[]{:S(2)}) %collective-permute-start.29) | collective-permute-done | bytes 786464 | tf_op jit(solution)/shard_map/ppermute | solution.py:42
  435.3 14.1 %collective-permute-done.28.refs_2_.refs_6_ = bf16[256,1536]{1,0:T(8,128)(2,1)} collective-permute-done((bf16[256,1536]{1,0:T(8,128)(2,1)}, bf16[256,1536]{1,0:T(8,128)(2,1)}, u32[]{:S(2)}, u32[]{:S(2)}) %collective-permute-start.28) | collective-permute-done | bytes 786464 | tf_op jit(solution)/shard_map/ppermute | solution.py:42
  449.3 14.8 %collective-permute-done.27.refs_1_.refs_5_ = bf16[256,1536]{1,0:T(8,128)(2,1)} collective-permute-done((bf16[256,1536]{1,0:T(8,128)(2,1)}, bf16[256,1536]{1,0:T(8,128)(2,1)}, u32[]{:S(2)}, u32[]{:S(2)}) %collective-permute-start.27) | collective-permute-done | bytes 786464 | tf_op jit(solution)/shard_map/ppermute | solution.py:42
  464.2 6.6 %shard_map.191 = (f32[4,256,384]{2,1,0:T(8,128)}, bf16[4,256,384]{2,1,0:T(8,128)(2,1)}) custom-call(bf16[256,1536]{1,0:T(8,128)(2,1)} %get-tuple-element.86.refs_0_.refs_4_, bf16[256,1536]{1,0:T(8,128)(2,1)} %collective-permute-done.27.refs_1_.refs_5_, bf16[256,1536]{1,0:T(8,128)(2,1)} %collective-permute-done.28.refs_2_.refs_6_, ...), custom_call_target="tpu_custom_call" | custom-call | flops 1207959552 | bytes 9830400 | tf_op jit(solution)/shard_map/pallas_call | solution.py:81
  475.4 23.2 %shard_map.197 = (bf16[256,1536]{1,0:T(8,128)(2,1)}, bf16[256,1536]{1,0:T(8,128)(2,1)}, bf16[256,1536]{1,0:T(8,128)(2,1)}, bf16[256,1536]{1,0:T(8,128)(2,1)}, bf16[8,208,1536]{2,1,0:T(8,128)(2,1)}) custom-call(bf16[272,1536]{1,0:T(8,128)(2,1)} %shard_map.178.refs_0_, bf16[272,1536]{1,0:T(8,128)(2,1)} %copy-done.14, ...), custom_call_target="tpu_custom_call" | custom-call | flops 8455716864 | bytes 28592640 | tf_op jit(solution)/shard_map/pallas_call | solution.py:81
  500.1 3.7 collective-permute-start.35
  503.8 6.8 %reduce-scatter.5.cloned.1.call-done = bf16[1,672,1536]{2,1,0:T(8,128)(2,1)} async-done(((bf16[8,672,1536]{2,1,0:T(8,128)(2,1)}), bf16[1,672,1536]{2,1,0:T(8,128)(2,1)}) %reduce-scatter.5.cloned.1.call-update) | async-done | bytes 2064400 | tf_op jit(solution)/shard_map/reduce_scatter | solution.py:481
  515.0 7.1 %all-to-all-start.1 = ((bf16[32,48,216]{2,1,0:T(8,128)(2,1)}), bf16[32,48,216]{2,1,0:T(8,128)(2,1)S(1)}, u32[]{:S(2)}, u32[]{:S(2)}) async-start(bf16[32,48,216]{2,1,0:T(8,128)(2,1)} %bitcast.200), calls=%async_computation.3 | async-start | bytes 1572864 | tf_op jit(solution)/shard_map/all_to_all | solution.py:574
  525.4 22.1 %collective-permute-done.36 = bf16[256,1536]{1,0:T(8,128)(2,1)} collective-permute-done((bf16[256,1536]{1,0:T(8,128)(2,1)}, bf16[256,1536]{1,0:T(8,128)(2,1)}, u32[]{:S(2)}, u32[]{:S(2)}) %collective-permute-start.36) | collective-permute-done | bytes 786464 | tf_op jit(solution)/shard_map/ppermute | solution.py:42
  553.3 33.5 %reduce-scatter.3.cloned.1.call-done = bf16[1,208,1536]{2,1,0:T(8,128)(2,1)} async-done(((bf16[8,208,1536]{2,1,0:T(8,128)(2,1)}), bf16[1,208,1536]{2,1,0:T(8,128)(2,1)}) %reduce-scatter.3.cloned.1.call-update) | async-done | bytes 638992 | tf_op jit(solution)/shard_map/reduce_scatter | solution.py:572
  596.8 6.0 collective-permute-start.42
  608.2 4.5 collective-permute-start.41
  (260 shorter events, 122.4 us)
Async XLA Ops:
  7.2 164.0 %all-gather.5.cloned.1.call-start = ((), (), s32[]{:S(2)}) async-start(), calls=%async_computation.6 | async-start | bytes 12386304 | tf_op jit(solution)/shard_map/all_gather | solution.py:394
  39.6 28.8 %collective-permute-start.8 = (bf16[208,1536]{1,0:T(8,128)(2,1)}, bf16[208,1536]{1,0:T(8,128)(2,1)}, u32[]{:S(2)}, u32[]{:S(2)}) collective-permute-start(bf16[208,1536]{1,0:T(8,128)(2,1)} %shard_map.177.refs_1_.refs_7_), channel_id=1, source_target_pairs={{0,2},{2,0},{4,6},{6,4},{1,3},{3,1},{5,7},{7,5},{8,10},{10,8},{12,... | collective-permute-start | bytes 1916936 | tf_op jit(solution)/shard_map/ppermute | solution.py:42
  43.4 79.5 %all-to-all-start = ((bf16[32,48,216]{2,1,0:T(8,128)(2,1)}), bf16[32,48,216]{2,1,0:T(8,128)(2,1)S(1)}, u32[]{:S(2)}, u32[]{:S(2)}) async-start(bf16[32,48,216]{2,1,0:T(8,128)(2,1)} %shard_map.181), calls=%async_computation | async-start | bytes 1572864 | tf_op jit(solution)/shard_map/all_to_all | solution.py:354
  46.1 189.3 %all-gather.7.cloned.1.call-start = ((), (), s32[]{:S(2)}) async-start(), calls=%async_computation.7 | async-start | bytes 6193152 | tf_op jit(solution)/shard_map/all_gather | solution.py:432
  71.1 75.9 %collective-permute-start.15 = (bf16[3,208,1536]{2,1,0:T(8,128)(2,1)}, bf16[3,208,1536]{2,1,0:T(8,128)(2,1)}, u32[]{:S(2)}, u32[]{:S(2)}) collective-permute-start(bf16[3,208,1536]{2,1,0:T(8,128)(2,1)} %pad_maximum_fusion), channel_id=1, source_target_pairs={{0,1},{1,0},{2,3},{3,2},{4,5},{5,4},{6,7},{7,6},{8,9},{9,8},{10,11... | collective-permute-start | bytes 5750792 | tf_op jit(solution)/shard_map/ppermute | solution.py:42
  72.0 40.0 %collective-permute-start.14 = (bf16[272,1536]{1,0:T(8,128)(2,1)}, bf16[272,1536]{1,0:T(8,128)(2,1)}, u32[]{:S(2)}, u32[]{:S(2)}) collective-permute-start(bf16[272,1536]{1,0:T(8,128)(2,1)} %shard_map.178.refs_0_), channel_id=1, source_target_pairs={{0,24},{8,16},{16,8},{24,0},{1,25},{9,17},{17,9},{25,1},{2,26},{10... | collective-permute-start | bytes 2506760 | tf_op jit(solution)/shard_map/ppermute | solution.py:42
  72.5 50.3 %collective-permute-start.13 = (bf16[272,1536]{1,0:T(8,128)(2,1)}, bf16[272,1536]{1,0:T(8,128)(2,1)}, u32[]{:S(2)}, u32[]{:S(2)}) collective-permute-start(bf16[272,1536]{1,0:T(8,128)(2,1)} %shard_map.178.refs_0_), channel_id=1, source_target_pairs={{0,16},{8,24},{16,0},{24,8},{1,17},{9,25},{17,1},{25,9},{2,18},{10... | collective-permute-start | bytes 2506760 | tf_op jit(solution)/shard_map/ppermute | solution.py:42
  73.5 49.3 %collective-permute-start.7 = (bf16[272,1536]{1,0:T(8,128)(2,1)}, bf16[272,1536]{1,0:T(8,128)(2,1)S(1)}, u32[]{:S(2)}, u32[]{:S(2)}) collective-permute-start(bf16[272,1536]{1,0:T(8,128)(2,1)} %shard_map.178.refs_0_), channel_id=1, source_target_pairs={{0,8},{8,0},{16,24},{24,16},{1,9},{9,1},{17,25},{25,17},{2,10},{10... | collective-permute-start | bytes 2506760 | tf_op jit(solution)/shard_map/ppermute | solution.py:42
  75.5 34.3 %collective-permute-start.9 = (bf16[208,1536]{1,0:T(8,128)(2,1)S(1)}, bf16[208,1536]{1,0:T(8,128)(2,1)}, u32[]{:S(2)}, u32[]{:S(2)}) collective-permute-start(bf16[208,1536]{1,0:T(8,128)(2,1)S(1)} %copy-done.7), channel_id=1, source_target_pairs={{0,4},{2,6},{4,0},{6,2},{1,5},{3,7},{5,1},{7,3},{8,12},{10,14},{12... | collective-permute-start | bytes 1916936 | tf_op jit(solution)/shard_map/ppermute | solution.py:42
  112.0 34.9 %collective-permute-start.11 = (bf16[256,1536]{1,0:T(8,128)(2,1)}, bf16[256,1536]{1,0:T(8,128)(2,1)}, u32[]{:S(2)}, u32[]{:S(2)}) collective-permute-start(bf16[256,1536]{1,0:T(8,128)(2,1)} %shard_map.179.refs_0_.refs_4_), channel_id=1, source_target_pairs={{0,2},{2,0},{4,6},{6,4},{1,3},{3,1},{5,7},{7,5},{8,10},{10,8},{12,... | collective-permute-start | bytes 2359304 | tf_op jit(solution)/shard_map/ppermute | solution.py:42
  171.2 339.4 %reduce-scatter.5.cloned.1.call-start = ((), (), s32[]{:S(2)}) async-start(), calls=%async_computation.5 | async-start | bytes 18579456 | tf_op jit(solution)/shard_map/reduce_scatter | solution.py:481
  171.7 28.1 %collective-permute-start.17 = (bf16[256,1536]{1,0:T(8,128)(2,1)}, bf16[256,1536]{1,0:T(8,128)(2,1)S(1)}, u32[]{:S(2)}, u32[]{:S(2)}) collective-permute-start(bf16[256,1536]{1,0:T(8,128)(2,1)} %get-tuple-element.48), channel_id=1, source_target_pairs={{0,8},{8,0},{16,24},{24,16},{1,9},{9,1},{17,25},{25,17},{2,10},{10... | collective-permute-start | bytes 2359304 | tf_op jit(solution)/shard_map/ppermute | solution.py:42
  173.4 37.5 %collective-permute-start.18 = (bf16[256,1536]{1,0:T(8,128)(2,1)}, bf16[256,1536]{1,0:T(8,128)(2,1)S(1)}, u32[]{:S(2)}, u32[]{:S(2)}) collective-permute-start(bf16[256,1536]{1,0:T(8,128)(2,1)} %get-tuple-element.49), channel_id=1, source_target_pairs={{0,16},{8,24},{16,0},{24,8},{1,17},{9,25},{17,1},{25,9},{2,18},{10... | collective-permute-start | bytes 2359304 | tf_op jit(solution)/shard_map/ppermute | solution.py:42
  174.9 53.4 %collective-permute-start.19 = (bf16[256,1536]{1,0:T(8,128)(2,1)}, bf16[256,1536]{1,0:T(8,128)(2,1)}, u32[]{:S(2)}, u32[]{:S(2)}) collective-permute-start(bf16[256,1536]{1,0:T(8,128)(2,1)} %get-tuple-element.50), channel_id=1, source_target_pairs={{0,24},{8,16},{16,8},{24,0},{1,25},{9,17},{17,9},{25,1},{2,26},{10... | collective-permute-start | bytes 2359304 | tf_op jit(solution)/shard_map/ppermute | solution.py:42
  175.3 60.2 %collective-permute-start.21 = (bf16[256,1536]{1,0:T(8,128)(2,1)S(1)}, bf16[256,1536]{1,0:T(8,128)(2,1)}, u32[]{:S(2)}, u32[]{:S(2)}) collective-permute-start(bf16[256,1536]{1,0:T(8,128)(2,1)S(1)} %copy-done.16), channel_id=1, source_target_pairs={{0,4},{2,6},{4,0},{6,2},{1,5},{3,7},{5,1},{7,3},{8,12},{10,14},{12... | collective-permute-start | bytes 2359304 | tf_op jit(solution)/shard_map/ppermute | solution.py:42
  232.0 33.3 %collective-permute-start.22 = (bf16[256,1536]{1,0:T(8,128)(2,1)}, bf16[256,1536]{1,0:T(8,128)(2,1)S(1)}, u32[]{:S(2)}, u32[]{:S(2)}) collective-permute-start(bf16[256,1536]{1,0:T(8,128)(2,1)} %multiply_convert_fusion.refs_0_), channel_id=1, source_target_pairs={{0,2},{2,0},{4,6},{6,4},{1,3},{3,1},{5,7},{7,5},{8,10},{10,8},{12,... | collective-permute-start | bytes 2359304 | tf_op jit(solution)/shard_map/ppermute | solution.py:42
  232.0 36.1 %collective-permute-start.23 = (bf16[256,1536]{1,0:T(8,128)(2,1)}, bf16[256,1536]{1,0:T(8,128)(2,1)}, u32[]{:S(2)}, u32[]{:S(2)}) collective-permute-start(bf16[256,1536]{1,0:T(8,128)(2,1)} %multiply_convert_fusion.refs_0_), channel_id=1, source_target_pairs={{0,6},{2,4},{4,2},{6,0},{1,7},{3,5},{5,3},{7,1},{8,14},{10,12},{12... | collective-permute-start | bytes 2359304 | tf_op jit(solution)/shard_map/ppermute | solution.py:42
  232.3 77.8 %collective-permute-start.20 = (bf16[256,1536]{1,0:T(8,128)(2,1)}, bf16[256,1536]{1,0:T(8,128)(2,1)}, u32[]{:S(2)}, u32[]{:S(2)}) collective-permute-start(bf16[256,1536]{1,0:T(8,128)(2,1)} %multiply_convert_fusion.refs_0_), channel_id=1, source_target_pairs={{0,4},{2,6},{4,0},{6,2},{1,5},{3,7},{5,1},{7,3},{8,12},{10,14},{12... | collective-permute-start | bytes 2359304 | tf_op jit(solution)/shard_map/ppermute | solution.py:42
  288.6 68.8 %collective-permute-start.24 = (bf16[256,1536]{1,0:T(8,128)(2,1)}, bf16[256,1536]{1,0:T(8,128)(2,1)S(1)}, u32[]{:S(2)}, u32[]{:S(2)}) collective-permute-start(bf16[256,1536]{1,0:T(8,128)(2,1)} %get-tuple-element.58), channel_id=1, source_target_pairs={{0,2},{2,0},{4,6},{6,4},{1,3},{3,1},{5,7},{7,5},{8,10},{10,8},{12,... | collective-permute-start | bytes 2359304 | tf_op jit(solution)/shard_map/ppermute | solution.py:42
  309.1 48.3 %collective-permute-start.26 = (bf16[256,1536]{1,0:T(8,128)(2,1)}, bf16[256,1536]{1,0:T(8,128)(2,1)S(1)}, u32[]{:S(2)}, u32[]{:S(2)}) collective-permute-start(bf16[256,1536]{1,0:T(8,128)(2,1)} %get-tuple-element.60), channel_id=1, source_target_pairs={{0,6},{2,4},{4,2},{6,0},{1,7},{3,5},{5,3},{7,1},{8,14},{10,12},{12... | collective-permute-start | bytes 2359304 | tf_op jit(solution)/shard_map/ppermute | solution.py:42
  359.3 227.4 %reduce-scatter.3.cloned.1.call-start = ((), (), s32[]{:S(2)}) async-start(), calls=%async_computation.4 | async-start | bytes 5750784 | tf_op jit(solution)/shard_map/reduce_scatter | solution.py:572
  359.4 30.1 %collective-permute-start.25 = (bf16[256,1536]{1,0:T(8,128)(2,1)}, bf16[256,1536]{1,0:T(8,128)(2,1)}, u32[]{:S(2)}, u32[]{:S(2)}) collective-permute-start(bf16[256,1536]{1,0:T(8,128)(2,1)} %get-tuple-element.59), channel_id=1, source_target_pairs={{0,4},{2,6},{4,0},{6,2},{1,5},{3,7},{5,1},{7,3},{8,12},{10,14},{12... | collective-permute-start | bytes 2359304 | tf_op jit(solution)/shard_map/ppermute | solution.py:42
  395.0 38.4 %collective-permute-start.29 = (bf16[256,1536]{1,0:T(8,128)(2,1)}, bf16[256,1536]{1,0:T(8,128)(2,1)}, u32[]{:S(2)}, u32[]{:S(2)}) collective-permute-start(bf16[256,1536]{1,0:T(8,128)(2,1)} %get-tuple-element.86.refs_0_.refs_4_), channel_id=1, source_target_pairs={{0,24},{8,16},{16,8},{24,0},{1,25},{9,17},{17,9},{25,1},{2,26},{10... | collective-permute-start | bytes 2359304 | tf_op jit(solution)/shard_map/ppermute | solution.py:42
  396.8 52.5 %collective-permute-start.28 = (bf16[256,1536]{1,0:T(8,128)(2,1)}, bf16[256,1536]{1,0:T(8,128)(2,1)}, u32[]{:S(2)}, u32[]{:S(2)}) collective-permute-start(bf16[256,1536]{1,0:T(8,128)(2,1)} %get-tuple-element.86.refs_0_.refs_4_), channel_id=1, source_target_pairs={{0,16},{8,24},{16,0},{24,8},{1,17},{9,25},{17,1},{25,9},{2,18},{10... | collective-permute-start | bytes 2359304 | tf_op jit(solution)/shard_map/ppermute | solution.py:42
  398.2 66.0 %collective-permute-start.27 = (bf16[256,1536]{1,0:T(8,128)(2,1)}, bf16[256,1536]{1,0:T(8,128)(2,1)}, u32[]{:S(2)}, u32[]{:S(2)}) collective-permute-start(bf16[256,1536]{1,0:T(8,128)(2,1)} %get-tuple-element.86.refs_0_.refs_4_), channel_id=1, source_target_pairs={{0,8},{8,0},{16,24},{24,16},{1,9},{9,1},{17,25},{25,17},{2,10},{10... | collective-permute-start | bytes 2359304 | tf_op jit(solution)/shard_map/ppermute | solution.py:42
  399.1 74.5 %collective-permute-start.30 = (bf16[256,1536]{1,0:T(8,128)(2,1)}, bf16[256,1536]{1,0:T(8,128)(2,1)S(1)}, u32[]{:S(2)}, u32[]{:S(2)}) collective-permute-start(bf16[256,1536]{1,0:T(8,128)(2,1)} %shard_map.193), channel_id=1, source_target_pairs={{0,2},{2,0},{4,6},{6,4},{1,3},{3,1},{5,7},{7,5},{8,10},{10,8},{12,... | collective-permute-start | bytes 2359304 | tf_op jit(solution)/shard_map/ppermute | solution.py:42
  399.1 74.5 %collective-permute-start.31 = (bf16[256,1536]{1,0:T(8,128)(2,1)}, bf16[256,1536]{1,0:T(8,128)(2,1)S(1)}, u32[]{:S(2)}, u32[]{:S(2)}) collective-permute-start(bf16[256,1536]{1,0:T(8,128)(2,1)} %shard_map.194), channel_id=1, source_target_pairs={{0,4},{2,6},{4,0},{6,2},{1,5},{3,7},{5,1},{7,3},{8,12},{10,14},{12... | collective-permute-start | bytes 2359304 | tf_op jit(solution)/shard_map/ppermute | solution.py:42
  433.5 40.1 %collective-permute-start.32 = (bf16[256,1536]{1,0:T(8,128)(2,1)}, bf16[256,1536]{1,0:T(8,128)(2,1)}, u32[]{:S(2)}, u32[]{:S(2)}) collective-permute-start(bf16[256,1536]{1,0:T(8,128)(2,1)} %shard_map.195), channel_id=1, source_target_pairs={{0,6},{2,4},{4,2},{6,0},{1,7},{3,5},{5,3},{7,1},{8,14},{10,12},{12... | collective-permute-start | bytes 2359304 | tf_op jit(solution)/shard_map/ppermute | solution.py:42
  500.1 25.3 %collective-permute-start.34 = (bf16[256,1536]{1,0:T(8,128)(2,1)}, bf16[256,1536]{1,0:T(8,128)(2,1)}, u32[]{:S(2)}, u32[]{:S(2)}) collective-permute-start(bf16[256,1536]{1,0:T(8,128)(2,1)} %get-tuple-element.76), channel_id=1, source_target_pairs={{0,8},{8,0},{16,24},{24,16},{1,9},{9,1},{17,25},{25,17},{2,10},{10... | collective-permute-start | bytes 2359304 | tf_op jit(solution)/shard_map/ppermute | solution.py:42
  500.1 25.3 %collective-permute-start.35 = (bf16[256,1536]{1,0:T(8,128)(2,1)}, bf16[256,1536]{1,0:T(8,128)(2,1)}, u32[]{:S(2)}, u32[]{:S(2)}) collective-permute-start(bf16[256,1536]{1,0:T(8,128)(2,1)} %get-tuple-element.77), channel_id=1, source_target_pairs={{0,16},{8,24},{16,0},{24,8},{1,17},{9,25},{17,1},{25,9},{2,18},{10... | collective-permute-start | bytes 2359304 | tf_op jit(solution)/shard_map/ppermute | solution.py:42
  503.8 43.7 %collective-permute-start.36 = (bf16[256,1536]{1,0:T(8,128)(2,1)}, bf16[256,1536]{1,0:T(8,128)(2,1)}, u32[]{:S(2)}, u32[]{:S(2)}) collective-permute-start(bf16[256,1536]{1,0:T(8,128)(2,1)} %get-tuple-element.78), channel_id=1, source_target_pairs={{0,24},{8,16},{16,8},{24,0},{1,25},{9,17},{17,9},{25,1},{2,26},{10... | collective-permute-start | bytes 2359304 | tf_op jit(solution)/shard_map/ppermute | solution.py:42
  515.0 71.8 %all-to-all-start.1 = ((bf16[32,48,216]{2,1,0:T(8,128)(2,1)}), bf16[32,48,216]{2,1,0:T(8,128)(2,1)S(1)}, u32[]{:S(2)}, u32[]{:S(2)}) async-start(bf16[32,48,216]{2,1,0:T(8,128)(2,1)} %bitcast.200), calls=%async_computation.3 | async-start | bytes 1572864 | tf_op jit(solution)/shard_map/all_to_all | solution.py:574
  (50 other events, 524.9 us)
Sparse Core Ops, SparseCore 0:
  10.0 105.9 all-gather.4
  171.3 62.2 all-gather.6
  359.5 151.1 reduce-scatter.4
  512.9 73.7 reduce-scatter.2

commit v3 on v2

--- a/solution.py
+++ b/solution.py
@@ -74,14 +74,15 @@
     return pl.BlockSpec(shape, lambda *_: (0,) * len(shape))
 
 
-def kernel_call(body, grid, ins, outs, scratch, flops, *args):
+def kernel_call(body, grid, ins, outs, scratch, flops, *args, waits=()):
+    held = len(args)
     shapes = [jax.ShapeDtypeStruct(shape, dtype) for shape, dtype, _ in outs]
     moved = sum(a.size * a.dtype.itemsize for a in args)
-    moved += sum(s.size * s.dtype.itemsize for s in shapes)
+    moved = (moved + sum(s.size * s.dtype.itemsize for s in shapes)) * (flops > 0)
     return pl.pallas_call(
-        body,
+        lambda *refs: body(*refs[:held], *refs[held + len(waits) :]),
         grid=grid,
-        in_specs=ins,
+        in_specs=ins + [pl.BlockSpec(memory_space=pl.ANY)] * len(waits),
         out_specs=[spec for _, _, spec in outs],
         out_shape=shapes,
         scratch_shapes=scratch,
@@ -89,7 +90,7 @@
             dimension_semantics=("arbitrary",) * len(grid), vmem_limit_bytes=vmem_bytes
         ),
         cost_estimate=pl.CostEstimate(flops=flops, bytes_accessed=moved, transcendentals=0),
-    )(*args)
+    )(*args, *waits)
 
 
 def shifted(block, distance, edge):
@@ -103,16 +104,30 @@
 
 
 def mixer_forward(seqs, group, lanes, line, in_place, *refs):
-    tok_refs, (gain_ref, taps_ref), refs = refs[:lanes], refs[lanes : lanes + 2], refs[lanes + 2 :]
+    tok_refs, refs = refs[:lanes], refs[lanes:]
     if in_place:
-        places_ref, source_refs, refs = refs[0], refs[1 : 1 + 2 * line], refs[1 + 2 * line :]
-        win_ref, wout_ref = refs[lanes + 8 : lanes + 10]
-        bring_weights(2 * line, places_ref, source_refs, win_ref, wout_ref, refs[-1])
+        places_ref, source_refs, other, refs = refs[0], refs[1 : 1 + line], refs[1 + line], refs[2 + line :]
+        source_refs = list(source_refs) + [other.at[r] for r in range(line)]
+        win_ref, wout_ref = refs[lanes + 9 : lanes + 11]
+        bring_weights(2 * line, places_ref, source_refs, win_ref, wout_ref, *refs[-2:])
     else:
-        (win_ref, wout_ref), refs = refs[:2], refs[2:]
+        (added_ref, taps_ref, win_ref, wout_ref), refs = refs[:4], refs[4:]
     part_refs, refs = refs[:lanes], refs[lanes:]
-    norm_ref, b_ref, c_ref, x_ref, conv_ref, gated_ref, halo_ref, y_ref = refs[:8]
-    tok_ref = refs[10 if in_place else 8]
+    norm_ref, b_ref, c_ref, x_ref, conv_ref, gated_ref, halo_ref, y_ref, small_ref = refs[:9]
+    tok_ref = refs[11 if in_place else 9]
+
+    @pl.when(pl.program_id(0) == 0)
+    def _():
+        if in_place:
+            small_ref[...] = sum(refs[-2][k].astype(f32) for k in range(2 * line))
+        else:
+            small_ref[...] = added_ref[...]
+
+    gain_ref = small_ref.at[0:1]
+    if in_place:
+        mine = wout_ref.shape[1]
+        at = pl.multiple_of(places_ref[2 * line] * mine, 128)
+        taps_ref = small_ref.at[2:5, pl.ds(at, mine)]
     pick(tok_refs, tok_ref)
     rows = seqs * group
     h = tok_ref[...].astype(f32)
@@ -144,13 +159,12 @@
     return ref[...].reshape(n * units, width)
 
 
-def hidden_gradient(line, *refs):
-    cot_refs, down_ref, out_refs = refs[:line], refs[line], refs[line + 1 :]
+def hidden_gradient(n, *refs):
+    cot_refs, down_ref, out_ref = refs[:n], refs[n], refs[n + 1]
     w_down = merged(down_ref)
     rows = cot_refs[0].shape[0]
-    for r in range(line):
-        at = slice(r // 2 * rows, (r // 2 + 1) * rows)
-        out_refs[r % 2][0, at] = dot_nt(cot_refs[r][...], w_down)
+    for r in range(n):
+        out_ref[0, r * rows : (r + 1) * rows] = dot_nt(cot_refs[r][...], w_down)
 
 
 def add_up(acc_ref, at, part, out_ref):
@@ -194,24 +208,21 @@
         add_up(acc_ref, slice(r * rows, (r + 1) * rows), part, out_refs[r])
 
 
-def feed_forward_grads(line, *refs):
-    u_refs, cot_refs, refs = refs[:line], refs[line : 2 * line], refs[2 * line :]
-    halves, out_ref, (u_all, cot_all) = (refs[:3], refs[3:6]), refs[6], refs[7:]
-    rows = u_refs[0].shape[0]
+def feed_forward_grads(line, kinds, *refs):
+    right_refs, halves, refs = refs[:line], refs[line : line + 2 * kinds], refs[line + 2 * kinds :]
+    out_ref, right_all = refs
+    rows = right_refs[0].shape[0]
 
     @pl.when(pl.program_id(0) == 0)
     def _():
         for r in range(line):
-            at = slice(r // 2 * rows, (r // 2 + 1) * rows)
-            u_all[r % 2, at] = u_refs[r][...]
-            cot_all[r % 2, at] = cot_refs[r][...]
+            right_all[r % 2, r // 2 * rows : (r // 2 + 1) * rows] = right_refs[r][...]
 
     n, units, width = out_ref.shape
-    units //= 3
-    for k, right in enumerate((cot_all, u_all, u_all)):
-        part = sum(dot_tn(halves[h][k][0], right[h]) for h in range(2))
-        at = (k - 1) % 3 * units
-        out_ref[:, at : at + units] = part.astype(bf16).reshape(n, units, width)
+    units //= kinds
+    for k in range(kinds):
+        part = sum(dot_tn(halves[h * kinds + k][0], right_all[h]) for h in range(2))
+        out_ref[:, k * units : (k + 1) * units] = part.astype(bf16).reshape(n, units, width)
 
 
 def pick(slot_refs, out_ref):
@@ -230,7 +241,7 @@
             ref[...] = block
 
 
-def bring_weights(pieces, places_ref, sources, win_ref, wout_ref, sems):
+def bring_weights(pieces, places_ref, sources, win_ref, wout_ref, small_ref, sems):
     width, mine = wout_ref.shape
     feats = mine // pieces
     copies = []
@@ -243,6 +254,7 @@
             rows = pl.ds(pl.multiple_of((f * pieces + s) * feats, 16), feats)
             columns = source.at[pl.ds(3 * feats, feats), pl.ds(f * mine, mine)]
             copies.append((columns, wout_ref.at[rows]))
+        copies.append((source.at[pl.ds(4 * feats, 16)], small_ref.at[k]))
     copies = [pltpu.make_async_copy(a, b, sems.at[n]) for n, (a, b) in enumerate(copies)]
 
     @pl.when(pl.program_id(0) == 0)
@@ -261,11 +273,12 @@
     dc_ref[0] = (dy * conv_ref[0]).astype(bf16)
 
 
-def mixer_backward_two(seqs, group, pieces, lanes, *refs):
+def mixer_backward_two(seqs, group, pieces, lanes, in_place, *refs):
     tok_refs, branch_refs, refs = refs[:lanes], refs[lanes : 2 * lanes], refs[2 * lanes :]
     (dconv_ref, ahead_ref, dc_ref, b_ref, x_ref, gated_ref, halo_ref, taps_ref, two_ref) = refs[:9]
-    (win_ref, norm_ref, y_ref), refs = refs[9:12], refs[12:]
-    part_refs, (out_ref, dm_ref, one_ref, dt_ref, tok_ref) = refs[:lanes], refs[lanes:]
+    (win_ref, norm_ref, y_ref, places_ref), refs = refs[9:13], refs[13:]
+    part_refs, out_refs, refs = refs[:lanes], refs[lanes : lanes + 2], refs[lanes + 2 :]
+    dm_ref, one_ref, dt_ref, tok_ref, gin_ref, gout_ref = refs
     pick(tok_refs, tok_ref)
     r = pl.program_id(0)
     rows = seqs * group
@@ -305,18 +318,27 @@
         feats = mine // pieces
         norm = norm_ref[...].reshape(slots * rows, width)
         for p in range(3):
-            g_in = dot_tn(dm_ref[p].reshape(slots * rows, mine), norm).astype(bf16)
-            for s in range(pieces):
-                out_ref[s, p * feats : (p + 1) * feats] = g_in[s * feats : (s + 1) * feats]
-        g_out = sum(dot_tn(branch_refs[f][...], y_ref[f]) for f in range(lanes)).astype(bf16)
+            gin_ref[p] = dot_tn(dm_ref[p].reshape(slots * rows, mine), norm).astype(bf16)
+        g_out = sum(dot_tn(branch_refs[f][...], y_ref[f]) for f in range(lanes))
+        gout_ref[...] = g_out.astype(bf16)
         small = jnp.concatenate([one_ref[...], two_ref[...], jnp.zeros((14, width), f32)], 0)
         small = small.astype(bf16)
-        for s in range(pieces):
+        for n in range(pieces):
+            out_ref, k = out_refs[n * 2 // pieces], n % (pieces // 2)
+            s = pl.multiple_of(places_ref[n] * feats, 16) if in_place else n * feats
+            for p in range(3):
+                out_ref[k, p * feats : (p + 1) * feats] = gin_ref[p, pl.ds(s, feats)]
             for f in range(lanes):
-                a = (f * pieces + s) * feats
-                out_ref[s, 3 * feats : 4 * feats, f * mine : (f + 1) * mine] = g_out[a : a + feats]
-            out_ref[s, 4 * feats :] = small
-            out_ref[s, 4 * feats + 2 : 4 * feats + 5, :mine] = dt_ref[...].astype(bf16)
+                at = pl.ds(f * pieces * feats + s, feats)
+                out_ref[k, 3 * feats : 4 * feats, f * mine : (f + 1) * mine] = gout_ref[at]
+            out_ref[k, 4 * feats :] = small
+            out_ref[k, 4 * feats + 2 : 4 * feats + 5, :mine] = dt_ref[...].astype(bf16)
+
+
+def add_cores(*refs):
+    own_ref, came_ref, out_refs = refs[0], refs[1], refs[2:]
+    for r, out_ref in enumerate(out_refs):
+        out_ref[...] = (own_ref[r].astype(f32) + came_ref[r].astype(f32)).astype(bf16)
 
 
 def on_device(tokens, gain_one, gain_two, conv_taps, w_in, w_out, w_gate, w_up, w_down, cotangent):
@@ -342,51 +364,52 @@
     in_parts = [
         lax.dynamic_index_in_dim(came, (index + p * count) % 3, 0, keepdims=False) for p in range(3)
     ]
-    smalls = jnp.concatenate([gain_one[None], gain_two[None], conv_taps], 0)
-    smalls = jnp.pad(smalls, ((0, 11), (0, mine - feats)))
+    smalls = jnp.pad(jnp.concatenate([gain_one[None], gain_two[None], conv_taps], 0), ((0, 11), (0, 0)))
+    smalls = lax.dynamic_update_slice(jnp.zeros((16, mine), bf16), smalls, (0, s_index * feats))
     out_blocks = w_out.T.reshape(feats, lanes, mine).transpose(1, 0, 2)
     out_blocks = jnp.concatenate([out_blocks, jnp.broadcast_to(smalls, (lanes, 16, mine))], 1)
     out_blocks = jnp.concatenate(exchange(out_blocks, "fsdp"), 1)
     edge = lax.ppermute(tokens[:, group - 2 :], ("line", "core"), onward).reshape(2 * seqs, width)
     edge = jnp.pad(edge, ((0, -2 * seqs % 16), (0, 0)))
     mixer_own = tie(jnp.concatenate(in_parts + [out_blocks], 0), edge)
+    mixer_slots = gather(mixer_own, "line")
+    token_rows = tokens.reshape(rows, width)
+    token_slots = gather(tie(jnp.concatenate([token_rows, edge], 0), mixer_own), "fsdp")
+
     down_rows = tie(w_down.T.reshape(feats, count, hid).transpose(1, 0, 2), mixer_own)
     down_rows = lax.all_to_all(down_rows, every, 0, 0, tiled=True)
-    mixer_slots = gather(mixer_own, "line")
-
-    token_rows = tokens.reshape(rows, width)
-    token_slots = gather(tie(jnp.concatenate([token_rows, edge], 0), mixer_own), "fsdp")
-
-    swapped = list(flip(jnp.stack(mixer_slots[:1] + mixer_slots[1::2]), "core", 1))
-    late = flip(tie(jnp.stack(mixer_slots[2::2]), *token_slots[1:], down_rows), "core", 1)
-    swapped = [swapped[0]] + [s for pair in zip(swapped[1:], list(late) + [None]) for s in pair][:-1]
+
+    swapped = tie(jnp.stack(mixer_slots), *token_slots[1:], down_rows)
+    swapped = flip(swapped, "core", 1)
     cot_rows = cotangent.reshape(rows, width)
     cot_slots = gather(tie(cot_rows, *mixer_slots[1:]), "line")
     z_index, c_index = lax.axis_index("line"), lax.axis_index("core")
-    near = jnp.arange(line, dtype=jnp.int32) ^ z_index
-    places = jnp.concatenate([2 * near + c_index, 2 * near + 1 - c_index])
-    small = jnp.stack([m[4 * feats : 4 * feats + 5] for m in mixer_slots + swapped])
-    small = small.reshape(pieces, 5, lanes, mine)[..., :feats].reshape(pieces, 5 * lanes * feats)
-    order = (places[None] == jnp.arange(pieces)[:, None]).astype(bf16)
-    small = dot(order, small).reshape(pieces, 5, lanes, feats)
-    small = small.transpose(1, 2, 0, 3).reshape(5, width)
-    taps = lax.dynamic_slice_in_dim(small[2:], f_index * mine, mine, 1)
+    near = [r ^ z_index for r in range(line)]
+    places = [2 * z + c_index for z in near]
+    places += [2 * z + 1 - c_index for z in near]
+    places = jnp.stack(places + [f_index]).astype(jnp.int32)
     anywhere = pl.BlockSpec(memory_space=pl.ANY)
     in_place = feats % 16 == 0 and mine % 128 == 0
     if in_place:
-        weights = [places] + mixer_slots + swapped
-        weight_specs = [pl.BlockSpec(memory_space=pltpu.SMEM)] + [anywhere] * pieces
+        weights = [places] + mixer_slots + [swapped]
+        weight_specs = [pl.BlockSpec(memory_space=pltpu.SMEM)] + [anywhere] * (line + 1)
         weight_outs = [((3, mine, width), bf16, whole((3, mine, width)))]
         weight_outs += [((width, mine), bf16, whole((width, mine)))]
-        weight_scratch = [pltpu.SemaphoreType.DMA((pieces * (3 + lanes),))]
+        weight_scratch = [
+            pltpu.VMEM((pieces, 16, width), bf16),
+            pltpu.SemaphoreType.DMA((pieces * (4 + lanes),)),
+        ]
     else:
-        mixer_w = jnp.stack(mixer_slots + swapped)[jnp.argsort(places)]
+        mixer_w = jnp.concatenate([jnp.stack(mixer_slots), swapped], 0)[jnp.argsort(places[:-1])]
         full_in = mixer_w[:, : 3 * feats].reshape(pieces, 3, feats, width)
         full_in = full_in.transpose(1, 0, 2, 3).reshape(3, mine, width)
         full_out = mixer_w[:, 3 * feats : 4 * feats].reshape(pieces, feats, lanes, mine)
         full_out = full_out.transpose(2, 0, 1, 3).reshape(width, mine)
-        weights = [full_in, full_out]
-        weight_specs = [whole((3, mine, width)), whole((width, mine))]
+        small = jnp.sum(mixer_w[:, 4 * feats :].astype(f32), axis=0)
+        taps = lax.dynamic_slice_in_dim(small[2:5], f_index * mine, mine, 1)
+        weights = [small, taps, full_in, full_out]
+        weight_specs = [whole((16, width)), whole((3, mine))]
+        weight_specs += [whole((3, mine, width)), whole((width, mine))]
         weight_outs = weight_scratch = []
 
     pad = ((0, units - hid), (0, 0))
@@ -401,24 +424,23 @@
     made = kernel_call(
         functools.partial(mixer_forward, seqs, group, lanes, line, in_place),
         (lanes,),
-        [whole((more, width))] * lanes + [whole((1, width)), whole((3, mine))] + weight_specs,
+        [whole((more, width))] * lanes + weight_specs,
         flat(rows, lanes)
         + [per_slot(bf16, rows, width)]
         + [per_slot(f32, rows, mine)] * 4
         + [per_slot(bf16, rows, mine), per_slot(bf16, more - rows, mine), per_slot(bf16, rows, mine)]
+        + [((16, width), f32, whole((16, width)))]
         + weight_outs,
         [pltpu.VMEM((more, width), bf16)] + weight_scratch,
-        8 * everyone * width * mine,
-        *token_slots[:1],
-        tie(token_slots[1], *cot_slots[1::2]),
-        *token_slots[2:],
-        small[:1],
-        taps,
+        24 * everyone * width * mine,
+        *token_slots,
         *weights,
     )
-    branch_o, held = made[:lanes], made[lanes + 8 :]
-    normed_a, b_part, c_part, x_part, conv, gated, halo, branch_y = made[lanes : lanes + 8]
-    full_in, full_out = held if in_place else weights
+    branch_o, held = list(made[:lanes]), made[lanes + 9 :]
+    normed_a, b_part, c_part, x_part, conv, gated, halo, branch_y, small = made[lanes : lanes + 9]
+    full_in, full_out = held if in_place else weights[2:]
+    taps = lax.dynamic_slice_in_dim(small[2:5], f_index * mine, mine, 1)
+    branch_o[1] = tie(branch_o[1], cot_slots[-1])
     branch_terms = scatter(branch_o, "fsdp")
     branch_o = total(branch_terms)
     hidden_in = token_rows.astype(f32)
@@ -428,28 +450,36 @@
     normed_u = (unit_two * small[1]).astype(bf16)
 
     down_rows = down_rows.reshape(width, hid).T
-    full_down = tie(jnp.pad(down_rows, pad), gate_up, normed_a)
+    full_down = tie(jnp.pad(down_rows, pad), gate_up, swapped)
     full_down = lax.all_gather(full_down, ("fsdp", "core"), axis=0)
 
-    u_slots = gather(normed_u, "line")
     some, half_rows = blocks // 2, line // 2 * rows
     third = lambda k: pl.BlockSpec((some, units, width), lambda j: (j, k, 0))
     half = (2, half_rows, some * units)
     per_half = pl.BlockSpec((1,) + half[1:], lambda j: (j, 0, 0))
     slot_specs = [whole((rows, width))] * line
     unit_flops = 2 * line * rows * blocks * units * width
-    dhidden = kernel_call(
-        functools.partial(hidden_gradient, line),
-        (2,),
-        slot_specs + [third(0)],
-        [(half, f32, per_half)] * 2,
-        [],
-        unit_flops,
-        *cot_slots,
-        full_down,
-    )
+    dhidden = [
+        kernel_call(
+            functools.partial(hidden_gradient, line // 2),
+            (2,),
+            slot_specs[: line // 2] + [third(0)],
+            [(half, f32, per_half)],
+            [],
+            unit_flops // 2,
+            *cot_slots[odd::2],
+            full_down,
+        )[0]
+        for odd in range(2)
+    ]
+    normed_u = tie(normed_u, *cot_slots[2::2])
+    u_slots = [normed_u] + [None] * (line - 1)
+    for r in range(1, line, 2):
+        u_slots[r] = flip(normed_u, "line", r)
+    held_back = tie(normed_u, *u_slots[1::2], dhidden[1])
+    for r in range(2, line, 2):
+        u_slots[r] = flip(held_back, "line", r)
     done, du_terms = [None, None], [None] * line
-    u_slots[1] = tie(u_slots[1], *dhidden)
     for odd in (1, 0):
         made = kernel_call(
             functools.partial(feed_forward, line // 2),
@@ -462,23 +492,28 @@
             gate_up,
             gate_up,
             dhidden[odd],
+            waits=[] if odd else [done[1][0]],
         )
         done[odd] = made[:3]
         du_terms[odd::2] = made[3:]
     du_terms = scatter(du_terms, "line")
-    (g_ff,) = kernel_call(
-        functools.partial(feed_forward_grads, line),
+    ff_grads = lambda kinds, *args: kernel_call(
+        functools.partial(feed_forward_grads, line, kinds),
         (2,),
-        slot_specs * 2 + [per_half] * 6,
-        [((blocks, 3 * units, width), bf16, pl.BlockSpec((some, 3 * units, width), lambda j: (j, 0, 0)))],
-        [pltpu.VMEM((2, half_rows, width), bf16)] * 2,
-        3 * unit_flops,
-        *u_slots,
-        *cot_slots,
-        *done[0],
-        *done[1],
-    )
-    g_ff = lax.psum_scatter(tie(g_ff, *du_terms[1::2]), ("fsdp", "core"), scatter_dimension=0)
+        slot_specs + [per_half] * (2 * kinds),
+        [
+            (
+                (blocks, kinds * units, width),
+                bf16,
+                pl.BlockSpec((some, kinds * units, width), lambda j: (j, 0, 0)),
+            )
+        ],
+        [pltpu.VMEM((2, half_rows, width), bf16)],
+        kinds * unit_flops,
+        *args,
+    )[0]
+    g_down = ff_grads(1, *cot_slots, done[0][0], done[1][0])
+    g_ff = ff_grads(2, *u_slots, *done[0][1:], *done[1][1:])
     part_out = kernel_call(
         functools.partial(feed_forward_out, line),
         (2,),
@@ -512,13 +547,16 @@
         full_out,
         c_part,
         conv,
-    )
+        waits=out_terms[1:-1] + [g_ff],
+    )
+    g_down = lax.psum_scatter(tie(g_down, dconv), ("fsdp", "core"), scatter_dimension=0)
     block_out = second + total([tie(out_terms[0], dconv)] + out_terms[1:])
     block_out = block_out.astype(bf16).reshape(seqs, group, width)
     ahead = dconv.reshape(lanes, seqs, group, mine)[:, :, :2]
     ahead = lax.ppermute(ahead, ("line", "core"), back).reshape(lanes, 2 * seqs, mine)
-    *dnormed, g_mixer = kernel_call(
-        functools.partial(mixer_backward_two, seqs, group, pieces, lanes),
+    g_rows = 4 * feats + 16
+    *dnormed, g_own, g_other = kernel_call(
+        functools.partial(mixer_backward_two, seqs, group, pieces, lanes, in_place),
         (lanes,),
         [whole((more, width))] * lanes
         + [whole((rows, width))] * lanes
@@ -535,19 +573,22 @@
             whole((3, mine, width)),
             whole((lanes, rows, width)),
             whole((lanes, rows, mine)),
+            pl.BlockSpec(memory_space=pltpu.SMEM),
         ],
         flat(rows, lanes)
-        + [((pieces, 4 * feats + 16, width), bf16, whole((pieces, 4 * feats + 16, width)))],
+        + [((line, g_rows, width), bf16, whole((line, g_rows, width)))] * 2,
         [
             pltpu.VMEM((3, lanes, rows, mine), bf16),
             pltpu.VMEM((1, width), f32),
             pltpu.VMEM((3, mine), f32),
             pltpu.VMEM((more, width), bf16),
+            pltpu.VMEM((3, mine, width), bf16),
+            pltpu.VMEM((width, mine), bf16),
         ],
         14 * everyone * width * mine,
         *token_slots,
         *branch_slots,
-        tie(dconv, *out_terms[1:]),
+        dconv,
         ahead,
         dc_part,
         b_part,
@@ -559,8 +600,30 @@
         full_in,
         normed_a,
         branch_y,
-    )
-    dnormed = total(scatter(dnormed, "fsdp"))
+        places,
+    )
+    if not in_place:
+        g_mixer = jnp.concatenate([g_own, g_other], 0)[places[:-1]]
+        g_own, g_other = g_mixer[:line], g_mixer[line:]
+    g_terms = kernel_call(
+        add_cores,
+        (1,),
+        [whole((line, g_rows, width))] * 2,
+        flat(g_rows, line),
+        [],
+        1,
+        g_own,
+        flip(g_other, "core", 1),
+    )
+    g_ff = tie(g_ff, g_other, out_terms[-1])
+    g_ff = lax.psum_scatter(g_ff, ("fsdp", "core"), scatter_dimension=0)
+    dnormed = [dnormed[0]] + [tie(d, g_terms[0]) for d in dnormed[1:]]
+    g_terms = scatter(g_terms, "line")
+    da_terms = scatter(dnormed, "fsdp")
+    g_down = g_down[:hid].T.reshape(count, feats, hid)
+    ready = g_down
+    g_down = lax.all_to_all(g_down, every, 0, 0, tiled=True)
+    dnormed = total(da_terms)
     scale_one = lax.rsqrt(jnp.mean(hidden_in * hidden_in, axis=-1, keepdims=True) + epsilon)
     unit_one = hidden_in * scale_one
     dnorm_one = dnormed * small[0]
@@ -569,10 +632,7 @@
     )
     grad_tokens = dinput.astype(bf16).reshape(seqs, group, width)
 
-    g_mixer = lax.psum_scatter(g_mixer, ("line", "core"), scatter_dimension=0)
-    g_down = g_ff[2 * units : 2 * units + hid].T.reshape(count, feats, hid)
-    g_down = lax.all_to_all(g_down, every, 0, 0, tiled=True)
-    g_mixer = tie(g_mixer, g_down)
+    g_mixer = total([tie(g_terms[0], ready)] + g_terms[1:]).astype(bf16)
     g_in = g_mixer[: 3 * feats].reshape(3, feats, width)
     homes = [[(d, k) for k, d in route] for route in routes]
     parts = []

time: 631 us -> 587 us (0.930)
  waiting for transfers between devices: 299 us -> 232 us
  starting transfers between devices: 96.7 us -> 121 us
  local copies, waits for them, and re-layouts: 41.5 us -> 29.1 us
  Pallas kernels: 140 us -> 152 us
    ppermute x35 -> x38, waiting for transfers between devices: 249 us -> 200 us  [flip(): return lax.ppermute(block, axis, [(i, i ^ bits) for i in range(size)])]
    reduce_scatter x2, waiting for transfers between devices: 40.3 us -> 21.8 us  [the longest x1 21.8 us: on_device(): g_ff = lax.psum_scatter(g_ff, ('fsdp', 'core'), scatter_dimension=0)]
    ppermute x3, starting transfers between devices: 11.1 us -> 26.9 us  [on_device(): parts.append(lax.ppermute(block, every, homes[j]))]
    pallas_call x8 -> x11, Pallas kernels: 140 us -> 152 us  [kernel_call(): pl.pallas_call(lambda *refs: body(*refs[:held], *refs[held + len(waits):]...]
    ppermute x35 -> x38, starting transfers between devices: 62.8 us -> 73.7 us  [flip(): return lax.ppermute(block, axis, [(i, i ^ bits) for i in range(size)])]
    unnamed x78 -> x60, local copies, waits for them, and re-layouts: 13.8 us -> 10 us
  transfers between devices with their start and end apart: 49 -> 52, of which waited for: 23 -> 24; matrix products, arithmetic and copies ran while one was open for 9% -> 7% of each run, Pallas kernels for 22% -> 25%
where the time goes in v3:
time: 587 us; the launch traced here: 581 us
  waiting for transfers between devices  232 us (40%)
  Pallas kernels  152 us (26%)
  starting transfers between devices  121 us (21%)
  other arithmetic  32.3 us (6%)
  local copies, waits for them, and re-layouts  29.1 us (5%)
  between operations  15.1 us (3%)
    ppermute x38, waiting for transfers between devices, flip(): return lax.ppermute(block, axis, [(i, i ^ bits) for i in range(size)])  200 us
    pallas_call x11, Pallas kernels, kernel_call(): pl.pallas_call(lambda *refs: body(*refs[:held], *refs[held + len(waits):]...  152 us
    ppermute x38, starting transfers between devices, flip(): return lax.ppermute(block, axis, [(i, i ^ bits) for i in range(size)])  73.7 us
    ppermute x3, starting transfers between devices, on_device(): parts.append(lax.ppermute(block, every, homes[j]))  26.9 us
    reduce_scatter x1, waiting for transfers between devices, on_device(): g_ff = lax.psum_scatter(g_ff, ('fsdp', 'core'), scatter_dimension=0)  21.8 us
  transfers between devices with their start and end apart: 52, of which 24 were waited for; matrix products, arithmetic and copies ran while one was open for 7% of the time, Pallas kernels for 25%

profile of v3, /device:TPU:0, one launch (start us, length us, event | category | flops | bytes accessed | tf_op | source)
XLA Modules:
  0.0 581.5 jit_solution(18434578609994458954)
XLA Ops:
  17.5 8.0 %collective-permute-start.3 = (bf16[48,1536]{1,0:T(8,128)(2,1)S(1)}, bf16[48,1536]{1,0:T(8,128)(2,1)S(1)}, u32[]{:S(2)}, u32[]{:S(2)}) collective-permute-start(bf16[48,1536]{1,0:T(8,128)(2,1)S(1)} %get-tuple-element.109), channel_id=1, source_target_pairs={{0,2},{1,5},{2,8},{3,11},{4,14},{5,17},{6,20},{7,23},{8,26},{9,29}... | collective-permute-start | bytes 442376 | tf_op jit(solution)/shard_map/ppermute | solution.py:363
  26.3 5.8 %collective-permute-done.3 = bf16[48,1536]{1,0:T(8,128)(2,1)S(1)} collective-permute-done((bf16[48,1536]{1,0:T(8,128)(2,1)S(1)}, bf16[48,1536]{1,0:T(8,128)(2,1)S(1)}, u32[]{:S(2)}, u32[]{:S(2)}) %collective-permute-start.3) | collective-permute-done | bytes 147488 | tf_op jit(solution)/shard_map/ppermute | solution.py:363
  35.3 4.7 collective-permute-start.12
  55.2 54.8 %collective-permute-done.11.refs_7_.refs_2_ = bf16[208,1536]{1,0:T(8,128)(2,1)S(1)} collective-permute-done((bf16[208,1536]{1,0:T(8,128)(2,1)}, bf16[208,1536]{1,0:T(8,128)(2,1)S(1)}, u32[]{:S(2)}, u32[]{:S(2)}) %collective-permute-start.11) | collective-permute-done | bytes 639008 | tf_op jit(solution)/shard_map/ppermute | solution.py:42
  116.2 6.8 %collective-permute-done.7.refs_1_ = bf16[272,1536]{1,0:T(8,128)(2,1)} collective-permute-done((bf16[272,1536]{1,0:T(8,128)(2,1)}, bf16[272,1536]{1,0:T(8,128)(2,1)}, u32[]{:S(2)}, u32[]{:S(2)}) %collective-permute-start.7) | collective-permute-done | bytes 835616 | tf_op jit(solution)/shard_map/ppermute | solution.py:42
  135.2 19.2 %shard_map.181 = (bf16[256,1536]{1,0:T(8,128)(2,1)}, bf16[256,1536]{1,0:T(8,128)(2,1)}, bf16[256,1536]{1,0:T(8,128)(2,1)}, bf16[256,1536]{1,0:T(8,128)(2,1)}, bf...) custom-call(bf16[272,1536]{1,0:T(8,128)(2,1)} %shard_map.178.refs_0_, ...), custom_call_target="tpu_custom_call" | custom-call | flops 14495514624 | bytes 27476004 | tf_op jit(solution)/shard_map/pallas_call | solution.py:82
  158.8 15.6 %collective-permute-start.21 = (bf16[256,1536]{1,0:T(8,128)(2,1)S(1)}, bf16[256,1536]{1,0:T(8,128)(2,1)}, u32[]{:S(2)}, u32[]{:S(2)}) collective-permute-start(bf16[256,1536]{1,0:T(8,128)(2,1)S(1)} %copy-done.4), channel_id=1, source_target_pairs={{0,2},{2,0},{4,6},{6,4},{1,3},{3,1},{5,7},{7,5},{8,10},{10,8},{12,... | collective-permute-start | bytes 2359304 | tf_op jit(solution)/shard_map/ppermute | solution.py:42
  176.3 11.9 %collective-permute-done.15 = bf16[256,1536]{1,0:T(8,128)(2,1)S(1)} collective-permute-done((bf16[256,1536]{1,0:T(8,128)(2,1)}, bf16[256,1536]{1,0:T(8,128)(2,1)S(1)}, u32[]{:S(2)}, u32[]{:S(2)}) %collective-permute-start.15) | collective-permute-done | bytes 786464 | tf_op jit(solution)/shard_map/ppermute | solution.py:42
  188.1 17.4 %collective-permute-done.17 = bf16[256,1536]{1,0:T(8,128)(2,1)S(1)} collective-permute-done((bf16[256,1536]{1,0:T(8,128)(2,1)S(1)}, bf16[256,1536]{1,0:T(8,128)(2,1)S(1)}, u32[]{:S(2)}, u32[]{:S(2)}) %collective-permute-start.17) | collective-permute-done | bytes 786464 | tf_op jit(solution)/shard_map/ppermute | solution.py:42
  214.7 7.1 %shard_map.186.refs_3_.refs_4_ = f32[2,512,896]{2,1,0:T(8,128)} custom-call(bf16[256,1536]{1,0:T(8,128)(2,1)} %collective-permute-done.21.refs_0_.refs_1_, bf16[256,1536]{1,0:T(8,128)(2,1)} %copy-done.13, bf16[8,224,1536]{2,1,0:T(8,128)(2,1)} %bitcast.172), custom_call_target="tpu_custom_call" | custom-call | flops 2818572288 | bytes 10747904 | tf_op jit(solution)/shard_map/pallas_call | solution.py:82
  221.8 10.9 %collective-permute-done.20.refs_2_.refs_1_.refs_3_ = bf16[256,1536]{1,0:T(8,128)(2,1)} collective-permute-done((bf16[256,1536]{1,0:T(8,128)(2,1)}, bf16[256,1536]{1,0:T(8,128)(2,1)}, u32[]{:S(2)}, u32[]{:S(2)}) %collective-permute-start.20) | collective-permute-done | bytes 786464 | tf_op jit(solution)/shard_map/ppermute | solution.py:42
  232.7 14.0 %collective-permute-done.19.refs_1_.refs_0_ = bf16[256,1536]{1,0:T(8,128)(2,1)} collective-permute-done((bf16[256,1536]{1,0:T(8,128)(2,1)}, bf16[256,1536]{1,0:T(8,128)(2,1)}, u32[]{:S(2)}, u32[]{:S(2)}) %collective-permute-start.19) | collective-permute-done | bytes 786464 | tf_op jit(solution)/shard_map/ppermute | solution.py:42
  247.3 20.7 %shard_map.189 = (bf16[2,512,896]{2,1,0:T(8,128)(2,1)}, bf16[2,512,896]{2,1,0:T(8,128)(2,1)}, bf16[2,512,896]{2,1,0:T(8,128)(2,1)}, bf16[256,1536]{1,0:T(8,128)(2,1)}, bf16[256,1536]{1,0:T(8,128)(2,1)}) custom-call(bf16[256,1536]{1,0:T(8,128)(2,1)} %collective-permute-done.19.refs_1_.refs_0_, ...), custom_call_target="tpu_custom_call" | custom-call | flops 11274289152 | bytes 34340864 | tf_op jit(solution)/shard_map/pallas_call | solution.py:82
  271.9 7.3 %shard_map.188.refs_4_ = f32[2,512,896]{2,1,0:T(8,128)} custom-call(bf16[256,1536]{1,0:T(8,128)(2,1)} %shard_map.182.refs_0_, bf16[256,1536]{1,0:T(8,128)(2,1)} %collective-permute-done.18.refs_1_.refs_2_, bf16[8,224,1536]{2,1,0:T(8,128)(2,1)} %bitcast.173), custom_call_target="tpu_custom_call" | custom-call | flops 2818572288 | bytes 10747904 | tf_op jit(solution)/shard_map/pallas_call | solution.py:82
  279.2 4.1 collective-permute-done.22.refs_1_.refs_2_
  284.1 20.7 %shard_map.190 = (bf16[2,512,896]{2,1,0:T(8,128)(2,1)}, bf16[2,512,896]{2,1,0:T(8,128)(2,1)}, bf16[2,512,896]{2,1,0:T(8,128)(2,1)}, bf16[256,1536]{1,0:T(8,128)(2,1)}, bf16[256,1536]{1,0:T(8,128)(2,1)}) custom-call(bf16[256,1536]{1,0:T(8,128)(2,1)} %shard_map.184.refs_0_, bf16[256,1536]{1,0:T(8,128)(2,1)} %copy-done.26, bf16[8,448,1536]{2,1,0:T(8,128)(2,1)} %bitcast.179, ...), custom_call_target="tpu_custom_call" | custom-call | flops 11274289152 | bytes 34340864 | tf_op jit(solution)/shard_map/pallas_call | solution.py:82
  304.9 12.9 %shard_map.191 = (bf16[256,1536]{1,0:T(8,128)(2,1)}, bf16[256,1536]{1,0:T(8,128)(2,1)}, bf16[256,1536]{1,0:T(8,128)(2,1)}, bf16[256,1536]{1,0:T(8,128)(2,1)}) custom-call(bf16[2,512,896]{2,1,0:T(8,128)(2,1)} %get-tuple-element.57.refs_0_.refs_4_, bf16[2,512,896]{2,1,0:T(8,128)(2,1)} %get-tuple-element.56.refs_5_.refs_1_, bf16[8,224,1536]{2,1,0:T(8,128)(2,1)} %bitcast.174), custom_call_target="tpu_custom_call" | custom-call | flops 5637144576 | bytes 12320768 | tf_op jit(solution)/shard_map/pallas_call | solution.py:82
  317.8 32.9 %collective-permute-done.24.refs_2_ = bf16[256,1536]{1,0:T(8,128)(2,1)} collective-permute-done((bf16[256,1536]{1,0:T(8,128)(2,1)}, bf16[256,1536]{1,0:T(8,128)(2,1)}, u32[]{:S(2)}, u32[]{:S(2)}) %collective-permute-start.24) | collective-permute-done | bytes 786464 | tf_op jit(solution)/shard_map/ppermute | solution.py:42
  361.9 17.7 %shard_map.195.refs_9_.refs_0_ = bf16[8,448,1536]{2,1,0:T(8,128)(2,1)} custom-call(bf16[256,1536]{1,0:T(8,128)(2,1)} %shard_map.184.refs_0_, bf16[256,1536]{1,0:T(8,128)(2,1)} %collective-permute-done.19.refs_1_.refs_0_, bf16[256,1536]{1,0:T(8,128)(2,1)} %copy-done.26, bf16[256,1536]{1,0:T(8,128)(2,1)} %collective-permute-done.20.refs_2_.refs_1_.refs_3_, ...), custom_call_target="tpu_custom_call" | custom-call | flops 11274289152 | bytes 21495808 | tf_op jit(solution)/shard_map/pallas_call | solution.py:82
  379.6 10.3 %shard_map.204.refs_0_ = bf16[8,224,1536]{2,1,0:T(8,128)(2,1)} custom-call(bf16[256,1536]{1,0:T(8,128)(2,1)} %shard_map.182.refs_0_, bf16[256,1536]{1,0:T(8,128)(2,1)} %collective-permute-done.21.refs_0_.refs_1_, bf16[256,1536]{1,0:T(8,128)(2,1)} %collective-permute-done.18.refs_1_.refs_2_, bf16[256,1536]{1,0:T(8,128)(2,1)} %copy-done.13, ...), custom_call_target="tpu_custom_call" | custom-call | flops 5637144576 | bytes 12320768 | tf_op jit(solution)/shard_map/pallas_call | solution.py:82
  389.9 3.6 collective-permute-done.27.refs_2_.refs_6_
  397.7 6.6 %shard_map.196 = (f32[4,256,384]{2,1,0:T(8,128)}, bf16[4,256,384]{2,1,0:T(8,128)(2,1)}) custom-call(bf16[256,1536]{1,0:T(8,128)(2,1)} %get-tuple-element.96.refs_0_.refs_4_, bf16[256,1536]{1,0:T(8,128)(2,1)} %collective-permute-done.26.refs_1_.refs_5_, bf16[256,1536]{1,0:T(8,128)(2,1)} %collective-permute-done.27.refs_2_.refs_6_, ...), custom_call_target="tpu_custom_call" | custom-call | flops 1207959552 | bytes 9830400 | tf_op jit(solution)/shard_map/pallas_call | solution.py:82
  411.3 24.9 %shard_map.199 = (bf16[256,1536]{1,0:T(8,128)(2,1)}, bf16[256,1536]{1,0:T(8,128)(2,1)}, bf16[256,1536]{1,0:T(8,128)(2,1)}, bf16[256,1536]{1,0:T(8,128)(2,1)}, bf...) custom-call(bf16[272,1536]{1,0:T(8,128)(2,1)} %shard_map.178.refs_0_, ...), custom_call_target="tpu_custom_call" | custom-call | flops 8455716864 | bytes 28592676 | tf_op jit(solution)/shard_map/pallas_call | solution.py:82
  437.6 4.7 collective-permute-done.33.refs_1_
  442.4 4.2 shard_map.200
  454.3 9.1 %collective-permute-start.37 = (bf16[208,1536]{1,0:T(8,128)(2,1)}, bf16[208,1536]{1,0:T(8,128)(2,1)S(1)}, u32[]{:S(2)}, u32[]{:S(2)}) collective-permute-start(bf16[208,1536]{1,0:T(8,128)(2,1)} %get-tuple-element.89), channel_id=1, source_target_pairs={{0,2},{2,0},{4,6},{6,4},{1,3},{3,1},{5,7},{7,5},{8,10},{10,8},{12,... | collective-permute-start | bytes 1916936 | tf_op jit(solution)/shard_map/ppermute | solution.py:42
  464.5 10.2 %collective-permute-done.34 = bf16[256,1536]{1,0:T(8,128)(2,1)} collective-permute-done((bf16[256,1536]{1,0:T(8,128)(2,1)}, bf16[256,1536]{1,0:T(8,128)(2,1)}, u32[]{:S(2)}, u32[]{:S(2)}) %collective-permute-start.34) | collective-permute-done | bytes 786464 | tf_op jit(solution)/shard_map/ppermute | solution.py:42
  477.2 14.2 %collective-permute-done.35 = bf16[256,1536]{1,0:T(8,128)(2,1)} collective-permute-done((bf16[256,1536]{1,0:T(8,128)(2,1)}, bf16[256,1536]{1,0:T(8,128)(2,1)}, u32[]{:S(2)}, u32[]{:S(2)}) %collective-permute-start.35) | collective-permute-done | bytes 786464 | tf_op jit(solution)/shard_map/ppermute | solution.py:42
  499.7 4.4 all-to-all-start.1
  504.1 4.4 collective-permute-done.38
  515.1 25.9 %collective-permute-start.45 = (bf16[48,1536]{1,0:T(8,128)(2,1)S(1)}, bf16[48,1536]{1,0:T(8,128)(2,1)S(1)}, u32[]{:S(2)}, u32[]{:S(2)}) collective-permute-start(bf16[48,1536]{1,0:T(8,128)(2,1)S(1)} %get-tuple-element.103), channel_id=1, source_target_pairs={{2,0},{5,1},{8,2},{11,3},{14,4},{17,5},{20,6},{23,7},{26,8},{29,9}... | collective-permute-start | bytes 442376 | tf_op jit(solution)/shard_map/ppermute | solution.py:642
  549.5 21.8 %reduce-scatter.5.cloned.1.call-done = bf16[1,448,1536]{2,1,0:T(8,128)(2,1)} async-done(((bf16[8,448,1536]{2,1,0:T(8,128)(2,1)}), bf16[1,448,1536]{2,1,0:T(8,128)(2,1)}) %reduce-scatter.5.cloned.1.call-update) | async-done | bytes 1376272 | tf_op jit(solution)/shard_map/reduce_scatter | solution.py:619
  (234 shorter events, 129.8 us)
Async XLA Ops:
  7.2 121.9 %all-gather.5.cloned.1.call-start = ((), (), s32[]{:S(2)}) async-start(), calls=%async_computation.6 | async-start | bytes 12386304 | tf_op jit(solution)/shard_map/all_gather | solution.py:417
  43.7 79.3 %all-to-all-start = ((bf16[32,48,216]{2,1,0:T(8,128)(2,1)}), bf16[32,48,216]{2,1,0:T(8,128)(2,1)S(1)}, u32[]{:S(2)}, u32[]{:S(2)}) async-start(bf16[32,48,216]{2,1,0:T(8,128)(2,1)} %shard_map.179), calls=%async_computation | async-start | bytes 1572864 | tf_op jit(solution)/shard_map/all_to_all | solution.py:380
  46.5 168.2 %all-gather.7.cloned.1.call-start = ((), (), s32[]{:S(2)}) async-start(), calls=%async_computation.7 | async-start | bytes 6193152 | tf_op jit(solution)/shard_map/all_gather | solution.py:454
  46.5 63.5 %collective-permute-start.11 = (bf16[208,1536]{1,0:T(8,128)(2,1)}, bf16[208,1536]{1,0:T(8,128)(2,1)S(1)}, u32[]{:S(2)}, u32[]{:S(2)}) collective-permute-start(bf16[208,1536]{1,0:T(8,128)(2,1)} %shard_map.177.refs_1_.refs_5_), channel_id=1, source_target_pairs={{0,4},{2,6},{4,0},{6,2},{1,5},{3,7},{5,1},{7,3},{8,12},{10,14},{12... | collective-permute-start | bytes 1916936 | tf_op jit(solution)/shard_map/ppermute | solution.py:42
  49.3 60.7 %collective-permute-start.10 = (bf16[208,1536]{1,0:T(8,128)(2,1)}, bf16[208,1536]{1,0:T(8,128)(2,1)S(1)}, u32[]{:S(2)}, u32[]{:S(2)}) collective-permute-start(bf16[208,1536]{1,0:T(8,128)(2,1)} %shard_map.177.refs_1_.refs_5_), channel_id=1, source_target_pairs={{0,2},{2,0},{4,6},{6,4},{1,3},{3,1},{5,7},{7,5},{8,10},{10,8},{12,... | collective-permute-start | bytes 1916936 | tf_op jit(solution)/shard_map/ppermute | solution.py:42
  51.7 61.7 %collective-permute-start.9 = (bf16[272,1536]{1,0:T(8,128)(2,1)}, bf16[272,1536]{1,0:T(8,128)(2,1)S(1)}, u32[]{:S(2)}, u32[]{:S(2)}) collective-permute-start(bf16[272,1536]{1,0:T(8,128)(2,1)} %shard_map.178.refs_0_), channel_id=1, source_target_pairs={{0,24},{8,16},{16,8},{24,0},{1,25},{9,17},{17,9},{25,1},{2,26},{10... | collective-permute-start | bytes 2506760 | tf_op jit(solution)/shard_map/ppermute | solution.py:42
  54.2 61.2 %collective-permute-start.8 = (bf16[272,1536]{1,0:T(8,128)(2,1)}, bf16[272,1536]{1,0:T(8,128)(2,1)S(1)}, u32[]{:S(2)}, u32[]{:S(2)}) collective-permute-start(bf16[272,1536]{1,0:T(8,128)(2,1)} %shard_map.178.refs_0_), channel_id=1, source_target_pairs={{0,16},{8,24},{16,0},{24,8},{1,17},{9,25},{17,1},{25,9},{2,18},{10... | collective-permute-start | bytes 2506760 | tf_op jit(solution)/shard_map/ppermute | solution.py:42
  55.2 67.8 %collective-permute-start.7 = (bf16[272,1536]{1,0:T(8,128)(2,1)}, bf16[272,1536]{1,0:T(8,128)(2,1)}, u32[]{:S(2)}, u32[]{:S(2)}) collective-permute-start(bf16[272,1536]{1,0:T(8,128)(2,1)} %shard_map.178.refs_0_), channel_id=1, source_target_pairs={{0,8},{8,0},{16,24},{24,16},{1,9},{9,1},{17,25},{25,17},{2,10},{10... | collective-permute-start | bytes 2506760 | tf_op jit(solution)/shard_map/ppermute | solution.py:42
  129.1 368.1 %reduce-scatter.3.cloned.1.call-start = ((), (), s32[]{:S(2)}) async-start(), calls=%async_computation.4 | async-start | bytes 6193152 | tf_op jit(solution)/shard_map/reduce_scatter | solution.py:552
  155.3 32.8 %collective-permute-start.15 = (bf16[256,1536]{1,0:T(8,128)(2,1)}, bf16[256,1536]{1,0:T(8,128)(2,1)S(1)}, u32[]{:S(2)}, u32[]{:S(2)}) collective-permute-start(bf16[256,1536]{1,0:T(8,128)(2,1)} %shard_map.183), channel_id=1, source_target_pairs={{0,8},{8,0},{16,24},{24,16},{1,9},{9,1},{17,25},{25,17},{2,10},{10... | collective-permute-start | bytes 2359304 | tf_op jit(solution)/shard_map/ppermute | solution.py:42
  156.4 31.7 %collective-permute-start.16 = (bf16[256,1536]{1,0:T(8,128)(2,1)}, bf16[256,1536]{1,0:T(8,128)(2,1)S(1)}, u32[]{:S(2)}, u32[]{:S(2)}) collective-permute-start(bf16[256,1536]{1,0:T(8,128)(2,1)} %get-tuple-element.53), channel_id=1, source_target_pairs={{0,16},{8,24},{16,0},{24,8},{1,17},{9,25},{17,1},{25,9},{2,18},{10... | collective-permute-start | bytes 2359304 | tf_op jit(solution)/shard_map/ppermute | solution.py:42
  157.4 48.2 %collective-permute-start.17 = (bf16[256,1536]{1,0:T(8,128)(2,1)S(1)}, bf16[256,1536]{1,0:T(8,128)(2,1)S(1)}, u32[]{:S(2)}, u32[]{:S(2)}) collective-permute-start(bf16[256,1536]{1,0:T(8,128)(2,1)S(1)} %copy-done.27), channel_id=1, source_target_pairs={{0,24},{8,16},{16,8},{24,0},{1,25},{9,17},{17,9},{25,1},{2,26},{10... | collective-permute-start | bytes 2359304 | tf_op jit(solution)/shard_map/ppermute | solution.py:42
  158.8 55.8 %collective-permute-start.21 = (bf16[256,1536]{1,0:T(8,128)(2,1)S(1)}, bf16[256,1536]{1,0:T(8,128)(2,1)}, u32[]{:S(2)}, u32[]{:S(2)}) collective-permute-start(bf16[256,1536]{1,0:T(8,128)(2,1)S(1)} %copy-done.4), channel_id=1, source_target_pairs={{0,2},{2,0},{4,6},{6,4},{1,3},{3,1},{5,7},{7,5},{8,10},{10,8},{12,... | collective-permute-start | bytes 2359304 | tf_op jit(solution)/shard_map/ppermute | solution.py:42
  174.4 35.7 %collective-permute-start.18 = (bf16[256,1536]{1,0:T(8,128)(2,1)S(1)}, bf16[256,1536]{1,0:T(8,128)(2,1)}, u32[]{:S(2)}, u32[]{:S(2)}) collective-permute-start(bf16[256,1536]{1,0:T(8,128)(2,1)S(1)} %copy-done.4), channel_id=1, source_target_pairs={{0,4},{2,6},{4,0},{6,2},{1,5},{3,7},{5,1},{7,3},{8,12},{10,14},{12... | collective-permute-start | bytes 2359304 | tf_op jit(solution)/shard_map/ppermute | solution.py:42
  212.5 34.2 %collective-permute-start.19 = (bf16[256,1536]{1,0:T(8,128)(2,1)}, bf16[256,1536]{1,0:T(8,128)(2,1)}, u32[]{:S(2)}, u32[]{:S(2)}) collective-permute-start(bf16[256,1536]{1,0:T(8,128)(2,1)} %shard_map.184.refs_0_), channel_id=1, source_target_pairs={{0,2},{2,0},{4,6},{6,4},{1,3},{3,1},{5,7},{7,5},{8,10},{10,8},{12,... | collective-permute-start | bytes 2359304 | tf_op jit(solution)/shard_map/ppermute | solution.py:42
  246.7 36.5 %collective-permute-start.22 = (bf16[256,1536]{1,0:T(8,128)(2,1)}, bf16[256,1536]{1,0:T(8,128)(2,1)S(1)}, u32[]{:S(2)}, u32[]{:S(2)}) collective-permute-start(bf16[256,1536]{1,0:T(8,128)(2,1)} %shard_map.187), channel_id=1, source_target_pairs={{0,4},{2,6},{4,0},{6,2},{1,5},{3,7},{5,1},{7,3},{8,12},{10,14},{12... | collective-permute-start | bytes 2359304 | tf_op jit(solution)/shard_map/ppermute | solution.py:42
  268.0 49.8 %collective-permute-start.23 = (bf16[256,1536]{1,0:T(8,128)(2,1)}, bf16[256,1536]{1,0:T(8,128)(2,1)S(1)}, u32[]{:S(2)}, u32[]{:S(2)}) collective-permute-start(bf16[256,1536]{1,0:T(8,128)(2,1)} %get-tuple-element.60), channel_id=1, source_target_pairs={{0,2},{2,0},{4,6},{6,4},{1,3},{3,1},{5,7},{7,5},{8,10},{10,8},{12,... | collective-permute-start | bytes 2359304 | tf_op jit(solution)/shard_map/ppermute | solution.py:42
  269.7 48.1 %collective-permute-start.25 = (bf16[256,1536]{1,0:T(8,128)(2,1)}, bf16[256,1536]{1,0:T(8,128)(2,1)}, u32[]{:S(2)}, u32[]{:S(2)}) collective-permute-start(bf16[256,1536]{1,0:T(8,128)(2,1)} %get-tuple-element.62), channel_id=1, source_target_pairs={{0,6},{2,4},{4,2},{6,0},{1,7},{3,5},{5,3},{7,1},{8,14},{10,12},{12... | collective-permute-start | bytes 2359304 | tf_op jit(solution)/shard_map/ppermute | solution.py:42
  304.8 45.9 %collective-permute-start.24 = (bf16[256,1536]{1,0:T(8,128)(2,1)}, bf16[256,1536]{1,0:T(8,128)(2,1)}, u32[]{:S(2)}, u32[]{:S(2)}) collective-permute-start(bf16[256,1536]{1,0:T(8,128)(2,1)} %get-tuple-element.61), channel_id=1, source_target_pairs={{0,4},{2,6},{4,0},{6,2},{1,5},{3,7},{5,1},{7,3},{8,12},{10,14},{12... | collective-permute-start | bytes 2359304 | tf_op jit(solution)/shard_map/ppermute | solution.py:42
  356.7 33.2 %collective-permute-start.28 = (bf16[256,1536]{1,0:T(8,128)(2,1)}, bf16[256,1536]{1,0:T(8,128)(2,1)}, u32[]{:S(2)}, u32[]{:S(2)}) collective-permute-start(bf16[256,1536]{1,0:T(8,128)(2,1)} %get-tuple-element.96.refs_0_.refs_4_), channel_id=1, source_target_pairs={{0,24},{8,16},{16,8},{24,0},{1,25},{9,17},{17,9},{25,1},{2,26},{10... | collective-permute-start | bytes 2359304 | tf_op jit(solution)/shard_map/ppermute | solution.py:42
  357.1 36.4 %collective-permute-start.27 = (bf16[256,1536]{1,0:T(8,128)(2,1)}, bf16[256,1536]{1,0:T(8,128)(2,1)}, u32[]{:S(2)}, u32[]{:S(2)}) collective-permute-start(bf16[256,1536]{1,0:T(8,128)(2,1)} %get-tuple-element.96.refs_0_.refs_4_), channel_id=1, source_target_pairs={{0,16},{8,24},{16,0},{24,8},{1,17},{9,25},{17,1},{25,9},{2,18},{10... | collective-permute-start | bytes 2359304 | tf_op jit(solution)/shard_map/ppermute | solution.py:42
  358.7 34.7 %collective-permute-start.26 = (bf16[256,1536]{1,0:T(8,128)(2,1)}, bf16[256,1536]{1,0:T(8,128)(2,1)}, u32[]{:S(2)}, u32[]{:S(2)}) collective-permute-start(bf16[256,1536]{1,0:T(8,128)(2,1)} %get-tuple-element.96.refs_0_.refs_4_), channel_id=1, source_target_pairs={{0,8},{8,0},{16,24},{24,16},{1,9},{9,1},{17,25},{25,17},{2,10},{10... | collective-permute-start | bytes 2359304 | tf_op jit(solution)/shard_map/ppermute | solution.py:42
  360.2 33.8 %collective-permute-start.29 = (bf16[256,1536]{1,0:T(8,128)(2,1)}, bf16[256,1536]{1,0:T(8,128)(2,1)S(1)}, u32[]{:S(2)}, u32[]{:S(2)}) collective-permute-start(bf16[256,1536]{1,0:T(8,128)(2,1)} %shard_map.193), channel_id=1, source_target_pairs={{0,2},{2,0},{4,6},{6,4},{1,3},{3,1},{5,7},{7,5},{8,10},{10,8},{12,... | collective-permute-start | bytes 2359304 | tf_op jit(solution)/shard_map/ppermute | solution.py:42
  360.2 36.6 %collective-permute-start.30 = (bf16[256,1536]{1,0:T(8,128)(2,1)}, bf16[256,1536]{1,0:T(8,128)(2,1)S(1)}, u32[]{:S(2)}, u32[]{:S(2)}) collective-permute-start(bf16[256,1536]{1,0:T(8,128)(2,1)} %shard_map.194), channel_id=1, source_target_pairs={{0,4},{2,6},{4,0},{6,2},{1,5},{3,7},{5,1},{7,3},{8,12},{10,14},{12... | collective-permute-start | bytes 2359304 | tf_op jit(solution)/shard_map/ppermute | solution.py:42
  404.3 167.0 %reduce-scatter.5.cloned.1.call-start = ((), (), s32[]{:S(2)}) async-start(), calls=%async_computation.5 | async-start | bytes 12386304 | tf_op jit(solution)/shard_map/reduce_scatter | solution.py:619
  447.5 43.9 %collective-permute-start.35 = (bf16[256,1536]{1,0:T(8,128)(2,1)}, bf16[256,1536]{1,0:T(8,128)(2,1)}, u32[]{:S(2)}, u32[]{:S(2)}) collective-permute-start(bf16[256,1536]{1,0:T(8,128)(2,1)} %shard_map.202), channel_id=1, source_target_pairs={{0,16},{8,24},{16,0},{24,8},{1,17},{9,25},{17,1},{25,9},{2,18},{10... | collective-permute-start | bytes 2359304 | tf_op jit(solution)/shard_map/ppermute | solution.py:42
  448.1 43.3 %collective-permute-start.36 = (bf16[256,1536]{1,0:T(8,128)(2,1)}, bf16[256,1536]{1,0:T(8,128)(2,1)}, u32[]{:S(2)}, u32[]{:S(2)}) collective-permute-start(bf16[256,1536]{1,0:T(8,128)(2,1)} %shard_map.203), channel_id=1, source_target_pairs={{0,24},{8,16},{16,8},{24,0},{1,25},{9,17},{17,9},{25,1},{2,26},{10... | collective-permute-start | bytes 2359304 | tf_op jit(solution)/shard_map/ppermute | solution.py:42
  454.3 49.8 %collective-permute-start.37 = (bf16[208,1536]{1,0:T(8,128)(2,1)}, bf16[208,1536]{1,0:T(8,128)(2,1)S(1)}, u32[]{:S(2)}, u32[]{:S(2)}) collective-permute-start(bf16[208,1536]{1,0:T(8,128)(2,1)} %get-tuple-element.89), channel_id=1, source_target_pairs={{0,2},{2,0},{4,6},{6,4},{1,3},{3,1},{5,7},{7,5},{8,10},{10,8},{12,... | collective-permute-start | bytes 1916936 | tf_op jit(solution)/shard_map/ppermute | solution.py:42
  463.3 45.1 %collective-permute-start.38 = (bf16[208,1536]{1,0:T(8,128)(2,1)}, bf16[208,1536]{1,0:T(8,128)(2,1)S(1)}, u32[]{:S(2)}, u32[]{:S(2)}) collective-permute-start(bf16[208,1536]{1,0:T(8,128)(2,1)} %get-tuple-element.90), channel_id=1, source_target_pairs={{0,4},{2,6},{4,0},{6,2},{1,5},{3,7},{5,1},{7,3},{8,12},{10,14},{12... | collective-permute-start | bytes 1916936 | tf_op jit(solution)/shard_map/ppermute | solution.py:42
  474.6 33.8 %collective-permute-start.39 = (bf16[208,1536]{1,0:T(8,128)(2,1)}, bf16[208,1536]{1,0:T(8,128)(2,1)S(1)}, u32[]{:S(2)}, u32[]{:S(2)}) collective-permute-start(bf16[208,1536]{1,0:T(8,128)(2,1)} %get-tuple-element.91), channel_id=1, source_target_pairs={{0,6},{2,4},{4,2},{6,0},{1,7},{3,5},{5,3},{7,1},{8,14},{10,12},{12... | collective-permute-start | bytes 1916936 | tf_op jit(solution)/shard_map/ppermute | solution.py:42
  499.7 46.6 %all-to-all-start.1 = ((bf16[32,48,216]{2,1,0:T(8,128)(2,1)}), bf16[32,48,216]{2,1,0:T(8,128)(2,1)S(1)}, u32[]{:S(2)}, u32[]{:S(2)}) async-start(bf16[32,48,216]{2,1,0:T(8,128)(2,1)} %bitcast.44.refs_1_), calls=%async_computation.3 | async-start | bytes 1572864 | tf_op jit(solution)/shard_map/all_to_all | solution.py:625
  510.3 30.8 %collective-permute-start.42 = (bf16[64,384]{1,0:T(8,128)(2,1)S(1)}, bf16[64,384]{1,0:T(8,128)(2,1)S(1)}, u32[]{:S(2)}, u32[]{:S(2)}) collective-permute-start(bf16[64,384]{1,0:T(8,128)(2,1)S(1)} %get-tuple-element.118), channel_id=1, source_target_pairs={{0,8},{8,0},{16,24},{24,16},{1,9},{9,1},{17,25},{25,17},{2,10},{10... | collective-permute-start | bytes 147464 | tf_op jit(solution)/shard_map/ppermute | solution.py:42
  (48 other events, 608.3 us)
Sparse Core Ops, SparseCore 0:
  10.0 115.3 all-gather.4
  129.3 56.0 all-gather.6
  404.5 62.4 reduce-scatter.2
  470.8 100.4 reduce-scatter.4

commit v4 on v3

--- a/solution.py
+++ b/solution.py
@@ -179,9 +179,9 @@
         out_ref[...] = (acc_ref[at] + part).astype(bf16)
 
 
-def feed_forward(n, *refs):
+def feed_forward(n, parts, *refs):
     u_refs, (gate_ref, up_ref, dh_ref), refs = refs[:n], refs[n : n + 3], refs[n + 3 :]
-    (hid_ref, dg_ref, dup_ref), du_refs, acc_ref = refs[:3], refs[3 : 3 + n], refs[3 + n]
+    (hid_ref, dg_ref, dup_ref), du_refs, acc_ref = refs[:3], refs[3:-1], refs[-1]
     w_gate, w_up = merged(gate_ref), merged(up_ref)
     rows = u_refs[0].shape[0]
     for r in range(n):
@@ -196,7 +196,11 @@
         dup = (dh * silu).astype(bf16)
         dg_ref[0, at] = dgate
         dup_ref[0, at] = dup
-        add_up(acc_ref, at, dot(dgate, w_gate) + dot(dup, w_up), du_refs[r])
+        du = dot(dgate, w_gate) + dot(dup, w_up)
+        ends = [0, rows // 8, rows] if parts == 2 else [0, rows]
+        for h in range(parts):
+            here = slice(r * rows + ends[h], r * rows + ends[h + 1])
+            add_up(acc_ref, here, du[ends[h] : ends[h + 1]], du_refs[r * parts + h])
 
 
 def feed_forward_out(line, *refs):
@@ -482,10 +486,11 @@
     done, du_terms = [None, None], [None] * line
     for odd in (1, 0):
         made = kernel_call(
-            functools.partial(feed_forward, line // 2),
+            functools.partial(feed_forward, line // 2, 2 - odd),
             (2,),
             slot_specs[: line // 2] + [third(0), third(1), per_half],
-            [(half, bf16, per_half)] * 3 + flat(rows, line // 2),
+            [(half, bf16, per_half)] * 3
+            + (flat(rows, 1) if odd else flat(rows // 8, 1) + flat(rows - rows // 8, 1)) * (line // 2),
             [pltpu.VMEM((half_rows, width), f32)],
             2 * unit_flops,
             *u_slots[odd::2],
@@ -495,8 +500,14 @@
             waits=[] if odd else [done[1][0]],
         )
         done[odd] = made[:3]
-        du_terms[odd::2] = made[3:]
-    du_terms = scatter(du_terms, "line")
+        if odd:
+            du_terms[1::2] = [flip(d, "line", 2 * n + 1) for n, d in enumerate(made[3:])]
+            continue
+        du_own, du_parts = jnp.concatenate(made[3:5], 0), []
+        for r in range(2, line, 2):
+            du_parts += [flip(d, "line", r) for d in made[3 + r : 5 + r]]
+            du_terms[r] = jnp.concatenate(du_parts[-2:], 0)
+    du_terms[0] = du_own
     ff_grads = lambda kinds, *args: kernel_call(
         functools.partial(feed_forward_grads, line, kinds),
         (2,),
@@ -512,8 +523,8 @@
         kinds * unit_flops,
         *args,
     )[0]
+    g_ff = ff_grads(2, *u_slots, *done[0][1:], *done[1][1:])
     g_down = ff_grads(1, *cot_slots, done[0][0], done[1][0])
-    g_ff = ff_grads(2, *u_slots, *done[0][1:], *done[1][1:])
     part_out = kernel_call(
         functools.partial(feed_forward_out, line),
         (2,),
@@ -525,8 +536,10 @@
         done[1][0],
         full_down,
     )
+    g_down = lax.psum_scatter(tie(g_down, *du_terms[1::2], *du_parts[:1]), ("fsdp", "core"), scatter_dimension=0)
     dunit = total([tie(du_terms[0], part_out[0])] + du_terms[1:])
-    out_terms = scatter([part_out[0]] + [tie(p, *du_terms[1:]) for p in part_out[1:]], "line")
+    out_terms = [tie(p, *du_terms[1::2], *du_parts) for p in part_out[1:]]
+    out_terms = scatter([part_out[0]] + out_terms, "line")
 
     grad_two = jnp.sum(dunit * unit_two, axis=0)
     dnorm_two = dunit * small[1]
@@ -549,9 +562,10 @@
         conv,
         waits=out_terms[1:-1] + [g_ff],
     )
-    g_down = lax.psum_scatter(tie(g_down, dconv), ("fsdp", "core"), scatter_dimension=0)
     block_out = second + total([tie(out_terms[0], dconv)] + out_terms[1:])
     block_out = block_out.astype(bf16).reshape(seqs, group, width)
+    g_ff = lax.psum_scatter(tie(g_ff, dconv), ("fsdp", "core"), scatter_dimension=0)
+    g_down = g_down[:hid].T.reshape(count, feats, hid)
     ahead = dconv.reshape(lanes, seqs, group, mine)[:, :, :2]
     ahead = lax.ppermute(ahead, ("line", "core"), back).reshape(lanes, 2 * seqs, mine)
     g_rows = 4 * feats + 16
@@ -601,6 +615,7 @@
         normed_a,
         branch_y,
         places,
+        waits=[g_down],
     )
     if not in_place:
         g_mixer = jnp.concatenate([g_own, g_other], 0)[places[:-1]]
@@ -613,16 +628,13 @@
         [],
         1,
         g_own,
-        flip(g_other, "core", 1),
-    )
-    g_ff = tie(g_ff, g_other, out_terms[-1])
-    g_ff = lax.psum_scatter(g_ff, ("fsdp", "core"), scatter_dimension=0)
+        flip(tie(g_other, out_terms[-1]), "core", 1),
+    )
+    g_down = lax.all_to_all(tie(g_down, g_terms[0]), every, 0, 0, tiled=True)
     dnormed = [dnormed[0]] + [tie(d, g_terms[0]) for d in dnormed[1:]]
     g_terms = scatter(g_terms, "line")
-    da_terms = scatter(dnormed, "fsdp")
-    g_down = g_down[:hid].T.reshape(count, feats, hid)
-    ready = g_down
-    g_down = lax.all_to_all(g_down, every, 0, 0, tiled=True)
+    da_terms = [flip(dnormed[r], "fsdp", r) for r in reversed(range(1, lanes))][::-1]
+    da_terms = [dnormed[0]] + da_terms
     dnormed = total(da_terms)
     scale_one = lax.rsqrt(jnp.mean(hidden_in * hidden_in, axis=-1, keepdims=True) + epsilon)
     unit_one = hidden_in * scale_one
@@ -632,7 +644,7 @@
     )
     grad_tokens = dinput.astype(bf16).reshape(seqs, group, width)
 
-    g_mixer = total([tie(g_terms[0], ready)] + g_terms[1:]).astype(bf16)
+    g_mixer = total(g_terms).astype(bf16)
     g_in = g_mixer[: 3 * feats].reshape(3, feats, width)
     homes = [[(d, k) for k, d in route] for route in routes]
     parts = []

time: 587 us -> 579 us (0.986)
  starting transfers between devices: 121 us -> 105 us
    ppermute x38 -> x39, waiting for transfers between devices: 200 us -> 227 us  [flip(): return lax.ppermute(block, axis, [(i, i ^ bits) for i in range(size)])]
    reduce_scatter x2, waiting for transfers between devices: 21.8 us -> 0.01 us  [the longest x1 0.01 us: on_device(): lax.psum_scatter(tie(g_down, *du_terms[1::2], *du_parts[:1]), ('fsdp', 'c...]
    ppermute x3, starting transfers between devices: 26.9 us -> 15.2 us  [on_device(): parts.append(lax.ppermute(block, every, homes[j]))]
    ppermute x38 -> x39, starting transfers between devices: 73.7 us -> 70.4 us  [flip(): return lax.ppermute(block, axis, [(i, i ^ bits) for i in range(size)])]
    unnamed x60 -> x82, local copies, waits for them, and re-layouts: 10 us -> 12.5 us
  transfers between devices with their start and end apart: 52 -> 53, of which waited for: 24 -> 22; matrix products, arithmetic and copies ran while one was open for 7% -> 9% of each run, Pallas kernels for 25% -> 27%
where the time goes in v4:
time: 579 us; the launch traced here: 571 us
  waiting for transfers between devices  235 us (41%)
  Pallas kernels  152 us (26%)
  starting transfers between devices  105 us (18%)
  local copies, waits for them, and re-layouts  33.5 us (6%)
  other arithmetic  30.8 us (5%)
  between operations  15.2 us (3%)
    ppermute x39, waiting for transfers between devices, flip(): return lax.ppermute(block, axis, [(i, i ^ bits) for i in range(size)])  227 us
    pallas_call x11, Pallas kernels, kernel_call(): pl.pallas_call(lambda *refs: body(*refs[:held], *refs[held + len(waits):]...  152 us
    ppermute x39, starting transfers between devices, flip(): return lax.ppermute(block, axis, [(i, i ^ bits) for i in range(size)])  70.4 us
    ppermute x3, starting transfers between devices, on_device(): parts.append(lax.ppermute(block, every, homes[j]))  15.2 us
    unnamed x82, local copies, waits for them, and re-layouts  12.5 us
  transfers between devices with their start and end apart: 53, of which 22 were waited for; matrix products, arithmetic and copies ran while one was open for 9% of the time, Pallas kernels for 27%

profile of v4, /device:TPU:0, one launch (start us, length us, event | category | flops | bytes accessed | tf_op | source)
XLA Modules:
  0.0 571.1 jit_solution(10604345912905624675)
XLA Ops:
  17.5 8.0 %collective-permute-start.3 = (bf16[48,1536]{1,0:T(8,128)(2,1)S(1)}, bf16[48,1536]{1,0:T(8,128)(2,1)S(1)}, u32[]{:S(2)}, u32[]{:S(2)}) collective-permute-start(bf16[48,1536]{1,0:T(8,128)(2,1)S(1)} %get-tuple-element.114), channel_id=1, source_target_pairs={{0,2},{1,5},{2,8},{3,11},{4,14},{5,17},{6,20},{7,23},{8,26},{9,29}... | collective-permute-start | bytes 442376 | tf_op jit(solution)/shard_map/ppermute | solution.py:367
  26.3 5.8 %collective-permute-done.3 = bf16[48,1536]{1,0:T(8,128)(2,1)S(1)} collective-permute-done((bf16[48,1536]{1,0:T(8,128)(2,1)S(1)}, bf16[48,1536]{1,0:T(8,128)(2,1)S(1)}, u32[]{:S(2)}, u32[]{:S(2)}) %collective-permute-start.3) | collective-permute-done | bytes 147488 | tf_op jit(solution)/shard_map/ppermute | solution.py:367
  35.3 4.7 collective-permute-start.12
  55.2 54.8 %collective-permute-done.11.refs_7_.refs_2_ = bf16[208,1536]{1,0:T(8,128)(2,1)S(1)} collective-permute-done((bf16[208,1536]{1,0:T(8,128)(2,1)}, bf16[208,1536]{1,0:T(8,128)(2,1)S(1)}, u32[]{:S(2)}, u32[]{:S(2)}) %collective-permute-start.11) | collective-permute-done | bytes 639008 | tf_op jit(solution)/shard_map/ppermute | solution.py:42
  116.2 6.8 %collective-permute-done.7.refs_1_ = bf16[272,1536]{1,0:T(8,128)(2,1)} collective-permute-done((bf16[272,1536]{1,0:T(8,128)(2,1)}, bf16[272,1536]{1,0:T(8,128)(2,1)}, u32[]{:S(2)}, u32[]{:S(2)}) %collective-permute-start.7) | collective-permute-done | bytes 835616 | tf_op jit(solution)/shard_map/ppermute | solution.py:42
  135.2 19.2 %shard_map.181 = (bf16[256,1536]{1,0:T(8,128)(2,1)}, bf16[256,1536]{1,0:T(8,128)(2,1)}, bf16[256,1536]{1,0:T(8,128)(2,1)}, bf16[256,1536]{1,0:T(8,128)(2,1)}, bf...) custom-call(bf16[272,1536]{1,0:T(8,128)(2,1)} %shard_map.178.refs_0_, ...), custom_call_target="tpu_custom_call" | custom-call | flops 14495514624 | bytes 27476004 | tf_op jit(solution)/shard_map/pallas_call | solution.py:82
  158.8 15.6 %collective-permute-start.21 = (bf16[256,1536]{1,0:T(8,128)(2,1)S(1)}, bf16[256,1536]{1,0:T(8,128)(2,1)}, u32[]{:S(2)}, u32[]{:S(2)}) collective-permute-start(bf16[256,1536]{1,0:T(8,128)(2,1)S(1)} %copy-done.11), channel_id=1, source_target_pairs={{0,2},{2,0},{4,6},{6,4},{1,3},{3,1},{5,7},{7,5},{8,10},{10,8},{12,... | collective-permute-start | bytes 2359304 | tf_op jit(solution)/shard_map/ppermute | solution.py:42
  176.2 11.9 %collective-permute-done.15 = bf16[256,1536]{1,0:T(8,128)(2,1)S(1)} collective-permute-done((bf16[256,1536]{1,0:T(8,128)(2,1)}, bf16[256,1536]{1,0:T(8,128)(2,1)S(1)}, u32[]{:S(2)}, u32[]{:S(2)}) %collective-permute-start.15) | collective-permute-done | bytes 786464 | tf_op jit(solution)/shard_map/ppermute | solution.py:42
  188.1 17.4 %collective-permute-done.17 = bf16[256,1536]{1,0:T(8,128)(2,1)S(1)} collective-permute-done((bf16[256,1536]{1,0:T(8,128)(2,1)S(1)}, bf16[256,1536]{1,0:T(8,128)(2,1)S(1)}, u32[]{:S(2)}, u32[]{:S(2)}) %collective-permute-start.17) | collective-permute-done | bytes 786464 | tf_op jit(solution)/shard_map/ppermute | solution.py:42
  214.6 7.1 %shard_map.186.refs_3_.refs_4_ = f32[2,512,896]{2,1,0:T(8,128)} custom-call(bf16[256,1536]{1,0:T(8,128)(2,1)} %collective-permute-done.21.refs_0_.refs_1_, bf16[256,1536]{1,0:T(8,128)(2,1)} %copy-done.19, bf16[8,224,1536]{2,1,0:T(8,128)(2,1)} %bitcast.175), custom_call_target="tpu_custom_call" | custom-call | flops 2818572288 | bytes 10747904 | tf_op jit(solution)/shard_map/pallas_call | solution.py:82
  221.7 11.0 %collective-permute-done.20.refs_2_.refs_1_.refs_3_ = bf16[256,1536]{1,0:T(8,128)(2,1)} collective-permute-done((bf16[256,1536]{1,0:T(8,128)(2,1)}, bf16[256,1536]{1,0:T(8,128)(2,1)}, u32[]{:S(2)}, u32[]{:S(2)}) %collective-permute-start.20) | collective-permute-done | bytes 786464 | tf_op jit(solution)/shard_map/ppermute | solution.py:42
  232.7 14.0 %collective-permute-done.19.refs_1_.refs_0_ = bf16[256,1536]{1,0:T(8,128)(2,1)} collective-permute-done((bf16[256,1536]{1,0:T(8,128)(2,1)}, bf16[256,1536]{1,0:T(8,128)(2,1)}, u32[]{:S(2)}, u32[]{:S(2)}) %collective-permute-start.19) | collective-permute-done | bytes 786464 | tf_op jit(solution)/shard_map/ppermute | solution.py:42
  247.3 20.7 %shard_map.189 = (bf16[2,512,896]{2,1,0:T(8,128)(2,1)}, bf16[2,512,896]{2,1,0:T(8,128)(2,1)}, bf16[2,512,896]{2,1,0:T(8,128)(2,1)}, bf16[256,1536]{1,0:T(8,128)(2,1)}, bf16[256,1536]{1,0:T(8,128)(2,1)}) custom-call(bf16[256,1536]{1,0:T(8,128)(2,1)} %collective-permute-done.19.refs_1_.refs_0_, ...), custom_call_target="tpu_custom_call" | custom-call | flops 11274289152 | bytes 34340864 | tf_op jit(solution)/shard_map/pallas_call | solution.py:82
  271.8 7.2 %shard_map.188.refs_4_ = f32[2,512,896]{2,1,0:T(8,128)} custom-call(bf16[256,1536]{1,0:T(8,128)(2,1)} %shard_map.182.refs_0_, bf16[256,1536]{1,0:T(8,128)(2,1)} %collective-permute-done.18.refs_1_.refs_2_, bf16[8,224,1536]{2,1,0:T(8,128)(2,1)} %bitcast.176), custom_call_target="tpu_custom_call" | custom-call | flops 2818572288 | bytes 10747904 | tf_op jit(solution)/shard_map/pallas_call | solution.py:82
  279.1 4.2 collective-permute-done.22.refs_1_.refs_2_
  284.1 20.7 %shard_map.190 = (bf16[2,512,896]{2,1,0:T(8,128)(2,1)}, bf16[2,512,896]{2,1,0:T(8,128)(2,1)}, bf16[2,512,896]{2,1,0:T(8,128)(2,1)}, bf16[32,1536]{1,0:T(8,128)(2...) custom-call(bf16[256,1536]{1,0:T(8,128)(2,1)} %shard_map.184.refs_0_, ...), custom_call_target="tpu_custom_call" | custom-call | flops 11274289152 | bytes 34340864 | tf_op jit(solution)/shard_map/pallas_call | solution.py:82
  305.0 10.3 %shard_map.199.refs_0_ = bf16[8,224,1536]{2,1,0:T(8,128)(2,1)} custom-call(bf16[256,1536]{1,0:T(8,128)(2,1)} %shard_map.182.refs_0_, bf16[256,1536]{1,0:T(8,128)(2,1)} %collective-permute-done.21.refs_0_.refs_1_, bf16[256,1536]{1,0:T(8,128)(2,1)} %collective-permute-done.18.refs_1_.refs_2_, bf16[256,1536]{1,0:T(8,128)(2,1)} %copy-done.19, ...), custom_call_target="tpu_custom_call" | custom-call | flops 5637144576 | bytes 12320768 | tf_op jit(solution)/shard_map/pallas_call | solution.py:82
  316.8 4.3 collective-permute-done.24.refs_3_
  323.8 12.9 %shard_map.191 = (bf16[256,1536]{1,0:T(8,128)(2,1)}, bf16[256,1536]{1,0:T(8,128)(2,1)}, bf16[256,1536]{1,0:T(8,128)(2,1)}, bf16[256,1536]{1,0:T(8,128)(2,1)}) custom-call(bf16[2,512,896]{2,1,0:T(8,128)(2,1)} %get-tuple-element.59.refs_0_.refs_4_, bf16[2,512,896]{2,1,0:T(8,128)(2,1)} %get-tuple-element.58.refs_5_.refs_1_, bf16[8,224,1536]{2,1,0:T(8,128)(2,1)} %bitcast.177), custom_call_target="tpu_custom_call" | custom-call | flops 5637144576 | bytes 12320768 | tf_op jit(solution)/shard_map/pallas_call | solution.py:82
  336.7 16.4 %collective-permute-done.25.refs_4_ = bf16[224,1536]{1,0:T(8,128)(2,1)} collective-permute-done((bf16[224,1536]{1,0:T(8,128)(2,1)}, bf16[224,1536]{1,0:T(8,128)(2,1)}, u32[]{:S(2)}, u32[]{:S(2)}) %collective-permute-start.25) | collective-permute-done | bytes 688160 | tf_op jit(solution)/shard_map/ppermute | solution.py:42
  362.9 17.7 %shard_map.195.refs_9_.refs_0_ = bf16[8,448,1536]{2,1,0:T(8,128)(2,1)} custom-call(bf16[256,1536]{1,0:T(8,128)(2,1)} %shard_map.184.refs_0_, bf16[256,1536]{1,0:T(8,128)(2,1)} %collective-permute-done.19.refs_1_.refs_0_, bf16[256,1536]{1,0:T(8,128)(2,1)} %copy-done.37, bf16[256,1536]{1,0:T(8,128)(2,1)} %collective-permute-done.20.refs_2_.refs_1_.refs_3_, ...), custom_call_target="tpu_custom_call" | custom-call | flops 11274289152 | bytes 21495808 | tf_op jit(solution)/shard_map/pallas_call | solution.py:82
  380.6 20.7 %collective-permute-done.28.refs_2_.refs_6_ = bf16[256,1536]{1,0:T(8,128)(2,1)} collective-permute-done((bf16[256,1536]{1,0:T(8,128)(2,1)}, bf16[256,1536]{1,0:T(8,128)(2,1)}, u32[]{:S(2)}, u32[]{:S(2)}) %collective-permute-start.28) | collective-permute-done | bytes 786464 | tf_op jit(solution)/shard_map/ppermute | solution.py:42
  402.4 6.6 %shard_map.196 = (f32[4,256,384]{2,1,0:T(8,128)}, bf16[4,256,384]{2,1,0:T(8,128)(2,1)}) custom-call(bf16[256,1536]{1,0:T(8,128)(2,1)} %fusion.38.refs_0_.refs_4_, bf16[256,1536]{1,0:T(8,128)(2,1)} %collective-permute-done.27.refs_1_.refs_5_, bf16[256,1536]{1,0:T(8,128)(2,1)} %collective-permute-done.28.refs_2_.refs_6_, ...), custom_call_target="tpu_custom_call" | custom-call | flops 1207959552 | bytes 9830400 | tf_op jit(solution)/shard_map/pallas_call | solution.py:82
  420.8 25.3 %shard_map.201 = (bf16[256,1536]{1,0:T(8,128)(2,1)}, bf16[256,1536]{1,0:T(8,128)(2,1)}, bf16[256,1536]{1,0:T(8,128)(2,1)}, bf16[256,1536]{1,0:T(8,128)(2,1)}, bf...) custom-call(bf16[272,1536]{1,0:T(8,128)(2,1)} %shard_map.178.refs_0_, ...), custom_call_target="tpu_custom_call" | custom-call | flops 8455716864 | bytes 28592676 | tf_op jit(solution)/shard_map/pallas_call | solution.py:82
  447.2 4.8 collective-permute-done.34.refs_1_
  453.5 4.1 shard_map.203
  457.6 4.7 collective-permute-start.38
  471.7 19.0 %collective-permute-done.38 = bf16[208,1536]{1,0:T(8,128)(2,1)} collective-permute-done((bf16[208,1536]{1,0:T(8,128)(2,1)}, bf16[208,1536]{1,0:T(8,128)(2,1)}, u32[]{:S(2)}, u32[]{:S(2)}) %collective-permute-start.38) | collective-permute-done | bytes 639008 | tf_op jit(solution)/shard_map/ppermute | solution.py:42
  492.1 18.7 %collective-permute-done.39 = bf16[208,1536]{1,0:T(8,128)(2,1)} collective-permute-done((bf16[208,1536]{1,0:T(8,128)(2,1)}, bf16[208,1536]{1,0:T(8,128)(2,1)}, u32[]{:S(2)}, u32[]{:S(2)}) %collective-permute-start.39) | collective-permute-done | bytes 639008 | tf_op jit(solution)/shard_map/ppermute | solution.py:42
  515.2 12.1 %collective-permute-done.43 = bf16[64,384]{1,0:T(8,128)(2,1)S(1)} collective-permute-done((bf16[64,384]{1,0:T(8,128)(2,1)S(1)}, bf16[64,384]{1,0:T(8,128)(2,1)S(1)}, u32[]{:S(2)}, u32[]{:S(2)}) %collective-permute-start.43) | collective-permute-done | bytes 49184 | tf_op jit(solution)/shard_map/ppermute | solution.py:42
  532.3 14.2 %collective-permute-start.46 = (bf16[48,1536]{1,0:T(8,128)(2,1)S(1)}, bf16[48,1536]{1,0:T(8,128)(2,1)S(1)}, u32[]{:S(2)}, u32[]{:S(2)}) collective-permute-start(bf16[48,1536]{1,0:T(8,128)(2,1)S(1)} %get-tuple-element.108), channel_id=1, source_target_pairs={{2,0},{5,1},{8,2},{11,3},{14,4},{17,5},{20,6},{23,7},{26,8},{29,9}... | collective-permute-start | bytes 442376 | tf_op jit(solution)/shard_map/ppermute | solution.py:654
  552.0 4.6 fusion.8
  (259 shorter events, 130.4 us)
Async XLA Ops:
  7.2 121.9 %all-gather.5.cloned.1.call-start = ((), (), s32[]{:S(2)}) async-start(), calls=%async_computation.6 | async-start | bytes 12386304 | tf_op jit(solution)/shard_map/all_gather | solution.py:421
  43.7 79.3 %all-to-all-start = ((bf16[32,48,216]{2,1,0:T(8,128)(2,1)}), bf16[32,48,216]{2,1,0:T(8,128)(2,1)S(1)}, u32[]{:S(2)}, u32[]{:S(2)}) async-start(bf16[32,48,216]{2,1,0:T(8,128)(2,1)} %shard_map.179), calls=%async_computation | async-start | bytes 1572864 | tf_op jit(solution)/shard_map/all_to_all | solution.py:384
  46.5 168.2 %all-gather.7.cloned.1.call-start = ((), (), s32[]{:S(2)}) async-start(), calls=%async_computation.7 | async-start | bytes 6193152 | tf_op jit(solution)/shard_map/all_gather | solution.py:458
  46.5 63.5 %collective-permute-start.11 = (bf16[208,1536]{1,0:T(8,128)(2,1)}, bf16[208,1536]{1,0:T(8,128)(2,1)S(1)}, u32[]{:S(2)}, u32[]{:S(2)}) collective-permute-start(bf16[208,1536]{1,0:T(8,128)(2,1)} %shard_map.177.refs_1_.refs_5_), channel_id=1, source_target_pairs={{0,4},{2,6},{4,0},{6,2},{1,5},{3,7},{5,1},{7,3},{8,12},{10,14},{12... | collective-permute-start | bytes 1916936 | tf_op jit(solution)/shard_map/ppermute | solution.py:42
  49.2 60.7 %collective-permute-start.10 = (bf16[208,1536]{1,0:T(8,128)(2,1)}, bf16[208,1536]{1,0:T(8,128)(2,1)S(1)}, u32[]{:S(2)}, u32[]{:S(2)}) collective-permute-start(bf16[208,1536]{1,0:T(8,128)(2,1)} %shard_map.177.refs_1_.refs_5_), channel_id=1, source_target_pairs={{0,2},{2,0},{4,6},{6,4},{1,3},{3,1},{5,7},{7,5},{8,10},{10,8},{12,... | collective-permute-start | bytes 1916936 | tf_op jit(solution)/shard_map/ppermute | solution.py:42
  51.7 61.6 %collective-permute-start.9 = (bf16[272,1536]{1,0:T(8,128)(2,1)}, bf16[272,1536]{1,0:T(8,128)(2,1)S(1)}, u32[]{:S(2)}, u32[]{:S(2)}) collective-permute-start(bf16[272,1536]{1,0:T(8,128)(2,1)} %shard_map.178.refs_0_), channel_id=1, source_target_pairs={{0,24},{8,16},{16,8},{24,0},{1,25},{9,17},{17,9},{25,1},{2,26},{10... | collective-permute-start | bytes 2506760 | tf_op jit(solution)/shard_map/ppermute | solution.py:42
  54.1 61.2 %collective-permute-start.8 = (bf16[272,1536]{1,0:T(8,128)(2,1)}, bf16[272,1536]{1,0:T(8,128)(2,1)S(1)}, u32[]{:S(2)}, u32[]{:S(2)}) collective-permute-start(bf16[272,1536]{1,0:T(8,128)(2,1)} %shard_map.178.refs_0_), channel_id=1, source_target_pairs={{0,16},{8,24},{16,0},{24,8},{1,17},{9,25},{17,1},{25,9},{2,18},{10... | collective-permute-start | bytes 2506760 | tf_op jit(solution)/shard_map/ppermute | solution.py:42
  55.2 67.8 %collective-permute-start.7 = (bf16[272,1536]{1,0:T(8,128)(2,1)}, bf16[272,1536]{1,0:T(8,128)(2,1)}, u32[]{:S(2)}, u32[]{:S(2)}) collective-permute-start(bf16[272,1536]{1,0:T(8,128)(2,1)} %shard_map.178.refs_0_), channel_id=1, source_target_pairs={{0,8},{8,0},{16,24},{24,16},{1,9},{9,1},{17,25},{25,17},{2,10},{10... | collective-permute-start | bytes 2506760 | tf_op jit(solution)/shard_map/ppermute | solution.py:42
  129.1 287.2 %reduce-scatter.3.cloned.1.call-start = ((), (), s32[]{:S(2)}) async-start(), calls=%async_computation.4 | async-start | bytes 6193152 | tf_op jit(solution)/shard_map/reduce_scatter | solution.py:539
  155.3 32.8 %collective-permute-start.15 = (bf16[256,1536]{1,0:T(8,128)(2,1)}, bf16[256,1536]{1,0:T(8,128)(2,1)S(1)}, u32[]{:S(2)}, u32[]{:S(2)}) collective-permute-start(bf16[256,1536]{1,0:T(8,128)(2,1)} %shard_map.183), channel_id=1, source_target_pairs={{0,8},{8,0},{16,24},{24,16},{1,9},{9,1},{17,25},{25,17},{2,10},{10... | collective-permute-start | bytes 2359304 | tf_op jit(solution)/shard_map/ppermute | solution.py:42
  156.4 31.7 %collective-permute-start.16 = (bf16[256,1536]{1,0:T(8,128)(2,1)}, bf16[256,1536]{1,0:T(8,128)(2,1)S(1)}, u32[]{:S(2)}, u32[]{:S(2)}) collective-permute-start(bf16[256,1536]{1,0:T(8,128)(2,1)} %get-tuple-element.55), channel_id=1, source_target_pairs={{0,16},{8,24},{16,0},{24,8},{1,17},{9,25},{17,1},{25,9},{2,18},{10... | collective-permute-start | bytes 2359304 | tf_op jit(solution)/shard_map/ppermute | solution.py:42
  157.3 48.2 %collective-permute-start.17 = (bf16[256,1536]{1,0:T(8,128)(2,1)S(1)}, bf16[256,1536]{1,0:T(8,128)(2,1)S(1)}, u32[]{:S(2)}, u32[]{:S(2)}) collective-permute-start(bf16[256,1536]{1,0:T(8,128)(2,1)S(1)} %copy-done.38), channel_id=1, source_target_pairs={{0,24},{8,16},{16,8},{24,0},{1,25},{9,17},{17,9},{25,1},{2,26},{10... | collective-permute-start | bytes 2359304 | tf_op jit(solution)/shard_map/ppermute | solution.py:42
  158.8 55.8 %collective-permute-start.21 = (bf16[256,1536]{1,0:T(8,128)(2,1)S(1)}, bf16[256,1536]{1,0:T(8,128)(2,1)}, u32[]{:S(2)}, u32[]{:S(2)}) collective-permute-start(bf16[256,1536]{1,0:T(8,128)(2,1)S(1)} %copy-done.11), channel_id=1, source_target_pairs={{0,2},{2,0},{4,6},{6,4},{1,3},{3,1},{5,7},{7,5},{8,10},{10,8},{12,... | collective-permute-start | bytes 2359304 | tf_op jit(solution)/shard_map/ppermute | solution.py:42
  174.3 35.7 %collective-permute-start.18 = (bf16[256,1536]{1,0:T(8,128)(2,1)S(1)}, bf16[256,1536]{1,0:T(8,128)(2,1)}, u32[]{:S(2)}, u32[]{:S(2)}) collective-permute-start(bf16[256,1536]{1,0:T(8,128)(2,1)S(1)} %copy-done.11), channel_id=1, source_target_pairs={{0,4},{2,6},{4,0},{6,2},{1,5},{3,7},{5,1},{7,3},{8,12},{10,14},{12... | collective-permute-start | bytes 2359304 | tf_op jit(solution)/shard_map/ppermute | solution.py:42
  212.5 34.2 %collective-permute-start.19 = (bf16[256,1536]{1,0:T(8,128)(2,1)}, bf16[256,1536]{1,0:T(8,128)(2,1)}, u32[]{:S(2)}, u32[]{:S(2)}) collective-permute-start(bf16[256,1536]{1,0:T(8,128)(2,1)} %shard_map.184.refs_0_), channel_id=1, source_target_pairs={{0,2},{2,0},{4,6},{6,4},{1,3},{3,1},{5,7},{7,5},{8,10},{10,8},{12,... | collective-permute-start | bytes 2359304 | tf_op jit(solution)/shard_map/ppermute | solution.py:42
  246.7 36.5 %collective-permute-start.22 = (bf16[256,1536]{1,0:T(8,128)(2,1)}, bf16[256,1536]{1,0:T(8,128)(2,1)S(1)}, u32[]{:S(2)}, u32[]{:S(2)}) collective-permute-start(bf16[256,1536]{1,0:T(8,128)(2,1)} %shard_map.187), channel_id=1, source_target_pairs={{0,4},{2,6},{4,0},{6,2},{1,5},{3,7},{5,1},{7,3},{8,12},{10,14},{12... | collective-permute-start | bytes 2359304 | tf_op jit(solution)/shard_map/ppermute | solution.py:42
  267.9 48.9 %collective-permute-start.23 = (bf16[256,1536]{1,0:T(8,128)(2,1)}, bf16[256,1536]{1,0:T(8,128)(2,1)S(1)}, u32[]{:S(2)}, u32[]{:S(2)}) collective-permute-start(bf16[256,1536]{1,0:T(8,128)(2,1)} %get-tuple-element.63), channel_id=1, source_target_pairs={{0,2},{2,0},{4,6},{6,4},{1,3},{3,1},{5,7},{7,5},{8,10},{10,8},{12,... | collective-permute-start | bytes 2359304 | tf_op jit(solution)/shard_map/ppermute | solution.py:42
  269.6 47.2 %collective-permute-start.26 = (bf16[256,1536]{1,0:T(8,128)(2,1)}, bf16[256,1536]{1,0:T(8,128)(2,1)}, u32[]{:S(2)}, u32[]{:S(2)}) collective-permute-start(bf16[256,1536]{1,0:T(8,128)(2,1)} %get-tuple-element.66), channel_id=1, source_target_pairs={{0,6},{2,4},{4,2},{6,0},{1,7},{3,5},{5,3},{7,1},{8,14},{10,12},{12... | collective-permute-start | bytes 2359304 | tf_op jit(solution)/shard_map/ppermute | solution.py:42
  321.7 239.2 %reduce-scatter.5.cloned.1.call-start = ((), (), s32[]{:S(2)}) async-start(), calls=%async_computation.5 | async-start | bytes 12386304 | tf_op jit(solution)/shard_map/reduce_scatter | solution.py:567
  321.8 31.4 %collective-permute-start.25 = (bf16[224,1536]{1,0:T(8,128)(2,1)}, bf16[224,1536]{1,0:T(8,128)(2,1)}, u32[]{:S(2)}, u32[]{:S(2)}) collective-permute-start(bf16[224,1536]{1,0:T(8,128)(2,1)} %get-tuple-element.65), channel_id=1, source_target_pairs={{0,4},{2,6},{4,0},{6,2},{1,5},{3,7},{5,1},{7,3},{8,12},{10,14},{12... | collective-permute-start | bytes 2064392 | tf_op jit(solution)/shard_map/ppermute | solution.py:42
  357.5 43.8 %collective-permute-start.28 = (bf16[256,1536]{1,0:T(8,128)(2,1)}, bf16[256,1536]{1,0:T(8,128)(2,1)}, u32[]{:S(2)}, u32[]{:S(2)}) collective-permute-start(bf16[256,1536]{1,0:T(8,128)(2,1)} %fusion.38.refs_0_.refs_4_), channel_id=1, source_target_pairs={{0,16},{8,24},{16,0},{24,8},{1,17},{9,25},{17,1},{25,9},{2,18},{10... | collective-permute-start | bytes 2359304 | tf_op jit(solution)/shard_map/ppermute | solution.py:42
  359.2 42.1 %collective-permute-start.27 = (bf16[256,1536]{1,0:T(8,128)(2,1)}, bf16[256,1536]{1,0:T(8,128)(2,1)}, u32[]{:S(2)}, u32[]{:S(2)}) collective-permute-start(bf16[256,1536]{1,0:T(8,128)(2,1)} %fusion.38.refs_0_.refs_4_), channel_id=1, source_target_pairs={{0,8},{8,0},{16,24},{24,16},{1,9},{9,1},{17,25},{25,17},{2,10},{10... | collective-permute-start | bytes 2359304 | tf_op jit(solution)/shard_map/ppermute | solution.py:42
  360.5 40.8 %collective-permute-start.30 = (bf16[256,1536]{1,0:T(8,128)(2,1)}, bf16[256,1536]{1,0:T(8,128)(2,1)S(1)}, u32[]{:S(2)}, u32[]{:S(2)}) collective-permute-start(bf16[256,1536]{1,0:T(8,128)(2,1)} %shard_map.193), channel_id=1, source_target_pairs={{0,2},{2,0},{4,6},{6,4},{1,3},{3,1},{5,7},{7,5},{8,10},{10,8},{12,... | collective-permute-start | bytes 2359304 | tf_op jit(solution)/shard_map/ppermute | solution.py:42
  360.5 40.8 %collective-permute-start.31 = (bf16[256,1536]{1,0:T(8,128)(2,1)}, bf16[256,1536]{1,0:T(8,128)(2,1)S(1)}, u32[]{:S(2)}, u32[]{:S(2)}) collective-permute-start(bf16[256,1536]{1,0:T(8,128)(2,1)} %shard_map.194), channel_id=1, source_target_pairs={{0,4},{2,6},{4,0},{6,2},{1,5},{3,7},{5,1},{7,3},{8,12},{10,14},{12... | collective-permute-start | bytes 2359304 | tf_op jit(solution)/shard_map/ppermute | solution.py:42
  413.3 32.8 %collective-permute-start.32 = (bf16[256,1536]{1,0:T(8,128)(2,1)}, bf16[256,1536]{1,0:T(8,128)(2,1)S(1)}, u32[]{:S(2)}, u32[]{:S(2)}) collective-permute-start(bf16[256,1536]{1,0:T(8,128)(2,1)} %shard_map.198), channel_id=1, source_target_pairs={{0,6},{2,4},{4,2},{6,0},{1,7},{3,5},{5,3},{7,1},{8,14},{10,12},{12... | collective-permute-start | bytes 2359304 | tf_op jit(solution)/shard_map/ppermute | solution.py:42
  457.6 33.1 %collective-permute-start.38 = (bf16[208,1536]{1,0:T(8,128)(2,1)}, bf16[208,1536]{1,0:T(8,128)(2,1)}, u32[]{:S(2)}, u32[]{:S(2)}) collective-permute-start(bf16[208,1536]{1,0:T(8,128)(2,1)} %get-tuple-element.93), channel_id=1, source_target_pairs={{0,2},{2,0},{4,6},{6,4},{1,3},{3,1},{5,7},{7,5},{8,10},{10,8},{12,... | collective-permute-start | bytes 1916936 | tf_op jit(solution)/shard_map/ppermute | solution.py:42
  462.3 48.4 %collective-permute-start.39 = (bf16[208,1536]{1,0:T(8,128)(2,1)}, bf16[208,1536]{1,0:T(8,128)(2,1)}, u32[]{:S(2)}, u32[]{:S(2)}) collective-permute-start(bf16[208,1536]{1,0:T(8,128)(2,1)} %get-tuple-element.94), channel_id=1, source_target_pairs={{0,4},{2,6},{4,0},{6,2},{1,5},{3,7},{5,1},{7,3},{8,12},{10,14},{12... | collective-permute-start | bytes 1916936 | tf_op jit(solution)/shard_map/ppermute | solution.py:42
  463.0 47.8 %collective-permute-start.40 = (bf16[208,1536]{1,0:T(8,128)(2,1)}, bf16[208,1536]{1,0:T(8,128)(2,1)}, u32[]{:S(2)}, u32[]{:S(2)}) collective-permute-start(bf16[208,1536]{1,0:T(8,128)(2,1)} %get-tuple-element.95), channel_id=1, source_target_pairs={{0,6},{2,4},{4,2},{6,0},{1,7},{3,5},{5,3},{7,1},{8,14},{10,12},{12... | collective-permute-start | bytes 1916936 | tf_op jit(solution)/shard_map/ppermute | solution.py:42
  465.0 91.6 %all-to-all-start.1 = ((bf16[32,48,216]{2,1,0:T(8,128)(2,1)}), bf16[32,48,216]{2,1,0:T(8,128)(2,1)}, u32[]{:S(2)}, u32[]{:S(2)}) async-start(bf16[32,48,216]{2,1,0:T(8,128)(2,1)} %shard_map.208), calls=%async_computation.3 | async-start | bytes 1572864 | tf_op jit(solution)/shard_map/all_to_all | solution.py:633
  468.5 79.4 %collective-permute-start.35 = (bf16[256,1536]{1,0:T(8,128)(2,1)}, bf16[256,1536]{1,0:T(8,128)(2,1)}, u32[]{:S(2)}, u32[]{:S(2)}) collective-permute-start(bf16[256,1536]{1,0:T(8,128)(2,1)} %shard_map.204), channel_id=1, source_target_pairs={{0,8},{8,0},{16,24},{24,16},{1,9},{9,1},{17,25},{25,17},{2,10},{10... | collective-permute-start | bytes 2359304 | tf_op jit(solution)/shard_map/ppermute | solution.py:42
  470.2 77.9 %collective-permute-start.36 = (bf16[256,1536]{1,0:T(8,128)(2,1)}, bf16[256,1536]{1,0:T(8,128)(2,1)}, u32[]{:S(2)}, u32[]{:S(2)}) collective-permute-start(bf16[256,1536]{1,0:T(8,128)(2,1)} %shard_map.205), channel_id=1, source_target_pairs={{0,16},{8,24},{16,0},{24,8},{1,17},{9,25},{17,1},{25,9},{2,18},{10... | collective-permute-start | bytes 2359304 | tf_op jit(solution)/shard_map/ppermute | solution.py:42
  490.7 57.5 %collective-permute-start.37 = (bf16[256,1536]{1,0:T(8,128)(2,1)}, bf16[256,1536]{1,0:T(8,128)(2,1)}, u32[]{:S(2)}, u32[]{:S(2)}) collective-permute-start(bf16[256,1536]{1,0:T(8,128)(2,1)} %shard_map.206), channel_id=1, source_target_pairs={{0,24},{8,16},{16,8},{24,0},{1,25},{9,17},{17,9},{25,1},{2,26},{10... | collective-permute-start | bytes 2359304 | tf_op jit(solution)/shard_map/ppermute | solution.py:42
  (60 other events, 560.0 us)
Sparse Core Ops, SparseCore 0:
  10.0 115.3 all-gather.4
  129.2 56.0 all-gather.6
  321.9 80.1 reduce-scatter.2
  409.2 98.6 reduce-scatter.4

commit v5 on v4

--- a/solution.py
+++ b/solution.py
@@ -564,7 +564,7 @@
     )
     block_out = second + total([tie(out_terms[0], dconv)] + out_terms[1:])
     block_out = block_out.astype(bf16).reshape(seqs, group, width)
-    g_ff = lax.psum_scatter(tie(g_ff, dconv), ("fsdp", "core"), scatter_dimension=0)
+    g_ff = lax.psum_scatter(tie(g_ff, *branch_slots[1:]), ("fsdp", "core"), scatter_dimension=0)
     g_down = g_down[:hid].T.reshape(count, feats, hid)
     ahead = dconv.reshape(lanes, seqs, group, mine)[:, :, :2]
     ahead = lax.ppermute(ahead, ("line", "core"), back).reshape(lanes, 2 * seqs, mine)

time: 579 us -> 613 us (1.059)
  waiting for transfers between devices: 235 us -> 249 us
  starting transfers between devices: 105 us -> 118 us
  local copies, waits for them, and re-layouts: 33.5 us -> 42.4 us
    ppermute x39, waiting for transfers between devices: 227 us -> 241 us  [flip(): return lax.ppermute(block, axis, [(i, i ^ bits) for i in range(size)])]
    ppermute x3, starting transfers between devices: 15.2 us -> 24.3 us  [on_device(): parts.append(lax.ppermute(block, every, homes[j]))]
    unnamed x82 -> x83, local copies, waits for them, and re-layouts: 12.5 us -> 21.5 us
  transfers between devices with their start and end apart: 53 -> 53, of which waited for: 22 -> 25; matrix products, arithmetic and copies ran while one was open for 9% -> 10% of each run, Pallas kernels for 27% -> 25%
where the time goes in v5:
time: 613 us; the launch traced here: 605 us
  waiting for transfers between devices  249 us (41%)
  Pallas kernels  150 us (24%)
  starting transfers between devices  118 us (19%)
  local copies, waits for them, and re-layouts  42.4 us (7%)
  other arithmetic  30.1 us (5%)
  between operations  15.2 us (2%)
    ppermute x39, waiting for transfers between devices, flip(): return lax.ppermute(block, axis, [(i, i ^ bits) for i in range(size)])  241 us
    pallas_call x11, Pallas kernels, kernel_call(): pl.pallas_call(lambda *refs: body(*refs[:held], *refs[held + len(waits):]...  150 us
    ppermute x39, starting transfers between devices, flip(): return lax.ppermute(block, axis, [(i, i ^ bits) for i in range(size)])  74 us
    ppermute x3, starting transfers between devices, on_device(): parts.append(lax.ppermute(block, every, homes[j]))  24.3 us
    unnamed x83, local copies, waits for them, and re-layouts  21.5 us
  transfers between devices with their start and end apart: 53, of which 25 were waited for; matrix products, arithmetic and copies ran while one was open for 10% of the time, Pallas kernels for 25%

profile of v5, /device:TPU:0, one launch (start us, length us, event | category | flops | bytes accessed | tf_op | source)
XLA Modules:
  0.0 605.2 jit_solution(6887846396658447636)
XLA Ops:
  17.6 8.0 %collective-permute-start.3 = (bf16[48,1536]{1,0:T(8,128)(2,1)S(1)}, bf16[48,1536]{1,0:T(8,128)(2,1)S(1)}, u32[]{:S(2)}, u32[]{:S(2)}) collective-permute-start(bf16[48,1536]{1,0:T(8,128)(2,1)S(1)} %get-tuple-element.114), channel_id=1, source_target_pairs={{0,2},{1,5},{2,8},{3,11},{4,14},{5,17},{6,20},{7,23},{8,26},{9,29}... | collective-permute-start | bytes 442376 | tf_op jit(solution)/shard_map/ppermute | solution.py:367
  26.4 5.8 collective-permute-done.3
  35.3 4.7 collective-permute-start.12
  55.3 54.8 %collective-permute-done.11.refs_7_.refs_2_ = bf16[208,1536]{1,0:T(8,128)(2,1)S(1)} collective-permute-done((bf16[208,1536]{1,0:T(8,128)(2,1)}, bf16[208,1536]{1,0:T(8,128)(2,1)S(1)}, u32[]{:S(2)}, u32[]{:S(2)}) %collective-permute-start.11) | collective-permute-done | bytes 639008 | tf_op jit(solution)/shard_map/ppermute | solution.py:42
  116.3 6.8 %collective-permute-done.7.refs_1_ = bf16[272,1536]{1,0:T(8,128)(2,1)} collective-permute-done((bf16[272,1536]{1,0:T(8,128)(2,1)}, bf16[272,1536]{1,0:T(8,128)(2,1)}, u32[]{:S(2)}, u32[]{:S(2)}) %collective-permute-start.7) | collective-permute-done | bytes 835616 | tf_op jit(solution)/shard_map/ppermute | solution.py:42
  135.2 19.2 %shard_map.181 = (bf16[256,1536]{1,0:T(8,128)(2,1)}, bf16[256,1536]{1,0:T(8,128)(2,1)}, bf16[256,1536]{1,0:T(8,128)(2,1)}, bf16[256,1536]{1,0:T(8,128)(2,1)}, bf...) custom-call(bf16[272,1536]{1,0:T(8,128)(2,1)} %shard_map.178.refs_0_, ...), custom_call_target="tpu_custom_call" | custom-call | flops 14495514624 | bytes 27476004 | tf_op jit(solution)/shard_map/pallas_call | solution.py:82
  158.8 15.6 %collective-permute-start.21 = (bf16[256,1536]{1,0:T(8,128)(2,1)S(1)}, bf16[256,1536]{1,0:T(8,128)(2,1)}, u32[]{:S(2)}, u32[]{:S(2)}) collective-permute-start(bf16[256,1536]{1,0:T(8,128)(2,1)S(1)} %copy-done.11), channel_id=1, source_target_pairs={{0,2},{2,0},{4,6},{6,4},{1,3},{3,1},{5,7},{7,5},{8,10},{10,8},{12,... | collective-permute-start | bytes 2359304 | tf_op jit(solution)/shard_map/ppermute | solution.py:42
  176.2 11.9 %collective-permute-done.15 = bf16[256,1536]{1,0:T(8,128)(2,1)S(1)} collective-permute-done((bf16[256,1536]{1,0:T(8,128)(2,1)}, bf16[256,1536]{1,0:T(8,128)(2,1)S(1)}, u32[]{:S(2)}, u32[]{:S(2)}) %collective-permute-start.15) | collective-permute-done | bytes 786464 | tf_op jit(solution)/shard_map/ppermute | solution.py:42
  188.2 17.4 %collective-permute-done.17 = bf16[256,1536]{1,0:T(8,128)(2,1)S(1)} collective-permute-done((bf16[256,1536]{1,0:T(8,128)(2,1)S(1)}, bf16[256,1536]{1,0:T(8,128)(2,1)S(1)}, u32[]{:S(2)}, u32[]{:S(2)}) %collective-permute-start.17) | collective-permute-done | bytes 786464 | tf_op jit(solution)/shard_map/ppermute | solution.py:42
  214.7 7.1 %shard_map.186.refs_3_.refs_4_ = f32[2,512,896]{2,1,0:T(8,128)} custom-call(bf16[256,1536]{1,0:T(8,128)(2,1)} %collective-permute-done.21.refs_0_.refs_1_, bf16[256,1536]{1,0:T(8,128)(2,1)} %copy-done.19, bf16[8,224,1536]{2,1,0:T(8,128)(2,1)} %bitcast.175), custom_call_target="tpu_custom_call" | custom-call | flops 2818572288 | bytes 10747904 | tf_op jit(solution)/shard_map/pallas_call | solution.py:82
  221.8 10.9 %collective-permute-done.20.refs_2_.refs_1_.refs_3_ = bf16[256,1536]{1,0:T(8,128)(2,1)} collective-permute-done((bf16[256,1536]{1,0:T(8,128)(2,1)}, bf16[256,1536]{1,0:T(8,128)(2,1)}, u32[]{:S(2)}, u32[]{:S(2)}) %collective-permute-start.20) | collective-permute-done | bytes 786464 | tf_op jit(solution)/shard_map/ppermute | solution.py:42
  232.7 14.0 %collective-permute-done.19.refs_1_.refs_0_ = bf16[256,1536]{1,0:T(8,128)(2,1)} collective-permute-done((bf16[256,1536]{1,0:T(8,128)(2,1)}, bf16[256,1536]{1,0:T(8,128)(2,1)}, u32[]{:S(2)}, u32[]{:S(2)}) %collective-permute-start.19) | collective-permute-done | bytes 786464 | tf_op jit(solution)/shard_map/ppermute | solution.py:42
  247.3 20.7 %shard_map.189 = (bf16[2,512,896]{2,1,0:T(8,128)(2,1)}, bf16[2,512,896]{2,1,0:T(8,128)(2,1)}, bf16[2,512,896]{2,1,0:T(8,128)(2,1)}, bf16[256,1536]{1,0:T(8,128)(2,1)}, bf16[256,1536]{1,0:T(8,128)(2,1)}) custom-call(bf16[256,1536]{1,0:T(8,128)(2,1)} %collective-permute-done.19.refs_1_.refs_0_, ...), custom_call_target="tpu_custom_call" | custom-call | flops 11274289152 | bytes 34340864 | tf_op jit(solution)/shard_map/pallas_call | solution.py:82
  271.9 7.2 %shard_map.188.refs_4_ = f32[2,512,896]{2,1,0:T(8,128)} custom-call(bf16[256,1536]{1,0:T(8,128)(2,1)} %shard_map.182.refs_0_, bf16[256,1536]{1,0:T(8,128)(2,1)} %collective-permute-done.18.refs_1_.refs_2_, bf16[8,224,1536]{2,1,0:T(8,128)(2,1)} %bitcast.176), custom_call_target="tpu_custom_call" | custom-call | flops 2818572288 | bytes 10747904 | tf_op jit(solution)/shard_map/pallas_call | solution.py:82
  284.2 20.7 %shard_map.190 = (bf16[2,512,896]{2,1,0:T(8,128)(2,1)}, bf16[2,512,896]{2,1,0:T(8,128)(2,1)}, bf16[2,512,896]{2,1,0:T(8,128)(2,1)}, bf16[32,1536]{1,0:T(8,128)(2...) custom-call(bf16[256,1536]{1,0:T(8,128)(2,1)} %shard_map.184.refs_0_, ...), custom_call_target="tpu_custom_call" | custom-call | flops 11274289152 | bytes 34340864 | tf_op jit(solution)/shard_map/pallas_call | solution.py:82
  305.0 10.3 %shard_map.199.refs_0_ = bf16[8,224,1536]{2,1,0:T(8,128)(2,1)} custom-call(bf16[256,1536]{1,0:T(8,128)(2,1)} %shard_map.182.refs_0_, bf16[256,1536]{1,0:T(8,128)(2,1)} %collective-permute-done.21.refs_0_.refs_1_, bf16[256,1536]{1,0:T(8,128)(2,1)} %collective-permute-done.18.refs_1_.refs_2_, bf16[256,1536]{1,0:T(8,128)(2,1)} %copy-done.19, ...), custom_call_target="tpu_custom_call" | custom-call | flops 5637144576 | bytes 12320768 | tf_op jit(solution)/shard_map/pallas_call | solution.py:82
  316.9 4.3 collective-permute-done.24.refs_3_
  323.8 12.9 %shard_map.191 = (bf16[256,1536]{1,0:T(8,128)(2,1)}, bf16[256,1536]{1,0:T(8,128)(2,1)}, bf16[256,1536]{1,0:T(8,128)(2,1)}, bf16[256,1536]{1,0:T(8,128)(2,1)}) custom-call(bf16[2,512,896]{2,1,0:T(8,128)(2,1)} %get-tuple-element.59.refs_0_.refs_4_, bf16[2,512,896]{2,1,0:T(8,128)(2,1)} %get-tuple-element.58.refs_5_.refs_1_, bf16[8,224,1536]{2,1,0:T(8,128)(2,1)} %bitcast.177), custom_call_target="tpu_custom_call" | custom-call | flops 5637144576 | bytes 12320768 | tf_op jit(solution)/shard_map/pallas_call | solution.py:82
  336.7 16.5 %collective-permute-done.25.refs_4_ = bf16[224,1536]{1,0:T(8,128)(2,1)} collective-permute-done((bf16[224,1536]{1,0:T(8,128)(2,1)}, bf16[224,1536]{1,0:T(8,128)(2,1)}, u32[]{:S(2)}, u32[]{:S(2)}) %collective-permute-start.25) | collective-permute-done | bytes 688160 | tf_op jit(solution)/shard_map/ppermute | solution.py:42
  360.3 17.7 %shard_map.195.refs_9_ = bf16[8,448,1536]{2,1,0:T(8,128)(2,1)} custom-call(bf16[256,1536]{1,0:T(8,128)(2,1)} %shard_map.184.refs_0_, bf16[256,1536]{1,0:T(8,128)(2,1)} %collective-permute-done.19.refs_1_.refs_0_, bf16[256,1536]{1,0:T(8,128)(2,1)} %copy-done.37, bf16[256,1536]{1,0:T(8,128)(2,1)} %collective-permute-done.20.refs_2_.refs_1_.refs_3_, ...), custom_call_target="tpu_custom_call" | custom-call | flops 11274289152 | bytes 21495808 | tf_op jit(solution)/shard_map/pallas_call | solution.py:82
  378.0 9.6 %copy.92.refs_0_ = bf16[8,448,1536]{2,1,0:T(8,128)(2,1)} copy(bf16[8,448,1536]{2,1,0:T(8,128)(2,1)} %shard_map.195.refs_9_) | data formatting | bytes 22020096
  387.6 13.0 %collective-permute-done.28.refs_2_.refs_6_ = bf16[256,1536]{1,0:T(8,128)(2,1)} collective-permute-done((bf16[256,1536]{1,0:T(8,128)(2,1)S(1)}, bf16[256,1536]{1,0:T(8,128)(2,1)}, u32[]{:S(2)}, u32[]{:S(2)}) %collective-permute-start.28) | collective-permute-done | bytes 786464 | tf_op jit(solution)/shard_map/ppermute | solution.py:42
  404.1 31.4 %collective-permute-done.30.refs_7_ = bf16[256,1536]{1,0:T(8,128)(2,1)S(1)} collective-permute-done((bf16[256,1536]{1,0:T(8,128)(2,1)}, bf16[256,1536]{1,0:T(8,128)(2,1)S(1)}, u32[]{:S(2)}, u32[]{:S(2)}) %collective-permute-start.30) | collective-permute-done | bytes 786464 | tf_op jit(solution)/shard_map/ppermute | solution.py:42
  437.3 6.6 %shard_map.196 = (f32[4,256,384]{2,1,0:T(8,128)}, bf16[4,256,384]{2,1,0:T(8,128)(2,1)}) custom-call(bf16[256,1536]{1,0:T(8,128)(2,1)} %copy-done.15, bf16[256,1536]{1,0:T(8,128)(2,1)} %collective-permute-done.27.refs_1_.refs_5_, bf16[256,1536]{1,0:T(8,128)(2,1)} %collective-permute-done.28.refs_2_.refs_6_, bf16[256,1536]{1,0:T(8,128)(2,1)} %copy-done.12, ...), custom_call_target="tpu_custom_call" | custom-call | flops 1207959552 | bytes 9830400 | tf_op jit(solution)/shard_map/pallas_call | solution.py:82
  454.9 23.7 %shard_map.201 = (bf16[256,1536]{1,0:T(8,128)(2,1)}, bf16[256,1536]{1,0:T(8,128)(2,1)}, bf16[256,1536]{1,0:T(8,128)(2,1)}, bf16[256,1536]{1,0:T(8,128)(2,1)}, bf...) custom-call(bf16[272,1536]{1,0:T(8,128)(2,1)} %shard_map.178.refs_0_, ...), custom_call_target="tpu_custom_call" | custom-call | flops 8455716864 | bytes 28592676 | tf_op jit(solution)/shard_map/pallas_call | solution.py:82
  479.7 4.9 collective-permute-done.34.refs_1_
  490.1 6.3 %collective-permute-start.38 = (bf16[208,1536]{1,0:T(8,128)(2,1)}, bf16[208,1536]{1,0:T(8,128)(2,1)}, u32[]{:S(2)}, u32[]{:S(2)}) collective-permute-start(bf16[208,1536]{1,0:T(8,128)(2,1)} %get-tuple-element.93), channel_id=1, source_target_pairs={{0,2},{2,0},{4,6},{6,4},{1,3},{3,1},{5,7},{7,5},{8,10},{10,8},{12,... | collective-permute-start | bytes 1916936 | tf_op jit(solution)/shard_map/ppermute | solution.py:42
  499.1 4.2 all-to-all-start.1
  506.5 18.1 %collective-permute-done.38 = bf16[208,1536]{1,0:T(8,128)(2,1)} collective-permute-done((bf16[208,1536]{1,0:T(8,128)(2,1)}, bf16[208,1536]{1,0:T(8,128)(2,1)}, u32[]{:S(2)}, u32[]{:S(2)}) %collective-permute-start.38) | collective-permute-done | bytes 639008 | tf_op jit(solution)/shard_map/ppermute | solution.py:42
  525.9 19.6 %collective-permute-done.39 = bf16[208,1536]{1,0:T(8,128)(2,1)} collective-permute-done((bf16[208,1536]{1,0:T(8,128)(2,1)}, bf16[208,1536]{1,0:T(8,128)(2,1)}, u32[]{:S(2)}, u32[]{:S(2)}) %collective-permute-start.39) | collective-permute-done | bytes 639008 | tf_op jit(solution)/shard_map/ppermute | solution.py:42
  557.1 23.4 %collective-permute-start.46 = (bf16[48,1536]{1,0:T(8,128)(2,1)S(1)}, bf16[48,1536]{1,0:T(8,128)(2,1)S(1)}, u32[]{:S(2)}, u32[]{:S(2)}) collective-permute-start(bf16[48,1536]{1,0:T(8,128)(2,1)S(1)} %get-tuple-element.108), channel_id=1, source_target_pairs={{2,0},{5,1},{8,2},{11,3},{14,4},{17,5},{20,6},{23,7},{26,8},{29,9}... | collective-permute-start | bytes 442376 | tf_op jit(solution)/shard_map/ppermute | solution.py:654
  586.0 4.8 fusion.8
  (260 shorter events, 137.7 us)
Async XLA Ops:
  7.2 121.9 %all-gather.5.cloned.1.call-start = ((), (), s32[]{:S(2)}) async-start(), calls=%async_computation.6 | async-start | bytes 12386304 | tf_op jit(solution)/shard_map/all_gather | solution.py:421
  43.7 79.3 %all-to-all-start = ((bf16[32,48,216]{2,1,0:T(8,128)(2,1)}), bf16[32,48,216]{2,1,0:T(8,128)(2,1)S(1)}, u32[]{:S(2)}, u32[]{:S(2)}) async-start(bf16[32,48,216]{2,1,0:T(8,128)(2,1)} %shard_map.179), calls=%async_computation | async-start | bytes 1572864 | tf_op jit(solution)/shard_map/all_to_all | solution.py:384
  46.5 168.2 %all-gather.7.cloned.1.call-start = ((), (), s32[]{:S(2)}) async-start(), calls=%async_computation.7 | async-start | bytes 6193152 | tf_op jit(solution)/shard_map/all_gather | solution.py:458
  46.6 63.5 %collective-permute-start.11 = (bf16[208,1536]{1,0:T(8,128)(2,1)}, bf16[208,1536]{1,0:T(8,128)(2,1)S(1)}, u32[]{:S(2)}, u32[]{:S(2)}) collective-permute-start(bf16[208,1536]{1,0:T(8,128)(2,1)} %shard_map.177.refs_1_.refs_5_), channel_id=1, source_target_pairs={{0,4},{2,6},{4,0},{6,2},{1,5},{3,7},{5,1},{7,3},{8,12},{10,14},{12... | collective-permute-start | bytes 1916936 | tf_op jit(solution)/shard_map/ppermute | solution.py:42
  49.3 60.7 %collective-permute-start.10 = (bf16[208,1536]{1,0:T(8,128)(2,1)}, bf16[208,1536]{1,0:T(8,128)(2,1)S(1)}, u32[]{:S(2)}, u32[]{:S(2)}) collective-permute-start(bf16[208,1536]{1,0:T(8,128)(2,1)} %shard_map.177.refs_1_.refs_5_), channel_id=1, source_target_pairs={{0,2},{2,0},{4,6},{6,4},{1,3},{3,1},{5,7},{7,5},{8,10},{10,8},{12,... | collective-permute-start | bytes 1916936 | tf_op jit(solution)/shard_map/ppermute | solution.py:42
  51.8 61.6 %collective-permute-start.9 = (bf16[272,1536]{1,0:T(8,128)(2,1)}, bf16[272,1536]{1,0:T(8,128)(2,1)S(1)}, u32[]{:S(2)}, u32[]{:S(2)}) collective-permute-start(bf16[272,1536]{1,0:T(8,128)(2,1)} %shard_map.178.refs_0_), channel_id=1, source_target_pairs={{0,24},{8,16},{16,8},{24,0},{1,25},{9,17},{17,9},{25,1},{2,26},{10... | collective-permute-start | bytes 2506760 | tf_op jit(solution)/shard_map/ppermute | solution.py:42
  54.2 61.2 %collective-permute-start.8 = (bf16[272,1536]{1,0:T(8,128)(2,1)}, bf16[272,1536]{1,0:T(8,128)(2,1)S(1)}, u32[]{:S(2)}, u32[]{:S(2)}) collective-permute-start(bf16[272,1536]{1,0:T(8,128)(2,1)} %shard_map.178.refs_0_), channel_id=1, source_target_pairs={{0,16},{8,24},{16,0},{24,8},{1,17},{9,25},{17,1},{25,9},{2,18},{10... | collective-permute-start | bytes 2506760 | tf_op jit(solution)/shard_map/ppermute | solution.py:42
  55.2 67.8 %collective-permute-start.7 = (bf16[272,1536]{1,0:T(8,128)(2,1)}, bf16[272,1536]{1,0:T(8,128)(2,1)}, u32[]{:S(2)}, u32[]{:S(2)}) collective-permute-start(bf16[272,1536]{1,0:T(8,128)(2,1)} %shard_map.178.refs_0_), channel_id=1, source_target_pairs={{0,8},{8,0},{16,24},{24,16},{1,9},{9,1},{17,25},{25,17},{2,10},{10... | collective-permute-start | bytes 2506760 | tf_op jit(solution)/shard_map/ppermute | solution.py:42
  129.2 321.5 %reduce-scatter.3.cloned.1.call-start = ((), (), s32[]{:S(2)}) async-start(), calls=%async_computation.4 | async-start | bytes 6193152 | tf_op jit(solution)/shard_map/reduce_scatter | solution.py:539
  155.3 32.9 %collective-permute-start.15 = (bf16[256,1536]{1,0:T(8,128)(2,1)}, bf16[256,1536]{1,0:T(8,128)(2,1)S(1)}, u32[]{:S(2)}, u32[]{:S(2)}) collective-permute-start(bf16[256,1536]{1,0:T(8,128)(2,1)} %shard_map.183), channel_id=1, source_target_pairs={{0,8},{8,0},{16,24},{24,16},{1,9},{9,1},{17,25},{25,17},{2,10},{10... | collective-permute-start | bytes 2359304 | tf_op jit(solution)/shard_map/ppermute | solution.py:42
  156.4 31.8 %collective-permute-start.16 = (bf16[256,1536]{1,0:T(8,128)(2,1)}, bf16[256,1536]{1,0:T(8,128)(2,1)S(1)}, u32[]{:S(2)}, u32[]{:S(2)}) collective-permute-start(bf16[256,1536]{1,0:T(8,128)(2,1)} %get-tuple-element.55), channel_id=1, source_target_pairs={{0,16},{8,24},{16,0},{24,8},{1,17},{9,25},{17,1},{25,9},{2,18},{10... | collective-permute-start | bytes 2359304 | tf_op jit(solution)/shard_map/ppermute | solution.py:42
  157.3 48.2 %collective-permute-start.17 = (bf16[256,1536]{1,0:T(8,128)(2,1)S(1)}, bf16[256,1536]{1,0:T(8,128)(2,1)S(1)}, u32[]{:S(2)}, u32[]{:S(2)}) collective-permute-start(bf16[256,1536]{1,0:T(8,128)(2,1)S(1)} %copy-done.38), channel_id=1, source_target_pairs={{0,24},{8,16},{16,8},{24,0},{1,25},{9,17},{17,9},{25,1},{2,26},{10... | collective-permute-start | bytes 2359304 | tf_op jit(solution)/shard_map/ppermute | solution.py:42
  158.8 55.9 %collective-permute-start.21 = (bf16[256,1536]{1,0:T(8,128)(2,1)S(1)}, bf16[256,1536]{1,0:T(8,128)(2,1)}, u32[]{:S(2)}, u32[]{:S(2)}) collective-permute-start(bf16[256,1536]{1,0:T(8,128)(2,1)S(1)} %copy-done.11), channel_id=1, source_target_pairs={{0,2},{2,0},{4,6},{6,4},{1,3},{3,1},{5,7},{7,5},{8,10},{10,8},{12,... | collective-permute-start | bytes 2359304 | tf_op jit(solution)/shard_map/ppermute | solution.py:42
  174.4 35.7 %collective-permute-start.18 = (bf16[256,1536]{1,0:T(8,128)(2,1)S(1)}, bf16[256,1536]{1,0:T(8,128)(2,1)}, u32[]{:S(2)}, u32[]{:S(2)}) collective-permute-start(bf16[256,1536]{1,0:T(8,128)(2,1)S(1)} %copy-done.11), channel_id=1, source_target_pairs={{0,4},{2,6},{4,0},{6,2},{1,5},{3,7},{5,1},{7,3},{8,12},{10,14},{12... | collective-permute-start | bytes 2359304 | tf_op jit(solution)/shard_map/ppermute | solution.py:42
  212.5 34.2 %collective-permute-start.19 = (bf16[256,1536]{1,0:T(8,128)(2,1)}, bf16[256,1536]{1,0:T(8,128)(2,1)}, u32[]{:S(2)}, u32[]{:S(2)}) collective-permute-start(bf16[256,1536]{1,0:T(8,128)(2,1)} %shard_map.184.refs_0_), channel_id=1, source_target_pairs={{0,2},{2,0},{4,6},{6,4},{1,3},{3,1},{5,7},{7,5},{8,10},{10,8},{12,... | collective-permute-start | bytes 2359304 | tf_op jit(solution)/shard_map/ppermute | solution.py:42
  246.7 36.5 %collective-permute-start.22 = (bf16[256,1536]{1,0:T(8,128)(2,1)}, bf16[256,1536]{1,0:T(8,128)(2,1)S(1)}, u32[]{:S(2)}, u32[]{:S(2)}) collective-permute-start(bf16[256,1536]{1,0:T(8,128)(2,1)} %shard_map.187), channel_id=1, source_target_pairs={{0,4},{2,6},{4,0},{6,2},{1,5},{3,7},{5,1},{7,3},{8,12},{10,14},{12... | collective-permute-start | bytes 2359304 | tf_op jit(solution)/shard_map/ppermute | solution.py:42
  268.0 48.8 %collective-permute-start.23 = (bf16[256,1536]{1,0:T(8,128)(2,1)}, bf16[256,1536]{1,0:T(8,128)(2,1)S(1)}, u32[]{:S(2)}, u32[]{:S(2)}) collective-permute-start(bf16[256,1536]{1,0:T(8,128)(2,1)} %get-tuple-element.63), channel_id=1, source_target_pairs={{0,2},{2,0},{4,6},{6,4},{1,3},{3,1},{5,7},{7,5},{8,10},{10,8},{12,... | collective-permute-start | bytes 2359304 | tf_op jit(solution)/shard_map/ppermute | solution.py:42
  269.7 47.1 %collective-permute-start.26 = (bf16[256,1536]{1,0:T(8,128)(2,1)}, bf16[256,1536]{1,0:T(8,128)(2,1)}, u32[]{:S(2)}, u32[]{:S(2)}) collective-permute-start(bf16[256,1536]{1,0:T(8,128)(2,1)} %get-tuple-element.66), channel_id=1, source_target_pairs={{0,6},{2,4},{4,2},{6,0},{1,7},{3,5},{5,3},{7,1},{8,14},{10,12},{12... | collective-permute-start | bytes 2359304 | tf_op jit(solution)/shard_map/ppermute | solution.py:42
  321.8 273.3 %reduce-scatter.5.cloned.1.call-start = ((), (), s32[]{:S(2)}) async-start(), calls=%async_computation.5 | async-start | bytes 12386304 | tf_op jit(solution)/shard_map/reduce_scatter | solution.py:567
  321.8 31.4 %collective-permute-start.25 = (bf16[224,1536]{1,0:T(8,128)(2,1)}, bf16[224,1536]{1,0:T(8,128)(2,1)}, u32[]{:S(2)}, u32[]{:S(2)}) collective-permute-start(bf16[224,1536]{1,0:T(8,128)(2,1)} %get-tuple-element.65), channel_id=1, source_target_pairs={{0,4},{2,6},{4,0},{6,2},{1,5},{3,7},{5,1},{7,3},{8,12},{10,14},{12... | collective-permute-start | bytes 2064392 | tf_op jit(solution)/shard_map/ppermute | solution.py:42
  357.3 43.4 %collective-permute-start.28 = (bf16[256,1536]{1,0:T(8,128)(2,1)S(1)}, bf16[256,1536]{1,0:T(8,128)(2,1)}, u32[]{:S(2)}, u32[]{:S(2)}) collective-permute-start(bf16[256,1536]{1,0:T(8,128)(2,1)S(1)} %fusion.38.refs_0_.refs_4_), channel_id=1, source_target_pairs={{0,16},{8,24},{16,0},{24,8},{1,17},{9,25},{17,1},{25,9},{2,18},{10... | collective-permute-start | bytes 2359304 | tf_op jit(solution)/shard_map/ppermute | solution.py:42
  358.9 41.7 %collective-permute-start.27 = (bf16[256,1536]{1,0:T(8,128)(2,1)S(1)}, bf16[256,1536]{1,0:T(8,128)(2,1)}, u32[]{:S(2)}, u32[]{:S(2)}) collective-permute-start(bf16[256,1536]{1,0:T(8,128)(2,1)S(1)} %fusion.38.refs_0_.refs_4_), channel_id=1, source_target_pairs={{0,8},{8,0},{16,24},{24,16},{1,9},{9,1},{17,25},{25,17},{2,10},{10... | collective-permute-start | bytes 2359304 | tf_op jit(solution)/shard_map/ppermute | solution.py:42
  400.7 34.9 %collective-permute-start.30 = (bf16[256,1536]{1,0:T(8,128)(2,1)}, bf16[256,1536]{1,0:T(8,128)(2,1)S(1)}, u32[]{:S(2)}, u32[]{:S(2)}) collective-permute-start(bf16[256,1536]{1,0:T(8,128)(2,1)} %shard_map.193), channel_id=1, source_target_pairs={{0,2},{2,0},{4,6},{6,4},{1,3},{3,1},{5,7},{7,5},{8,10},{10,8},{12,... | collective-permute-start | bytes 2359304 | tf_op jit(solution)/shard_map/ppermute | solution.py:42
  400.9 36.4 %collective-permute-start.31 = (bf16[256,1536]{1,0:T(8,128)(2,1)}, bf16[256,1536]{1,0:T(8,128)(2,1)}, u32[]{:S(2)}, u32[]{:S(2)}) collective-permute-start(bf16[256,1536]{1,0:T(8,128)(2,1)} %shard_map.194), channel_id=1, source_target_pairs={{0,4},{2,6},{4,0},{6,2},{1,5},{3,7},{5,1},{7,3},{8,12},{10,14},{12... | collective-permute-start | bytes 2359304 | tf_op jit(solution)/shard_map/ppermute | solution.py:42
  447.3 31.4 %collective-permute-start.32 = (bf16[256,1536]{1,0:T(8,128)(2,1)}, bf16[256,1536]{1,0:T(8,128)(2,1)S(1)}, u32[]{:S(2)}, u32[]{:S(2)}) collective-permute-start(bf16[256,1536]{1,0:T(8,128)(2,1)} %shard_map.198), channel_id=1, source_target_pairs={{0,6},{2,4},{4,2},{6,0},{1,7},{3,5},{5,3},{7,1},{8,14},{10,12},{12... | collective-permute-start | bytes 2359304 | tf_op jit(solution)/shard_map/ppermute | solution.py:42
  490.1 34.6 %collective-permute-start.38 = (bf16[208,1536]{1,0:T(8,128)(2,1)}, bf16[208,1536]{1,0:T(8,128)(2,1)}, u32[]{:S(2)}, u32[]{:S(2)}) collective-permute-start(bf16[208,1536]{1,0:T(8,128)(2,1)} %get-tuple-element.93), channel_id=1, source_target_pairs={{0,2},{2,0},{4,6},{6,4},{1,3},{3,1},{5,7},{7,5},{8,10},{10,8},{12,... | collective-permute-start | bytes 1916936 | tf_op jit(solution)/shard_map/ppermute | solution.py:42
  496.4 49.1 %collective-permute-start.39 = (bf16[208,1536]{1,0:T(8,128)(2,1)}, bf16[208,1536]{1,0:T(8,128)(2,1)}, u32[]{:S(2)}, u32[]{:S(2)}) collective-permute-start(bf16[208,1536]{1,0:T(8,128)(2,1)} %get-tuple-element.94), channel_id=1, source_target_pairs={{0,4},{2,6},{4,0},{6,2},{1,5},{3,7},{5,1},{7,3},{8,12},{10,14},{12... | collective-permute-start | bytes 1916936 | tf_op jit(solution)/shard_map/ppermute | solution.py:42
  496.8 48.7 %collective-permute-start.40 = (bf16[208,1536]{1,0:T(8,128)(2,1)}, bf16[208,1536]{1,0:T(8,128)(2,1)}, u32[]{:S(2)}, u32[]{:S(2)}) collective-permute-start(bf16[208,1536]{1,0:T(8,128)(2,1)} %get-tuple-element.95), channel_id=1, source_target_pairs={{0,6},{2,4},{4,2},{6,0},{1,7},{3,5},{5,3},{7,1},{8,14},{10,12},{12... | collective-permute-start | bytes 1916936 | tf_op jit(solution)/shard_map/ppermute | solution.py:42
  499.1 91.7 %all-to-all-start.1 = ((bf16[32,48,216]{2,1,0:T(8,128)(2,1)}), bf16[32,48,216]{2,1,0:T(8,128)(2,1)}, u32[]{:S(2)}, u32[]{:S(2)}) async-start(bf16[32,48,216]{2,1,0:T(8,128)(2,1)} %shard_map.208), calls=%async_computation.3 | async-start | bytes 1572864 | tf_op jit(solution)/shard_map/all_to_all | solution.py:633
  503.3 78.5 %collective-permute-start.35 = (bf16[256,1536]{1,0:T(8,128)(2,1)}, bf16[256,1536]{1,0:T(8,128)(2,1)}, u32[]{:S(2)}, u32[]{:S(2)}) collective-permute-start(bf16[256,1536]{1,0:T(8,128)(2,1)} %shard_map.204), channel_id=1, source_target_pairs={{0,8},{8,0},{16,24},{24,16},{1,9},{9,1},{17,25},{25,17},{2,10},{10... | collective-permute-start | bytes 2359304 | tf_op jit(solution)/shard_map/ppermute | solution.py:42
  505.1 77.1 %collective-permute-start.36 = (bf16[256,1536]{1,0:T(8,128)(2,1)}, bf16[256,1536]{1,0:T(8,128)(2,1)}, u32[]{:S(2)}, u32[]{:S(2)}) collective-permute-start(bf16[256,1536]{1,0:T(8,128)(2,1)} %shard_map.205), channel_id=1, source_target_pairs={{0,16},{8,24},{16,0},{24,8},{1,17},{9,25},{17,1},{25,9},{2,18},{10... | collective-permute-start | bytes 2359304 | tf_op jit(solution)/shard_map/ppermute | solution.py:42
  524.7 57.5 %collective-permute-start.37 = (bf16[256,1536]{1,0:T(8,128)(2,1)}, bf16[256,1536]{1,0:T(8,128)(2,1)}, u32[]{:S(2)}, u32[]{:S(2)}) collective-permute-start(bf16[256,1536]{1,0:T(8,128)(2,1)} %shard_map.206), channel_id=1, source_target_pairs={{0,24},{8,16},{16,8},{24,0},{1,25},{9,17},{17,9},{25,1},{2,26},{10... | collective-permute-start | bytes 2359304 | tf_op jit(solution)/shard_map/ppermute | solution.py:42
  (60 other events, 594.4 us)
Sparse Core Ops, SparseCore 0:
  10.0 115.2 all-gather.4
  129.3 56.0 all-gather.6
  321.9 80.0 reduce-scatter.2
  405.9 83.4 reduce-scatter.4
